TPU v7x, 512 devices: a whole 4x4x16 slice. The times are simulated.
512 devices in a mesh: freq: 16 (over y_hi, x, core), rgrp: 32 (over z, y_lo).
Axes of the slice: x: 4, y: 4 (y_hi: 2, y_lo: 2; y = y_hi * 2 + y_lo), z: 16, core: 2. Of those that a mesh axis runs over, the one named last changes fastest.
Arguments:
- traces: bfloat16 [1024, 147456], P('rgrp', 'freq'), may hold values from -6 to 6
- segment_offsets: int32 [64], P('freq'), may hold values from 0 to 1024
- channel_order: int32 [32, 32], P('rgrp'), may hold values from 0 to 31, each once within a row
- pilot_channel: int32 [1], replicated, may hold values from 0 to 1023
Outputs:
- cross_spectra: bfloat16 [2, 1024, 32, 2048], P(None, 'rgrp', None, 'freq')
All inputs are finite; a program needn't handle non-finite values.
Results may differ from a plain program's by a relative error of at most 0.0077.
Values may be sent and summed in bfloat16 or wider, within the bound.
No kernel may reach another device: no remote copies, remote signals or barrier semaphores. Data moves between devices by JAX's collectives and lax.ppermute only.
A program may use at most 64 MiB of HBM per device.

v0:
```python
import math

import jax
import jax.numpy as jnp
from jax import lax
from jax.sharding import PartitionSpec as P

L = 2048
K = 1024
SEG_DEV = 4


def broadcast(shard, axis, root):
    mine = lax.axis_index(axis) == root
    return lax.psum(jnp.where(mine, shard, jnp.zeros_like(shard)), axis)


def shifted(value, axis, steps):
    count = lax.axis_size(axis)
    pairs = [(source, (source + steps) % count) for source in range(count)]
    return lax.ppermute(value, axis, pairs)


def build_table(length, bin_count, blocks):
    sample = jnp.arange(length, dtype=jnp.int32)[:, None]
    which_bin = jnp.arange(bin_count, dtype=jnp.int32)[None, :] + 1
    residue = sample * which_bin % length
    phase_angle = residue.astype(jnp.float32) * (2.0 * math.pi / length)
    factor = 1.0 / math.sqrt(length)
    cosine = jnp.cos(phase_angle) * factor
    sine = -jnp.sin(phase_angle) * factor
    width_block = bin_count // blocks
    stacked = jnp.stack(
        [cosine.reshape(length, blocks, width_block), sine.reshape(length, blocks, width_block)],
        axis=2,
    )
    return stacked.reshape(length, 2 * bin_count).astype(jnp.bfloat16)


def whiten(spectra, pilot_spec, blocks):
    seg_count, chan_count, columns = spectra.shape
    width_block = columns // (2 * blocks)
    parts = spectra.reshape(seg_count, chan_count, blocks, 2, width_block)
    guide = pilot_spec.astype(jnp.float32).reshape(seg_count, 1, blocks, 2, width_block)
    real_x = parts[:, :, :, 0]
    imag_x = parts[:, :, :, 1]
    real_p = guide[:, :, :, 0]
    imag_p = guide[:, :, :, 1]
    real_z = real_x * real_p + imag_x * imag_p
    imag_z = imag_x * real_p - real_x * imag_p
    energy = real_z * real_z + imag_z * imag_z
    average = jnp.mean(energy, axis=(2, 3), keepdims=True)
    factor = lax.rsqrt(energy + 0.1 * average + 1e-06)
    return (
        jnp.stack([real_z * factor, imag_z * factor], axis=3)
        .reshape(seg_count, chan_count, columns)
        .astype(jnp.bfloat16)
    )


def cross_stack(first_block, second_block):
    seg_count, chan_count, columns = first_block.shape
    width_block = columns // 2
    real_a = first_block[:, :, :width_block]
    imag_a = first_block[:, :, width_block:]
    real_b = second_block[:, :, :width_block]
    imag_b = second_block[:, :, width_block:]

    def product(left_part, right_part):
        return jnp.einsum("sik,sjk->ijk", left_part, right_part, preferred_element_type=jnp.float32)

    real_c = product(real_a, real_b) + product(imag_a, imag_b)
    imag_c = product(imag_a, real_b) - product(real_a, imag_b)
    factor = 1.0 / math.sqrt(seg_count)
    return jnp.concatenate([real_c, imag_c], axis=2) * factor


def local(traces, segment_offsets, channel_order, pilot_channel):
    bands = lax.axis_size("freq")
    dft_table = build_table(L, K, bands)
    picked = jnp.take(traces, channel_order[0], axis=0)
    window_starts = jnp.arange(SEG_DEV, dtype=jnp.int32) * L + segment_offsets
    windows = jax.vmap(lambda window_start: lax.dynamic_slice_in_dim(picked, window_start, L, 1))(
        window_starts
    )
    spectra = jnp.einsum("scl,lf->scf", windows, dft_table, preferred_element_type=jnp.float32)
    chan_count = traces.shape[0]
    owner_group = pilot_channel[0] // chan_count
    pilot_row = lax.dynamic_index_in_dim(
        spectra, pilot_channel[0] % chan_count, 1, keepdims=False
    ).astype(jnp.bfloat16)
    pilot_spec = broadcast(pilot_row, "rgrp", owner_group)
    whitened = whiten(spectra, pilot_spec, bands)
    banded = lax.all_to_all(whitened, "freq", split_axis=2, concat_axis=0, tiled=True)
    nearest = shifted(banded, "rgrp", 1)
    farther = shifted(nearest, "rgrp", 1)
    return jnp.stack([cross_stack(banded, nearest), cross_stack(banded, farther)]).astype(
        jnp.bfloat16
    )


def solution(mesh):
    in_specs = (P("rgrp", "freq"), P("freq"), P("rgrp", None), P())
    out_specs = P(None, "rgrp", None, "freq")
    return jax.shard_map(local, mesh=mesh, in_specs=in_specs, out_specs=out_specs, check_vma=False)
```

profile of v0, /device:TPU:1, one launch (start us, length us, event | category | flops | bytes accessed | tf_op | source)
XLA Modules:
  0.0 278.2 jit_solution(11164198079138280365)
XLA Ops:
  0.0 0.0 copy-start
  0.8 0.7 fusion.13
  1.4 0.7 compare_and_fusion
  2.1 37.3 %multiply_convert_fusion.1 = (bf16[2048,16,1,64]{0,3,2,1:T(8,128)(2,1)}, bf16[2048,16,1,64]{0,3,2,1:T(8,128)(2,1)}) fusion(s32[16,64]{1,0:T(8,128)S(1)} %add_add_fusion), kind=kLoop, calls=%fused_computation.11 | loop fusion | flops 39845888 | bytes 8392704 | tf_op jit(solution)/shard_map/convert.5
  39.4 0.0 copy-done.2
  39.5 0.0 copy-done
  39.5 0.9 gather_fusion
  40.4 0.1 broadcast_select_fusion
  40.5 5.1 %while.1 = (s32[]{:T(128)}, bf16[32,9216]{1,0:T(8,128)(2,1)S(1)}, s32[4,2]{0,1:T(2,128)S(1)}, bf16[4,32,2048]{2,1,0:T(8,128)(2,1)S(1)}, s32[]{:T(128)}) while((s32[]{:T(128)}, bf16[32,9216]{1,0:T(8,128)(2,1)S(1)}, s32[4,2]{0,1:T(2,128)S(1)}, bf16[4,32,2048]{2,1,0:T(8,128)(2,1)S(1)}, s32[]{:T(128)}) %tuple.24), condition=%wide.while_cond, body=%wide.while_body.sunk | while | flops 2 | bytes 262241 | solution.py:83
  40.5 0.1 constant_dynamic-slice_fusion.2
  40.6 0.5 slice.76
  41.1 0.7 bitcast_dynamic-update-slice_fusion.2
  41.8 0.1 constant_dynamic-slice_fusion.2
  41.9 0.5 slice.76
  42.4 0.7 bitcast_dynamic-update-slice_fusion.2
  43.1 0.1 constant_dynamic-slice_fusion.2
  43.2 0.5 slice.76
  43.7 0.7 bitcast_dynamic-update-slice_fusion.2
  44.4 0.1 constant_dynamic-slice_fusion.2
  44.4 0.5 slice.76
  44.9 0.7 bitcast_dynamic-update-slice_fusion.2
  45.6 7.5 %pad_maximum_fusion = bf16[2048,16,2,64]{0,3,2,1:T(8,128)(2,1)} fusion(bf16[2048,16,1,64]{0,3,2,1:T(8,128)(2,1)} %get-tuple-element.34, bf16[2048,16,1,64]{0,3,2,1:T(8,128)(2,1)} %get-tuple-element.33), kind=kLoop, calls=%fused_computation.9 | loop fusion | flops 4194304 | bytes 16777216 | tf_op jit(solution)/shard_map/stack | solution.py:33
  53.1 7.3 %fusion.20 = f32[4,32,2048]{2,1,0:T(8,128)} fusion(bf16[4,32,2048]{2,1,0:T(8,128)(2,1)S(1)} %get-tuple-element.12, bf16[2048,2048,1]{0,1,2:T(8,128)(2,1)} %bitcast.89), kind=kOutput, calls=%fused_computation.52 | convolution fusion | flops 1073741824 | bytes 9961472 | tf_op jit(solution)/shard_map/scl,lf->scf/dot_general | solution.py:86
  60.4 2.8 reshape.200
  63.2 1.1 fusion.12
  64.2 0.1 reshape.201
  64.3 102.1 %psum.7 = bf16[4,1,16,2,64]{4,3,2,0,1:T(2,128)(2,1)S(1)} all-reduce(bf16[4,1,16,2,64]{4,3,2,0,1:T(2,128)(2,1)S(1)} %reshape.201), channel_id=1, replica_groups=mesh['freq'=16,'rgrp'=32] {'rgrp'}, use_global_device_ids=true, to_apply=%region_0.1 | all-reduce | flops 8192 | bytes 32768 | tf_op jit(solution)/shard_map/psum | solution.py:15
  166.5 1.6 fusion.15
  168.1 0.6 add_reduce_fusion
  168.7 0.6 multiply_convert_fusion.3
  169.3 1.2 pad_maximum_fusion.1
  170.5 3.4 %copy.84 = bf16[4,32,16,2,64]{1,0,4,3,2:T(4,128)(2,1)S(1)} copy(bf16[4,32,16,2,64]{4,2,3,1,0:T(8,128)(2,1)} %pad_maximum_fusion.1) | data formatting | bytes 1048576 | tf_op jit(solution)/shard_map/convert_element_type | solution.py:57
  173.8 2.0 reshape.233
  175.8 46.2 %all_to_all.18 = bf16[16,2,8192]{2,1,0:T(2,128)(2,1)} all-to-all(bf16[16,2,8192]{2,1,0:T(2,128)(2,1)S(1)} %reshape.233), channel_id=1, replica_groups=mesh['freq'=16,'rgrp'=32] {'freq'}, dimensions={0} | all-to-all | bytes 1048576 | tf_op jit(solution)/shard_map/all_to_all | solution.py:94
  222.0 3.6 %reshape.234 = bf16[2048,4,32]{2,1,0:T(4,128)(2,1)S(1)} reshape(bf16[16,2,8192]{2,1,0:T(2,128)(2,1)} %all_to_all.18) | data formatting | bytes 1048576
  225.7 1.0 copy.86
  226.7 1.9 collective-permute-start
  228.6 0.2 fusion.17
  228.8 1.1 copy.93
  229.9 1.1 copy.91
  231.0 12.0 %collective-permute-done = bf16[64,32,128]{2,1,0:T(8,128)(2,1)S(1)} collective-permute-done((bf16[64,32,128]{2,1,0:T(8,128)(2,1)S(1)}, bf16[64,32,128]{2,1,0:T(8,128)(2,1)S(1)}, u32[]{:S(2)}, u32[]{:S(2)}) %collective-permute-start) | collective-permute-done | bytes 524320 | tf_op jit(solution)/shard_map/ppermute | solution.py:21
  243.0 0.2 fusion.16
  243.3 0.6 copy-done.1
  243.8 1.1 copy.92
  244.9 1.1 copy.90
  246.0 0.4 fusion.21
  246.4 2.1 collective-permute-start.1
  248.5 1.4 fusion.9
  249.9 2.7 copy.76
  252.6 0.4 fusion.22
  253.0 1.4 fusion.8
  254.4 2.7 copy.77
  257.1 4.9 %collective-permute-done.1 = bf16[64,32,128]{2,1,0:T(8,128)(2,1)S(1)} collective-permute-done((bf16[64,32,128]{2,1,0:T(8,128)(2,1)}, bf16[64,32,128]{2,1,0:T(8,128)(2,1)S(1)}, u32[]{:S(2)}, u32[]{:S(2)}) %collective-permute-start.1) | collective-permute-done | bytes 524320 | tf_op jit(solution)/shard_map/ppermute | solution.py:21
  262.0 1.0 fusion.18
  263.0 1.1 copy.95
  264.1 1.4 fusion.23
  265.4 0.4 fusion.24
  265.8 2.1 copy.94
  268.0 2.6 fusion.7
  270.6 1.9 copy.80
  272.5 1.4 fusion.6
  273.9 1.9 copy.81
  275.8 1.5 fusion.10
  277.4 0.8 pad_maximum_fusion.2
  (9 shorter events, 0.1 us)
Async XLA Ops:
  0.0 39.5 %copy-start = (bf16[32,9216]{1,0:T(8,128)(2,1)S(1)}, bf16[32,9216]{1,0:T(8,128)(2,1)}, u32[]{:S(2)}) copy-start(bf16[32,9216]{1,0:T(8,128)(2,1)} %param.4) | copy-start | bytes 1769476
  0.0 39.4 %copy-start.2 = (s32[4]{0:T(128)S(1)}, s32[4]{0:T(128)}, u32[]{:S(2)}) copy-start(s32[4]{0:T(128)} %param.5) | copy-start | bytes 52
  226.7 16.3 %collective-permute-start = (bf16[64,32,128]{2,1,0:T(8,128)(2,1)S(1)}, bf16[64,32,128]{2,1,0:T(8,128)(2,1)S(1)}, u32[]{:S(2)}, u32[]{:S(2)}) collective-permute-start(bf16[64,32,128]{2,1,0:T(8,128)(2,1)S(1)} %bitcast.98), channel_id=1, source_target_pairs={{0,1},{1,2},{2,3},{3,4},{4,5},{5,6},{6,7},{7,8},{8,9},{9,10},{10,1... | collective-permute-start | bytes 1572872 | tf_op jit(solution)/shard_map/ppermute | solution.py:21
  243.0 0.8 copy-start.1
  246.4 15.6 %collective-permute-start.1 = (bf16[64,32,128]{2,1,0:T(8,128)(2,1)}, bf16[64,32,128]{2,1,0:T(8,128)(2,1)S(1)}, u32[]{:S(2)}, u32[]{:S(2)}) collective-permute-start(bf16[64,32,128]{2,1,0:T(8,128)(2,1)} %copy-done.1), channel_id=1, source_target_pairs={{0,1},{1,2},{2,3},{3,4},{4,5},{5,6},{6,7},{7,8},{8,9},{9,10},{10,1... | collective-permute-start | bytes 1572872 | tf_op jit(solution)/shard_map/ppermute | solution.py:21
where the time goes:
time: 280 us; the launch traced here: 278 us
  blocking collectives  148 us (53%)
  other arithmetic  52.1 us (19%)
  local copies, waits for them, and re-layouts  39.1 us (14%)
  waiting for transfers between devices  17 us (6%)
  matrix products  16.5 us (6%)
  starting transfers between devices  4.06 us (1%)
    psum x1, blocking collectives, broadcast(): return lax.psum(jnp.where(mine, shard, jnp.zeros_like(shard)), axis)  102 us
    all_to_all x1, blocking collectives, local(): lax.all_to_all(whitened, 'freq', split_axis=2, concat_axis=0, tiled=True)  46.2 us
    another operation x3, other arithmetic  39.5 us
    ppermute x2, waiting for transfers between devices, shifted(): return lax.ppermute(value, axis, pairs)  17 us
    unnamed x14, local copies, waits for them, and re-layouts  13.7 us
    concatenate x4, local copies, waits for them, and re-layouts, cross_stack(): return jnp.concatenate([real_c, imag_c], axis=2) * factor  9.26 us
    dot_general x8, matrix products, product(): jnp.einsum('sik,sjk->ijk', left_part, right_part, preferred_element_type=...  9.25 us
    another operation x1, other arithmetic, build_table(): jnp.stack([cosine.reshape(length, blocks, width_block), sine.reshape(leng...  7.47 us
  transfers between devices with their start and end apart: 2, of which 2 were waited for; matrix products, arithmetic and copies ran while one was open for 4% of the time, Pallas kernels for 0%

commit v1 on v0

v1 whole, which is shorter than its diff:
```python
import functools
import math

import jax
import jax.numpy as jnp
import ml_dtypes
import numpy as np
from jax import lax
from jax.experimental import pallas as pl
from jax.experimental.pallas import tpu as pltpu
from jax.sharding import PartitionSpec as P

L = 2048
HALF = 1024
BANDS = 16
SEG = 4
CH = 32
PAIRS = 32
SPAN = 9216
ROWS = SEG * PAIRS
LANES = 128
BANDS_STEP = 2
BF16 = jnp.bfloat16
F32 = jnp.float32


def half_table():
    band, parity, pair = np.ogrid[:BANDS, :2, :PAIRS]
    which_bin = 64 * band + 2 * pair + parity + 1
    sample = np.arange(HALF)
    residue = (which_bin[..., None] * sample) % L
    phase_angle = residue.astype(np.float32) * np.float32(2.0 * math.pi / L)
    factor = np.float32(1.0 / math.sqrt(L))
    cosine = np.cos(phase_angle) * factor
    sine = -np.sin(phase_angle) * factor
    return np.concatenate([cosine, sine], axis=2).astype(ml_dtypes.bfloat16)


def lane_index(rows):
    return lax.broadcasted_iota(jnp.int32, (rows, LANES), 1)


def cut_windows(offset_ref, order_ref, traces_ref, wave_ref):
    lane = lane_index(CH)
    row = lax.broadcasted_iota(jnp.int32, (CH, CH), 0)
    picked = jnp.zeros((CH, CH), jnp.int32)
    for channel in range(CH):
        picked = jnp.where(row == channel, order_ref[0, channel], picked)
    chosen = (lax.broadcasted_iota(jnp.int32, (CH, CH), 1) == picked).astype(F32).astype(BF16)
    tiles = L // LANES
    for seg in range(SEG):
        start = seg * L + offset_ref[seg]
        base = jnp.minimum((start // LANES) * LANES, SPAN - (L + LANES))
        base = pl.multiple_of(base, LANES)
        rest = start - base
        turn = lax.rem(LANES - rest, LANES)
        rolled = []
        for tile in range(tiles + 1):
            part = traces_ref[:, pl.ds(pl.multiple_of(base + tile * LANES, LANES), LANES)]
            rolled.append(pltpu.roll(part.astype(F32), turn, 1))
        window = [
            jnp.where(lane < LANES - rest, rolled[tile], rolled[tile + 1]) for tile in range(tiles)
        ]
        rows = pl.ds(seg * CH, CH)
        for parity in range(2):
            sign = -1.0 if parity == 0 else 1.0
            folded = jnp.concatenate(
                [window[t] + sign * window[t + tiles // 2] for t in range(tiles // 2)], axis=1
            ).astype(BF16)
            wave_ref[parity, rows, :] = jnp.dot(
                chosen, folded, preferred_element_type=F32
            ).astype(BF16)


def spectra_kernel(
    offset_ref, order_ref, pilot_ref, traces_ref, table_ref, block_ref, guide_ref, wave_ref, power_ref
):
    step = pl.program_id(0)

    @pl.when(step == 0)
    def _():
        power_ref[...] = jnp.zeros_like(power_ref)
        cut_windows(offset_ref, order_ref, traces_ref, wave_ref)

    lane = lane_index(PAIRS)
    channel = lax.rem(pilot_ref[0], CH)
    for local_band in range(BANDS_STEP):
        band = step * BANDS_STEP + local_band
        parts = {}
        for parity in range(2):
            product = lax.dot_general(
                table_ref[local_band, parity],
                wave_ref[parity],
                (((1,), (1,)), ((), ())),
                preferred_element_type=F32,
            )
            for side in range(2):
                parts[side, parity] = product[side * PAIRS : (side + 1) * PAIRS]
            real = parts[0, parity].astype(BF16).astype(F32)
            imag = parts[1, parity].astype(BF16).astype(F32)
            place = 2 * band + parity
            power = pltpu.roll(real * real + imag * imag, lax.rem(place - channel + LANES, LANES), 1)
            power_ref[...] = jnp.where(lane % 32 == place, power, power_ref[...])
        for seg in range(SEG):
            line = None
            for side in range(2):
                for parity in range(2):
                    group = side * 2 + parity
                    part = parts[side, parity]
                    if group != seg:
                        part = pltpu.roll(part, (group - seg) * 32 % LANES, 1)
                    line = part if line is None else jnp.where(lane // 32 == group, part, line)
            block_ref[local_band, seg * PAIRS : (seg + 1) * PAIRS, :] = line.astype(BF16)

    @pl.when(step == BANDS // BANDS_STEP - 1)
    def _():
        guide_ref[...] = jnp.sqrt(power_ref[...]).astype(BF16)


def spectra_of(offsets, order, pilot, traces, table):
    steps = BANDS // BANDS_STEP
    smem = pl.BlockSpec(memory_space=pltpu.SMEM)
    return pl.pallas_call(
        spectra_kernel,
        grid=(steps,),
        in_specs=[
            smem,
            smem,
            smem,
            pl.BlockSpec((CH, SPAN), lambda i: (0, 0)),
            pl.BlockSpec((BANDS_STEP, 2, 2 * PAIRS, HALF), lambda i: (i, 0, 0, 0)),
        ],
        out_specs=[
            pl.BlockSpec((BANDS_STEP, ROWS, LANES), lambda i: (i, 0, 0)),
            pl.BlockSpec((PAIRS, LANES), lambda i: (0, 0)),
        ],
        out_shape=[
            jax.ShapeDtypeStruct((BANDS, ROWS, LANES), BF16),
            jax.ShapeDtypeStruct((PAIRS, LANES), BF16),
        ],
        scratch_shapes=[
            pltpu.VMEM((2, SEG * CH, HALF), BF16),
            pltpu.VMEM((PAIRS, LANES), F32),
        ],
        compiler_params=pltpu.CompilerParams(vmem_limit_bytes=32 * 1024 * 1024),
        name="spectra",
    )(offsets, order, pilot, traces, table)


def level_kernel(pilot_ref, guides_ref, block_ref, note_ref, turned_ref):
    owner = pilot_ref[0] // (2 * CH)
    guide = guides_ref[owner].astype(F32)
    lane = lane_index(PAIRS)
    even = (lane // 32) % 2 == 0
    totals = [jnp.zeros((PAIRS, LANES), F32) for _ in range(SEG)]
    for band in range(BANDS):
        for seg in range(SEG):
            first = 32 * seg + 2 * band
            weight = jnp.where(even, guide[:, first : first + 1], guide[:, first + 1 : first + 2])
            part = block_ref[band, seg * PAIRS : (seg + 1) * PAIRS, :].astype(F32) * weight
            totals[seg] = totals[seg] + part * part
    levels = []
    for seg in range(SEG):
        total = jnp.sum(totals[seg], axis=0, keepdims=True)
        total = jnp.broadcast_to(total, (8, LANES))
        total = total + pltpu.roll(total, 64, 1)
        total = total + pltpu.roll(total, 32, 1)
        levels.append((total * (0.1 / (64.0 * BANDS)) + 1e-06)[:1])
    level = jnp.concatenate(levels + levels, axis=0)
    turned_ref[...] = jnp.transpose(
        jnp.concatenate([guide] * (LANES // PAIRS), axis=0)
    )
    for band in range(BANDS):
        even_rows = turned_ref[pl.ds(2 * band, SEG, stride=32), :]
        odd_rows = turned_ref[pl.ds(2 * band + 1, SEG, stride=32), :]
        note_ref[band] = jnp.concatenate([even_rows, odd_rows, level], axis=0).astype(BF16)


def notes_of(pilot, guides, blocks):
    vmem = pl.BlockSpec(memory_space=pltpu.VMEM)
    return pl.pallas_call(
        level_kernel,
        in_specs=[pl.BlockSpec(memory_space=pltpu.SMEM), vmem, vmem],
        out_specs=vmem,
        out_shape=jax.ShapeDtypeStruct((BANDS, 16, LANES), BF16),
        scratch_shapes=[pltpu.VMEM((LANES, LANES), F32)],
        compiler_params=pltpu.CompilerParams(vmem_limit_bytes=32 * 1024 * 1024),
        name="level",
    )(pilot, guides, blocks)


def cross_kernel(
    own_ref, near_ref, far_ref, own_note_ref, near_note_ref, far_note_ref, out_ref,
    own_white, near_white, far_white, stack_ref, guide_ref,
):
    lane = lane_index(PAIRS)
    even = (lane // 32) % 2 == 0
    rows = jnp.concatenate([own_note_ref[t, :8, :] for t in range(BANDS)], axis=0).astype(F32)
    guide_ref[...] = jnp.transpose(rows)[:PAIRS]
    for window in range(BANDS):
        for seg in range(SEG):
            first = 8 * window + seg
            guide = jnp.where(
                even, guide_ref[:, first : first + 1], guide_ref[:, first + 4 : first + 5]
            )
            for block_ref, note_ref, white_ref in (
                (own_ref, own_note_ref, own_white),
                (near_ref, near_note_ref, near_white),
                (far_ref, far_note_ref, far_white),
            ):
                value = block_ref[window, seg * PAIRS : (seg + 1) * PAIRS, :].astype(F32) * guide
                energy = value * value
                energy = energy + pltpu.roll(energy, 64, 1)
                level = note_ref[window, 8 + seg : 9 + seg, :].astype(F32)
                at = window * ROWS + seg * PAIRS
                white_ref[at : at + PAIRS, :] = value * lax.rsqrt(energy + level)

    wide = lane_index(BANDS * SEG)
    even_wide = (wide // 32) % 2 == 0
    sign = jnp.where(lane < 64, 1.0, -1.0)

    def bin_pair(pair, carry):
        at = pl.ds(pair, BANDS * SEG, stride=PAIRS)
        own = jnp.transpose(own_white[at, :]).astype(BF16)
        near = near_white[at, :]
        far = far_white[at, :]
        mixes = (
            jnp.where(even_wide, near, pltpu.roll(far, 32, 1)),
            jnp.where(even_wide, pltpu.roll(near, 96, 1), far),
        )
        for parity in range(2):
            left = jnp.concatenate(
                [own[parity * 32 : parity * 32 + 32], own[64 + parity * 32 : 96 + parity * 32]], axis=0
            )
            product = jnp.dot(left, mixes[parity].astype(BF16), preferred_element_type=F32)
            value = sign * product[:CH] + pltpu.roll(product[CH:], 64, 1)
            stack_ref[pl.ds(pl.multiple_of((2 * pair + parity) * CH, CH), CH), :] = value
        return carry

    lax.fori_loop(0, PAIRS, bin_pair, 0, unroll=4)

    full = lane_index(64)
    low = full < 64
    for half in range(CH // 2):
        first = stack_ref[pl.ds(2 * half, 64, stride=CH), :]
        second = stack_ref[pl.ds(2 * half + 1, 64, stride=CH), :]
        turned = jnp.transpose(jnp.concatenate([first, second], axis=0)) * 0.125
        real = turned[:64]
        imag = turned[64:]
        lines = (
            jnp.where(low, real, pltpu.roll(imag, 64, 1)),
            jnp.where(low, pltpu.roll(real, 64, 1), imag),
        )
        for k in range(2):
            for back in range(2):
                out_ref[back, 2 * half + k] = lines[k][back * 32 : back * 32 + 32].astype(BF16)


def cross_of(blocks, notes):
    vmem = pl.BlockSpec(memory_space=pltpu.VMEM)
    white = pltpu.VMEM((BANDS * ROWS, LANES), F32)
    return pl.pallas_call(
        cross_kernel,
        in_specs=[vmem] * 6,
        out_specs=vmem,
        out_shape=jax.ShapeDtypeStruct((2, CH, CH, LANES), BF16),
        scratch_shapes=[
            white,
            white,
            white,
            pltpu.VMEM((64 * CH, LANES), F32),
            pltpu.VMEM((PAIRS, LANES), F32),
        ],
        compiler_params=pltpu.CompilerParams(vmem_limit_bytes=48 * 1024 * 1024),
        name="cross",
    )(*blocks, *notes)


def shifted(value, steps):
    pairs = [(source, (source + steps) % 32) for source in range(32)]
    return lax.ppermute(value, "rgrp", pairs)


def local(table, traces, segment_offsets, channel_order, pilot_channel):
    blocks, guide = spectra_of(segment_offsets, channel_order, pilot_channel, traces, table)
    banded = lax.all_to_all(blocks, "freq", split_axis=0, concat_axis=0, tiled=True)

    group = lax.axis_index("rgrp")
    owner_side = (pilot_channel[0] // CH) % 2
    other = lax.ppermute(guide, "rgrp", [(g, g ^ 1) for g in range(32)])
    guide = jnp.where(group % 2 == owner_side, guide, other)
    lines = [[2 * z + side for z in range(16)] for side in range(2)]
    guides = lax.all_to_all(
        jnp.broadcast_to(guide, (16, PAIRS, LANES)),
        "rgrp",
        split_axis=0,
        concat_axis=0,
        tiled=True,
        axis_index_groups=lines,
    )
    notes = notes_of(pilot_channel, guides, blocks)
    own_note = lax.all_to_all(notes, "freq", split_axis=0, concat_axis=0, tiled=True)
    return cross_of(
        (banded, shifted(banded, 1), shifted(banded, 2)),
        (own_note, shifted(own_note, 1), shifted(own_note, 2)),
    )


def solution(mesh):
    table = half_table()
    specs = (P(), P("rgrp", "freq"), P("freq"), P("rgrp", None), P())
    inner = jax.shard_map(
        local, mesh=mesh, in_specs=specs, out_specs=P(None, "rgrp", None, "freq"), check_vma=False
    )

    def run(traces, segment_offsets, channel_order, pilot_channel):
        return inner(jnp.asarray(table), traces, segment_offsets, channel_order, pilot_channel)

    return run
```

time: 280 us -> 101 us (0.36)
  blocking collectives: 148 us -> 14.5 us
  other arithmetic: 52.1 us -> 0.01 us
  starting transfers between devices: 4.06 us -> 40.4 us
  local copies, waits for them, and re-layouts: 39.1 us -> 5.22 us
  Pallas kernels: 0 us -> 19.8 us
  matrix products: 16.5 us -> 0 us
  waiting for transfers between devices: 17 us -> 19.9 us
    psum x1 -> x0, blocking collectives: 102 us -> none  [broadcast(): return lax.psum(jnp.where(mine, shard, jnp.zeros_like(shard)), axis)]
    another operation x6 -> x0, other arithmetic: 49 us -> none
    all_to_all x1, blocking collectives: 46.2 us -> 14.5 us  [local(): lax.all_to_all(notes, 'freq', split_axis=0, concat_axis=0, tiled=True)]
    all_to_all x0 -> x2, starting transfers between devices: none -> 23.3 us  [the longest x1 13 us: local(): lax.all_to_all(jnp.broadcast_to(guide, (16, PAIRS, LANES)), 'rgrp', split...]
    pallas_call x0 -> x3, Pallas kernels: none -> 19.8 us  [the longest x1 11.5 us: cross_of(): pl.pallas_call(cross_kernel, in_specs=[vmem] * 6, out_specs=vmem, out_sha...]
    dot_general x9 -> x0, matrix products: 16.5 us -> none  [the longest x8 9.25 us: product(): jnp.einsum('sik,sjk->ijk', left_part, right_part, preferred_element_type=...]
    ppermute x2 -> x5, starting transfers between devices: 4.06 us -> 17.2 us  [the longest x4 15.3 us: shifted(): return lax.ppermute(value, 'rgrp', pairs)]
    all_to_all x0 -> x2, waiting for transfers between devices: none -> 13 us  [the longest x1 6.55 us: local(): lax.all_to_all(blocks, 'freq', split_axis=0, concat_axis=0, tiled=True)]
  transfers between devices with their start and end apart: 2 -> 7, of which waited for: 2 -> 4; matrix products, arithmetic and copies ran while one was open for 4% -> 0% of each run, Pallas kernels for 0% -> 2%
where the time goes in v1:
time: 101 us
  starting transfers between devices  40.4 us (40%)
  waiting for transfers between devices  19.9 us (20%)
  Pallas kernels  19.8 us (20%)
  blocking collectives  14.5 us (14%)
  local copies, waits for them, and re-layouts  5.22 us (5%)
    ppermute x4, starting transfers between devices, shifted(): return lax.ppermute(value, 'rgrp', pairs)  15.3 us
    all_to_all x1, blocking collectives, local(): lax.all_to_all(notes, 'freq', split_axis=0, concat_axis=0, tiled=True)  14.5 us
    all_to_all x1, starting transfers between devices, local(): lax.all_to_all(jnp.broadcast_to(guide, (16, PAIRS, LANES)), 'rgrp', split...  13 us
    pallas_call x1, Pallas kernels, cross_of(): pl.pallas_call(cross_kernel, in_specs=[vmem] * 6, out_specs=vmem, out_sha...  11.5 us
    all_to_all x1, starting transfers between devices, local(): lax.all_to_all(blocks, 'freq', split_axis=0, concat_axis=0, tiled=True)  10.2 us
    all_to_all x1, waiting for transfers between devices, local(): lax.all_to_all(blocks, 'freq', split_axis=0, concat_axis=0, tiled=True)  6.55 us
    pallas_call x1, Pallas kernels, spectra_of(): pl.pallas_call(spectra_kernel, grid=(steps,), in_specs=[smem, smem, smem,...  6.51 us
    all_to_all x1, waiting for transfers between devices, local(): lax.all_to_all(jnp.broadcast_to(guide, (16, PAIRS, LANES)), 'rgrp', split...  6.41 us
  transfers between devices with their start and end apart: 7, of which 4 were waited for; matrix products, arithmetic and copies ran while one was open for 0% of the time, Pallas kernels for 2%

profile of v1, /device:TPU:1, one launch (start us, length us, event | category | flops | bytes accessed | tf_op | source)
XLA Modules:
  0.0 100.6 jit_solution(12304623066224481991)
XLA Ops:
  0.7 0.0 copy-start
  0.7 2.2 %copy-done = bf16[16,2,64,1024]{3,2,1,0:T(8,128)(2,1)S(1)} copy-done((bf16[16,2,64,1024]{3,2,1,0:T(8,128)(2,1)S(1)}, bf16[16,2,64,1024]{3,2,1,0:T(8,128)(2,1)}, u32[]{:S(2)}) %copy-start) | copy-done | bytes 4194328
  2.8 0.0 copy-start.1
  2.8 1.1 %copy-done.1 = bf16[32,9216]{1,0:T(8,128)(2,1)S(1)} copy-done((bf16[32,9216]{1,0:T(8,128)(2,1)S(1)}, bf16[32,9216]{1,0:T(8,128)(2,1)}, u32[]{:S(2)}) %copy-start.1) | copy-done | bytes 589848
  3.9 0.0 copy-start.2
  3.9 0.7 copy-done.2
  4.6 0.0 copy-start.3
  4.6 0.7 copy-done.3
  5.2 6.5 %spectra.1 = (bf16[16,128,128]{2,1,0:T(8,128)(2,1)}, bf16[32,128]{1,0:T(8,128)(2,1)S(1)}) custom-call(s32[4]{0:T(128)S(1)} %copy-done.2, s32[1,32]{1,0:T(1,128)S(1)} %copy-done.3, s32[1]{0:T(128)} %copy.6.pilot_ref, bf16[32,9216]{1,0:T(8,128)(2,1)S(1)} %copy-done.1, bf16[16,2,64,1024]{3,2,1,0:T(8,128)(2,1)S(1)} %copy-done), custom_call_target="tpu_custom_call" | custom-call | tf_op jit(solution)/shard_map/spectra/pallas_call | solution.py:123
  11.7 10.2 %all-to-all-start = ((bf16[16,128,128]{2,1,0:T(8,128)(2,1)}), bf16[16,128,128]{2,1,0:T(8,128)(2,1)S(1)}, u32[]{:S(2)}, u32[]{:S(2)}) async-start(bf16[16,128,128]{2,1,0:T(8,128)(2,1)} %get-tuple-element.7.block_ref), calls=%async_computation | async-start | bytes 1048576 | tf_op jit(solution)/shard_map/all_to_all | solution.py:286
  22.0 1.9 %collective-permute-start.2 = (bf16[32,128]{1,0:T(8,128)(2,1)S(1)}, bf16[32,128]{1,0:T(8,128)(2,1)S(1)}, u32[]{:S(2)}, u32[]{:S(2)}) collective-permute-start(bf16[32,128]{1,0:T(8,128)(2,1)S(1)} %get-tuple-element.8), channel_id=1, source_target_pairs={{0,1},{1,0},{2,3},{3,2},{4,5},{5,4},{6,7},{7,6},{8,9},{9,8},{10,11... | collective-permute-start | bytes 24584 | tf_op jit(solution)/shard_map/ppermute | solution.py:290
  23.9 3.0 %collective-permute-done.2 = bf16[32,128]{1,0:T(8,128)(2,1)S(1)} collective-permute-done((bf16[32,128]{1,0:T(8,128)(2,1)S(1)}, bf16[32,128]{1,0:T(8,128)(2,1)S(1)}, u32[]{:S(2)}, u32[]{:S(2)}) %collective-permute-start.2) | collective-permute-done | bytes 8224 | tf_op jit(solution)/shard_map/ppermute | solution.py:290
  26.9 6.6 %all-to-all-done.own_ref = bf16[16,128,128]{2,1,0:T(8,128)(2,1)S(1)} async-done(((bf16[16,128,128]{2,1,0:T(8,128)(2,1)}), bf16[16,128,128]{2,1,0:T(8,128)(2,1)S(1)}, u32[]{:S(2)}, u32[]{:S(2)}) %all-to-all-start) | async-done | bytes 524320 | tf_op jit(solution)/shard_map/all_to_all | solution.py:286
  33.5 0.7 broadcast_in_dim.3
  34.1 13.0 %all-to-all-start.1 = ((bf16[16,32,128]{2,1,0:T(8,128)(2,1)}), bf16[16,32,128]{2,1,0:T(8,128)(2,1)S(1)}, u32[]{:S(2)}, u32[]{:S(2)}) async-start(bf16[16,32,128]{2,1,0:T(8,128)(2,1)} %broadcast_in_dim.3), calls=%async_computation.1 | async-start | bytes 262144 | tf_op jit(solution)/shard_map/all_to_all | solution.py:293
  47.2 3.3 %collective-permute-start.1 = (bf16[16,128,128]{2,1,0:T(8,128)(2,1)S(1)}, bf16[16,128,128]{2,1,0:T(8,128)(2,1)S(1)}, u32[]{:S(2)}, u32[]{:S(2)}) collective-permute-start(bf16[16,128,128]{2,1,0:T(8,128)(2,1)S(1)} %all-to-all-done.own_ref), channel_id=1, source_target_pairs={{0,2},{1,3},{2,4},{3,5},{4,6},{5,7},{6,8},{7,9},{8,10},{9,11},{10,... | collective-permute-start | bytes 1572872 | tf_op jit(solution)/shard_map/ppermute | solution.py:281
  50.4 2.3 %collective-permute-start = (bf16[16,128,128]{2,1,0:T(8,128)(2,1)S(1)}, bf16[16,128,128]{2,1,0:T(8,128)(2,1)S(1)}, u32[]{:S(2)}, u32[]{:S(2)}) collective-permute-start(bf16[16,128,128]{2,1,0:T(8,128)(2,1)S(1)} %all-to-all-done.own_ref), channel_id=1, source_target_pairs={{0,1},{1,2},{2,3},{3,4},{4,5},{5,6},{6,7},{7,8},{8,9},{9,10},{10,1... | collective-permute-start | bytes 1572872 | tf_op jit(solution)/shard_map/ppermute | solution.py:281
  52.7 6.4 %all-to-all-done.1.guides_ref = bf16[16,32,128]{2,1,0:T(8,128)(2,1)S(1)} async-done(((bf16[16,32,128]{2,1,0:T(8,128)(2,1)}), bf16[16,32,128]{2,1,0:T(8,128)(2,1)S(1)}, u32[]{:S(2)}, u32[]{:S(2)}) %all-to-all-start.1) | async-done | bytes 131104 | tf_op jit(solution)/shard_map/all_to_all | solution.py:293
  59.2 1.8 %level.1 = bf16[16,16,128]{2,1,0:T(8,128)(2,1)S(1)} custom-call(s32[1]{0:T(128)} %copy.6.pilot_ref, bf16[16,32,128]{2,1,0:T(8,128)(2,1)S(1)} %all-to-all-done.1.guides_ref, bf16[16,128,128]{2,1,0:T(8,128)(2,1)} %get-tuple-element.7.block_ref), custom_call_target="tpu_custom_call" | custom-call | tf_op jit(solution)/shard_map/level/pallas_call | solution.py:181
  60.9 14.5 %all_to_all.15.own_note_ref = bf16[16,16,128]{2,1,0:T(8,128)(2,1)S(1)} all-to-all(bf16[16,16,128]{2,1,0:T(8,128)(2,1)S(1)} %level.1), channel_id=1, replica_groups=mesh['freq'=16,'rgrp'=32] {'freq'}, dimensions={0} | all-to-all | bytes 131072 | tf_op jit(solution)/shard_map/all_to_all | solution.py:302
  75.4 2.4 %collective-permute-start.4 = (bf16[16,16,128]{2,1,0:T(8,128)(2,1)S(1)}, bf16[16,16,128]{2,1,0:T(8,128)(2,1)S(1)}, u32[]{:S(2)}, u32[]{:S(2)}) collective-permute-start(bf16[16,16,128]{2,1,0:T(8,128)(2,1)S(1)} %all_to_all.15.own_note_ref), channel_id=1, source_target_pairs={{0,2},{1,3},{2,4},{3,5},{4,6},{5,7},{6,8},{7,9},{8,10},{9,11},{10,... | collective-permute-start | bytes 196616 | tf_op jit(solution)/shard_map/ppermute | solution.py:281
  77.8 7.3 %collective-permute-start.3 = (bf16[16,16,128]{2,1,0:T(8,128)(2,1)S(1)}, bf16[16,16,128]{2,1,0:T(8,128)(2,1)S(1)}, u32[]{:S(2)}, u32[]{:S(2)}) collective-permute-start(bf16[16,16,128]{2,1,0:T(8,128)(2,1)S(1)} %all_to_all.15.own_note_ref), channel_id=1, source_target_pairs={{0,1},{1,2},{2,3},{3,4},{4,5},{5,6},{6,7},{7,8},{8,9},{9,10},{10,1... | collective-permute-start | bytes 196616 | tf_op jit(solution)/shard_map/ppermute | solution.py:281
  85.1 0.0 collective-permute-done.4.far_note_ref
  85.1 4.0 %collective-permute-done.3.near_note_ref = bf16[16,16,128]{2,1,0:T(8,128)(2,1)S(1)} collective-permute-done((bf16[16,16,128]{2,1,0:T(8,128)(2,1)S(1)}, bf16[16,16,128]{2,1,0:T(8,128)(2,1)S(1)}, u32[]{:S(2)}, u32[]{:S(2)}) %collective-permute-start.3) | collective-permute-done | bytes 65568 | tf_op jit(solution)/shard_map/ppermute | solution.py:281
  89.1 0.0 collective-permute-done.1.far_ref
  89.1 0.0 collective-permute-done.near_ref
  89.1 11.5 %cross.1 = bf16[2,32,32,128]{3,2,1,0:T(8,128)(2,1)} custom-call(bf16[16,128,128]{2,1,0:T(8,128)(2,1)S(1)} %all-to-all-done.own_ref, bf16[16,128,128]{2,1,0:T(8,128)(2,1)S(1)} %collective-permute-done.near_ref, bf16[16,128,128]{2,1,0:T(8,128)(2,1)S(1)} %collective-permute-done.1.far_ref, bf16[16,16,128]{2,1,0:T(8,128)(2,1)S(1)} %all_to_all.15.own_note_ref, ...), custom_call_target="tpu_custom_call" | custom-call | tf_op jit(solution)/shard_map/cross/pallas_call | solution.py:262
  (1 shorter events, 0.0 us)
Async XLA Ops:
  0.7 2.2 %copy-start = (bf16[16,2,64,1024]{3,2,1,0:T(8,128)(2,1)S(1)}, bf16[16,2,64,1024]{3,2,1,0:T(8,128)(2,1)}, u32[]{:S(2)}) copy-start(bf16[16,2,64,1024]{3,2,1,0:T(8,128)(2,1)} %constant.37.clone.table_ref) | copy-start | bytes 12582916
  2.8 1.1 %copy-start.1 = (bf16[32,9216]{1,0:T(8,128)(2,1)S(1)}, bf16[32,9216]{1,0:T(8,128)(2,1)}, u32[]{:S(2)}) copy-start(bf16[32,9216]{1,0:T(8,128)(2,1)} %traces_ref.1) | copy-start | bytes 1769476
  3.9 0.7 copy-start.2
  4.6 0.7 copy-start.3
  11.7 21.7 %all-to-all-start = ((bf16[16,128,128]{2,1,0:T(8,128)(2,1)}), bf16[16,128,128]{2,1,0:T(8,128)(2,1)S(1)}, u32[]{:S(2)}, u32[]{:S(2)}) async-start(bf16[16,128,128]{2,1,0:T(8,128)(2,1)} %get-tuple-element.7.block_ref), calls=%async_computation | async-start | bytes 1048576 | tf_op jit(solution)/shard_map/all_to_all | solution.py:286
  22.0 4.9 %collective-permute-start.2 = (bf16[32,128]{1,0:T(8,128)(2,1)S(1)}, bf16[32,128]{1,0:T(8,128)(2,1)S(1)}, u32[]{:S(2)}, u32[]{:S(2)}) collective-permute-start(bf16[32,128]{1,0:T(8,128)(2,1)S(1)} %get-tuple-element.8), channel_id=1, source_target_pairs={{0,1},{1,0},{2,3},{3,2},{4,5},{5,4},{6,7},{7,6},{8,9},{9,8},{10,11... | collective-permute-start | bytes 24584 | tf_op jit(solution)/shard_map/ppermute | solution.py:290
  34.1 25.0 %all-to-all-start.1 = ((bf16[16,32,128]{2,1,0:T(8,128)(2,1)}), bf16[16,32,128]{2,1,0:T(8,128)(2,1)S(1)}, u32[]{:S(2)}, u32[]{:S(2)}) async-start(bf16[16,32,128]{2,1,0:T(8,128)(2,1)} %broadcast_in_dim.3), calls=%async_computation.1 | async-start | bytes 262144 | tf_op jit(solution)/shard_map/all_to_all | solution.py:293
  47.2 42.0 %collective-permute-start.1 = (bf16[16,128,128]{2,1,0:T(8,128)(2,1)S(1)}, bf16[16,128,128]{2,1,0:T(8,128)(2,1)S(1)}, u32[]{:S(2)}, u32[]{:S(2)}) collective-permute-start(bf16[16,128,128]{2,1,0:T(8,128)(2,1)S(1)} %all-to-all-done.own_ref), channel_id=1, source_target_pairs={{0,2},{1,3},{2,4},{3,5},{4,6},{5,7},{6,8},{7,9},{8,10},{9,11},{10,... | collective-permute-start | bytes 1572872 | tf_op jit(solution)/shard_map/ppermute | solution.py:281
  50.4 38.7 %collective-permute-start = (bf16[16,128,128]{2,1,0:T(8,128)(2,1)S(1)}, bf16[16,128,128]{2,1,0:T(8,128)(2,1)S(1)}, u32[]{:S(2)}, u32[]{:S(2)}) collective-permute-start(bf16[16,128,128]{2,1,0:T(8,128)(2,1)S(1)} %all-to-all-done.own_ref), channel_id=1, source_target_pairs={{0,1},{1,2},{2,3},{3,4},{4,5},{5,6},{6,7},{7,8},{8,9},{9,10},{10,1... | collective-permute-start | bytes 1572872 | tf_op jit(solution)/shard_map/ppermute | solution.py:281
  75.4 9.7 %collective-permute-start.4 = (bf16[16,16,128]{2,1,0:T(8,128)(2,1)S(1)}, bf16[16,16,128]{2,1,0:T(8,128)(2,1)S(1)}, u32[]{:S(2)}, u32[]{:S(2)}) collective-permute-start(bf16[16,16,128]{2,1,0:T(8,128)(2,1)S(1)} %all_to_all.15.own_note_ref), channel_id=1, source_target_pairs={{0,2},{1,3},{2,4},{3,5},{4,6},{5,7},{6,8},{7,9},{8,10},{9,11},{10,... | collective-permute-start | bytes 196616 | tf_op jit(solution)/shard_map/ppermute | solution.py:281
  77.8 11.3 %collective-permute-start.3 = (bf16[16,16,128]{2,1,0:T(8,128)(2,1)S(1)}, bf16[16,16,128]{2,1,0:T(8,128)(2,1)S(1)}, u32[]{:S(2)}, u32[]{:S(2)}) collective-permute-start(bf16[16,16,128]{2,1,0:T(8,128)(2,1)S(1)} %all_to_all.15.own_note_ref), channel_id=1, source_target_pairs={{0,1},{1,2},{2,3},{3,4},{4,5},{5,6},{6,7},{7,8},{8,9},{9,10},{10,1... | collective-permute-start | bytes 196616 | tf_op jit(solution)/shard_map/ppermute | solution.py:281

commit v2 on v1

v2 whole, which is shorter than its diff:
```python
import functools
import math

import jax
import jax.numpy as jnp
import ml_dtypes
import numpy as np
from jax import lax
from jax.experimental import pallas as pl
from jax.experimental.pallas import tpu as pltpu
from jax.sharding import PartitionSpec as P

L = 2048
HALF = 1024
BANDS = 16
SEG = 4
CH = 32
PAIRS = 32
SPAN = 9216
ROWS = SEG * PAIRS
LANES = 128
BF16 = jnp.bfloat16
F32 = jnp.float32


def half_table():
    band, parity, pair = np.ogrid[:BANDS, :2, :PAIRS]
    which_bin = 64 * band + 2 * pair + parity + 1
    sample = np.arange(HALF)
    residue = (which_bin[..., None] * sample) % L
    phase_angle = residue.astype(np.float32) * np.float32(2.0 * math.pi / L)
    factor = np.float32(1.0 / math.sqrt(L))
    cosine = np.cos(phase_angle) * factor
    sine = -np.sin(phase_angle) * factor
    return np.concatenate([cosine, sine], axis=2).astype(ml_dtypes.bfloat16)


def lane_index(rows):
    return lax.broadcasted_iota(jnp.int32, (rows, LANES), 1)


def cut_windows(offset_ref, order_ref, traces_ref, wave_ref):
    lane = lane_index(CH)
    row = lax.broadcasted_iota(jnp.int32, (CH, CH), 0)
    picked = jnp.zeros((CH, CH), jnp.int32)
    for channel in range(CH):
        picked = jnp.where(row == channel, order_ref[0, channel], picked)
    chosen = (lax.broadcasted_iota(jnp.int32, (CH, CH), 1) == picked).astype(F32).astype(BF16)
    tiles = L // LANES
    for seg in range(SEG):
        start = seg * L + offset_ref[seg]
        base = jnp.minimum((start // LANES) * LANES, SPAN - (L + LANES))
        base = pl.multiple_of(base, LANES)
        rest = start - base
        turn = lax.rem(LANES - rest, LANES)
        rolled = []
        for tile in range(tiles + 1):
            part = traces_ref[:, pl.ds(pl.multiple_of(base + tile * LANES, LANES), LANES)]
            rolled.append(pltpu.roll(part.astype(F32), turn, 1))
        window = [
            jnp.where(lane < LANES - rest, rolled[tile], rolled[tile + 1]) for tile in range(tiles)
        ]
        rows = pl.ds(seg * CH, CH)
        for parity in range(2):
            sign = -1.0 if parity == 0 else 1.0
            folded = jnp.concatenate(
                [window[t] + sign * window[t + tiles // 2] for t in range(tiles // 2)], axis=1
            ).astype(BF16)
            wave_ref[parity, rows, :] = jnp.dot(
                chosen, folded, preferred_element_type=F32
            ).astype(BF16)


def spectra_kernel(
    offset_hbm, order_hbm, pilot_hbm, traces_hbm, table_hbm, block_ref, guide_ref,
    offset_ref, order_ref, pilot_ref, traces_ref, table_ref, wave_ref, power_ref, sems, table_sems,
):
    small = [
        pltpu.make_async_copy(source, target, sems.at[k])
        for k, (source, target) in enumerate(
            (
                (offset_hbm, offset_ref),
                (order_hbm, order_ref),
                (pilot_hbm, pilot_ref),
                (traces_hbm, traces_ref),
            )
        )
    ]
    for copy in small:
        copy.start()
    for part in range(4):
        pltpu.make_async_copy(
            table_hbm.at[pl.ds(4 * part, 4)], table_ref.at[pl.ds(4 * part, 4)], table_sems.at[part]
        ).start()
    power_ref[...] = jnp.zeros_like(power_ref)
    for copy in small:
        copy.wait()
    cut_windows(offset_ref, order_ref, traces_ref, wave_ref)

    lane = lane_index(PAIRS)
    channel = lax.rem(pilot_ref[0], CH)
    for quarter in range(4):
        pltpu.make_async_copy(
            table_hbm.at[pl.ds(4 * quarter, 4)],
            table_ref.at[pl.ds(4 * quarter, 4)],
            table_sems.at[quarter],
        ).wait()
        for local_band in range(4):
            band = quarter * 4 + local_band
            parts = {}
            for parity in range(2):
                product = lax.dot_general(
                    table_ref[band, parity],
                    wave_ref[parity],
                    (((1,), (1,)), ((), ())),
                    preferred_element_type=F32,
                )
                for side in range(2):
                    parts[side, parity] = product[side * PAIRS : (side + 1) * PAIRS]
                real = parts[0, parity].astype(BF16).astype(F32)
                imag = parts[1, parity].astype(BF16).astype(F32)
                place = 2 * band + parity
                power = pltpu.roll(
                    real * real + imag * imag, lax.rem(place - channel + LANES, LANES), 1
                )
                power_ref[...] = jnp.where(lane % 32 == place, power, power_ref[...])
            for seg in range(SEG):
                line = None
                for side in range(2):
                    for parity in range(2):
                        group = side * 2 + parity
                        part = parts[side, parity]
                        if group != seg:
                            part = pltpu.roll(part, (group - seg) * 32 % LANES, 1)
                        line = part if line is None else jnp.where(lane // 32 == group, part, line)
                block_ref[band, seg * PAIRS : (seg + 1) * PAIRS, :] = line
    mine = pilot_ref[0] // CH == lax.axis_index("rgrp")
    guide_ref[...] = jnp.where(mine, jnp.sqrt(power_ref[...]), 0.0).astype(BF16)


def spectra_of(offsets, order, pilot, traces, table):
    vmem = pl.BlockSpec(memory_space=pltpu.VMEM)
    return pl.pallas_call(
        spectra_kernel,
        in_specs=[pl.BlockSpec(memory_space=pl.ANY)] * 5,
        out_specs=[vmem, vmem],
        out_shape=[
            jax.ShapeDtypeStruct((BANDS, ROWS, LANES), F32),
            jax.ShapeDtypeStruct((PAIRS, LANES), BF16),
        ],
        scratch_shapes=[
            pltpu.SMEM((SEG,), jnp.int32),
            pltpu.SMEM((1, CH), jnp.int32),
            pltpu.SMEM((1,), jnp.int32),
            pltpu.VMEM((CH, SPAN), BF16),
            pltpu.VMEM((BANDS, 2, 2 * PAIRS, HALF), BF16),
            pltpu.VMEM((2, SEG * CH, HALF), BF16),
            pltpu.VMEM((PAIRS, LANES), F32),
            pltpu.SemaphoreType.DMA((4,)),
            pltpu.SemaphoreType.DMA((4,)),
        ],
        compiler_params=pltpu.CompilerParams(vmem_limit_bytes=56 * 1024 * 1024),
        name="spectra",
    )(offsets, order, pilot, traces, table)


def whiten_kernel(guides_ref, block_ref, white_ref, value_ref, guide_ref):
    guide = guides_ref[0].astype(F32)
    for line in range(1, 16):
        guide = guide + guides_ref[line].astype(F32)
    guide_ref[...] = guide
    lane = lane_index(PAIRS)
    even = (lane // 32) % 2 == 0
    totals = [jnp.zeros((PAIRS, LANES), F32) for _ in range(SEG)]
    for band in range(BANDS):
        for seg in range(SEG):
            first = 32 * seg + 2 * band
            rows = slice(seg * PAIRS, (seg + 1) * PAIRS)
            weight = jnp.where(
                even, guide_ref[:, first : first + 1], guide_ref[:, first + 1 : first + 2]
            )
            value = block_ref[band, rows, :] * weight
            value_ref[band, rows, :] = value
            totals[seg] = totals[seg] + value * value
    levels = []
    for seg in range(SEG):
        total = jnp.sum(totals[seg], axis=0, keepdims=True)
        total = jnp.broadcast_to(total, (8, LANES))
        total = total + pltpu.roll(total, 64, 1)
        total = total + pltpu.roll(total, 32, 1)
        levels.append((total * (0.1 / (64.0 * BANDS)) + 1e-06)[:1])
    for band in range(BANDS):
        for seg in range(SEG):
            rows = slice(seg * PAIRS, (seg + 1) * PAIRS)
            value = value_ref[band, rows, :]
            energy = value * value
            energy = energy + pltpu.roll(energy, 64, 1)
            white_ref[band, rows, :] = (value * lax.rsqrt(energy + levels[seg])).astype(BF16)


def whitened_of(guides, blocks):
    vmem = pl.BlockSpec(memory_space=pltpu.VMEM)
    return pl.pallas_call(
        whiten_kernel,
        in_specs=[vmem, vmem],
        out_specs=vmem,
        out_shape=jax.ShapeDtypeStruct((BANDS, ROWS, LANES), BF16),
        scratch_shapes=[pltpu.VMEM((BANDS, ROWS, LANES), F32), pltpu.VMEM((PAIRS, LANES), F32)],
        compiler_params=pltpu.CompilerParams(vmem_limit_bytes=32 * 1024 * 1024),
        name="whiten",
    )(guides, blocks)


def gather_kernel(band_ref, right_ref, wide_ref):
    for window in range(BANDS):
        wide_ref[window * ROWS : (window + 1) * ROWS, :] = band_ref[window].astype(F32)

    def bin_pair(pair, carry):
        right_ref[pair] = wide_ref[pl.ds(pair, BANDS * SEG, stride=PAIRS), :].astype(BF16)
        return carry

    lax.fori_loop(0, PAIRS, bin_pair, 0, unroll=4)


def gathered_of(banded):
    vmem = pl.BlockSpec(memory_space=pltpu.VMEM)
    return pl.pallas_call(
        gather_kernel,
        in_specs=[vmem],
        out_specs=vmem,
        out_shape=jax.ShapeDtypeStruct((PAIRS, BANDS * SEG, LANES), BF16),
        scratch_shapes=[pltpu.VMEM((BANDS * ROWS, LANES), F32)],
        compiler_params=pltpu.CompilerParams(vmem_limit_bytes=32 * 1024 * 1024),
        name="gather",
    )(banded)


def left_kernel(right_ref, left_ref):
    def bin_pair(pair, carry):
        turned = jnp.transpose(right_ref[pair].astype(F32))
        left_ref[pair] = jnp.concatenate([turned[:64], turned[64:]], axis=1).astype(BF16)
        return carry

    lax.fori_loop(0, PAIRS, bin_pair, 0, unroll=4)


def left_of(right):
    vmem = pl.BlockSpec(memory_space=pltpu.VMEM)
    return pl.pallas_call(
        left_kernel,
        in_specs=[vmem],
        out_specs=vmem,
        out_shape=jax.ShapeDtypeStruct((PAIRS, 2 * CH, LANES), BF16),
        compiler_params=pltpu.CompilerParams(vmem_limit_bytes=32 * 1024 * 1024),
        name="left",
    )(right)


def cross_one(left_ref, right_ref, stack_ref, store):
    side = jnp.where(lane_index(BANDS * SEG) < 64, 1.0, -1.0)

    def bin_pair(pair, carry):
        right = right_ref[pair].astype(F32)
        mix = jnp.concatenate([right * side, pltpu.roll(right, 64, 1)], axis=0).astype(BF16)
        product = jnp.dot(left_ref[pair], mix, preferred_element_type=F32)
        stack_ref[pl.ds(pl.multiple_of(pair * 2 * CH, 2 * CH), 2 * CH), :] = product
        return carry

    lax.fori_loop(0, PAIRS, bin_pair, 0, unroll=4)

    lane = lane_index(CH)
    low = lane < 64
    even = lane % 2 == 0
    for half in range(CH // 2):
        first = stack_ref[pl.ds(2 * half, 64, stride=CH), :]
        second = stack_ref[pl.ds(2 * half + 1, 64, stride=CH), :]
        turned = jnp.transpose(jnp.concatenate([first, second], axis=0)) * 0.125
        real = jnp.where(even, turned[:32], turned[32:64])
        imag = jnp.where(even, turned[64:96], turned[96:])
        store(2 * half, jnp.where(low, real, pltpu.roll(imag, 64, 1)).astype(BF16))
        store(2 * half + 1, jnp.where(low, pltpu.roll(real, 64, 1), imag).astype(BF16))


def near_kernel(left_ref, right_ref, out_ref, stack_ref):
    def store(channel, lines):
        out_ref[channel] = lines

    cross_one(left_ref, right_ref, stack_ref, store)


def far_kernel(left_ref, right_ref, near_ref, out_ref, stack_ref):
    def store(channel, lines):
        out_ref[1, channel] = lines

    out_ref[0] = near_ref[...]
    cross_one(left_ref, right_ref, stack_ref, store)


def cross_of(kernel, shape, *arrays):
    vmem = pl.BlockSpec(memory_space=pltpu.VMEM)
    return pl.pallas_call(
        kernel,
        in_specs=[vmem] * len(arrays),
        out_specs=vmem,
        out_shape=jax.ShapeDtypeStruct(shape, BF16),
        scratch_shapes=[pltpu.VMEM((64 * CH, LANES), F32)],
        compiler_params=pltpu.CompilerParams(vmem_limit_bytes=32 * 1024 * 1024),
        name=kernel.__name__,
    )(*arrays)


def shifted(value, steps):
    pairs = [(source, (source + steps) % 32) for source in range(32)]
    return lax.ppermute(value, "rgrp", pairs)


def local(table, traces, segment_offsets, channel_order, pilot_channel):
    blocks, guide = spectra_of(segment_offsets, channel_order, pilot_channel, traces, table)
    guide = guide + lax.ppermute(guide, "rgrp", [(g, g ^ 1) for g in range(32)])
    lines = [[2 * z + side for z in range(16)] for side in range(2)]
    guides = lax.all_to_all(
        jnp.broadcast_to(guide, (16, PAIRS, LANES)),
        "rgrp",
        split_axis=0,
        concat_axis=0,
        tiled=True,
        axis_index_groups=lines,
    )
    white = whitened_of(guides, blocks)
    banded = lax.all_to_all(white, "freq", split_axis=0, concat_axis=0, tiled=True)
    own = gathered_of(banded)
    near, far = shifted(own, 1), shifted(own, 2)
    left = left_of(own)
    first = cross_of(near_kernel, (CH, CH, LANES), left, near)
    return cross_of(far_kernel, (2, CH, CH, LANES), left, far, first)


def solution(mesh):
    table = half_table()
    specs = (P(), P("rgrp", "freq"), P("freq"), P("rgrp", None), P())
    inner = jax.shard_map(
        local, mesh=mesh, in_specs=specs, out_specs=P(None, "rgrp", None, "freq"), check_vma=False
    )

    def run(traces, segment_offsets, channel_order, pilot_channel):
        return inner(jnp.asarray(table), traces, segment_offsets, channel_order, pilot_channel)

    return run
```

time: 101 us -> 97.1 us (0.961)
  the two profiles are of different devices: /device:TPU:1 before, /device:TPU:8 now
where the time goes in v2:
time: 97.1 us; the launch traced here: 96.8 us
  blocking collectives  43.5 us (45%)
  waiting for transfers between devices  19.6 us (20%)
  Pallas kernels  17.1 us (18%)
  starting transfers between devices  13.9 us (14%)
  local copies, waits for them, and re-layouts  1.25 us (1%)
    all_to_all x1, blocking collectives, local(): lax.all_to_all(jnp.broadcast_to(guide, (16, PAIRS, LANES)), 'rgrp', split...  25.2 us
    all_to_all x1, blocking collectives, local(): lax.all_to_all(white, 'freq', split_axis=0, concat_axis=0, tiled=True)  18.3 us
    ppermute x2, waiting for transfers between devices, shifted(): return lax.ppermute(value, 'rgrp', pairs)  17.8 us
    ppermute x1, starting transfers between devices, local(): guide = guide + lax.ppermute(guide, 'rgrp', [(g, g ^ 1) for g in range(32)])  7.72 us
    pallas_call x1, Pallas kernels, spectra_of(): pl.pallas_call(spectra_kernel, in_specs=[pl.BlockSpec(memory_space=pl.ANY...  7.3 us
    ppermute x2, starting transfers between devices, shifted(): return lax.ppermute(value, 'rgrp', pairs)  6.22 us
    pallas_call x2, Pallas kernels, cross_of(): pl.pallas_call(kernel, in_specs=[vmem] * len(arrays), out_specs=vmem, out...  5.9 us
  transfers between devices with their start and end apart: 3, of which 3 were waited for; matrix products, arithmetic and copies ran while one was open for 0% of the time, Pallas kernels for 4%

profile of v2, /device:TPU:8, one launch (start us, length us, event | category | flops | bytes accessed | tf_op | source)
XLA Modules:
  0.0 96.8 jit_solution(15355480147568762277)
XLA Ops:
  0.7 7.3 %spectra.1 = (f32[16,128,128]{2,1,0:T(8,128)}, bf16[32,128]{1,0:T(8,128)(2,1)}) custom-call(s32[4]{0:T(128)} %offset_hbm.1, s32[1,32]{1,0:T(1,128)} %order_hbm.1, s32[1]{0:T(128)S(6)} %copy.6.pilot_hbm, bf16[32,9216]{1,0:T(8,128)(2,1)} %traces_hbm.1, bf16[16,2,64,1024]{3,2,1,0:T(8,128)(2,1)} %constant.2.clone.table_hbm), custom_call_target="tpu_custom_call" | custom-call | tf_op jit(solution)/shard_map/spectra/pallas_call | solution.py:143
  8.0 7.7 %collective-permute-start = (bf16[32,128]{1,0:T(8,128)(2,1)}, bf16[32,128]{1,0:T(8,128)(2,1)S(1)}, u32[]{:S(2)}, u32[]{:S(2)}) collective-permute-start(bf16[32,128]{1,0:T(8,128)(2,1)} %get-tuple-element.7), channel_id=1, source_target_pairs={{0,1},{1,0},{2,3},{3,2},{4,5},{5,4},{6,7},{7,6},{8,9},{9,8},{10,11... | collective-permute-start | bytes 24584 | tf_op jit(solution)/shard_map/ppermute | solution.py:319
  15.7 1.8 %collective-permute-done = bf16[32,128]{1,0:T(8,128)(2,1)S(1)} collective-permute-done((bf16[32,128]{1,0:T(8,128)(2,1)}, bf16[32,128]{1,0:T(8,128)(2,1)S(1)}, u32[]{:S(2)}, u32[]{:S(2)}) %collective-permute-start) | collective-permute-done | bytes 8224 | tf_op jit(solution)/shard_map/ppermute | solution.py:319
  17.5 0.7 add.3
  18.2 25.2 %all_to_all.10.guides_ref = bf16[16,32,128]{2,1,0:T(8,128)(2,1)S(1)} all-to-all(bf16[16,32,128]{2,1,0:T(8,128)(2,1)S(1)} %broadcast_in_dim.3), channel_id=1, replica_groups={{0,2,4,6,8,10,12,14,16,18,20,22,24,26,28,30},{1,3,5,7,9,11,13,15,17,19,..., dimensions={0} | all-to-all | bytes 262144 | tf_op jit(solution)/shard_map/all_to_all | solution.py:321
  43.4 0.0 copy-start
  43.4 1.2 %copy-done = f32[16,128,128]{2,1,0:T(8,128)S(1)} copy-done((f32[16,128,128]{2,1,0:T(8,128)S(1)}, f32[16,128,128]{2,1,0:T(8,128)}, u32[]{:S(2)}) %copy-start) | copy-done | bytes 1048600
  44.6 1.3 %whiten.1 = bf16[16,128,128]{2,1,0:T(8,128)(2,1)S(1)} custom-call(bf16[16,32,128]{2,1,0:T(8,128)(2,1)S(1)} %all_to_all.10.guides_ref, f32[16,128,128]{2,1,0:T(8,128)S(1)} %copy-done), custom_call_target="tpu_custom_call" | custom-call | tf_op jit(solution)/shard_map/whiten/pallas_call | solution.py:203
  45.9 18.3 %all_to_all.11.band_ref = bf16[16,128,128]{2,1,0:T(8,128)(2,1)S(1)} all-to-all(bf16[16,128,128]{2,1,0:T(8,128)(2,1)S(1)} %whiten.1), channel_id=1, replica_groups=mesh['freq'=16,'rgrp'=32] {'freq'}, dimensions={0} | all-to-all | bytes 1048576 | tf_op jit(solution)/shard_map/all_to_all | solution.py:330
  64.2 0.8 gather.1.right_ref
  65.0 3.4 %collective-permute-start.2 = (bf16[32,64,128]{2,1,0:T(8,128)(2,1)S(1)}, bf16[32,64,128]{2,1,0:T(8,128)(2,1)S(1)}, u32[]{:S(2)}, u32[]{:S(2)}) collective-permute-start(bf16[32,64,128]{2,1,0:T(8,128)(2,1)S(1)} %gather.1.right_ref), channel_id=1, source_target_pairs={{0,1},{1,2},{2,3},{3,4},{4,5},{5,6},{6,7},{7,8},{8,9},{9,10},{10,1... | collective-permute-start | bytes 1572872 | tf_op jit(solution)/shard_map/ppermute | solution.py:314
  68.4 2.8 %collective-permute-start.1 = (bf16[32,64,128]{2,1,0:T(8,128)(2,1)S(1)}, bf16[32,64,128]{2,1,0:T(8,128)(2,1)S(1)}, u32[]{:S(2)}, u32[]{:S(2)}) collective-permute-start(bf16[32,64,128]{2,1,0:T(8,128)(2,1)S(1)} %gather.1.right_ref), channel_id=1, source_target_pairs={{0,2},{1,3},{2,4},{3,5},{4,6},{5,7},{6,8},{7,9},{8,10},{9,11},{10,... | collective-permute-start | bytes 1572872 | tf_op jit(solution)/shard_map/ppermute | solution.py:314
  71.3 1.8 %left.1.left_ref = bf16[32,64,128]{2,1,0:T(8,128)(2,1)S(1)} custom-call(bf16[32,64,128]{2,1,0:T(8,128)(2,1)S(1)} %gather.1.right_ref), custom_call_target="tpu_custom_call" | custom-call | tf_op jit(solution)/shard_map/left/pallas_call | solution.py:249
  73.1 7.7 %collective-permute-done.2.right_ref = bf16[32,64,128]{2,1,0:T(8,128)(2,1)S(1)} collective-permute-done((bf16[32,64,128]{2,1,0:T(8,128)(2,1)S(1)}, bf16[32,64,128]{2,1,0:T(8,128)(2,1)S(1)}, u32[]{:S(2)}, u32[]{:S(2)}) %collective-permute-start.2) | collective-permute-done | bytes 524320 | tf_op jit(solution)/shard_map/ppermute | solution.py:314
  80.8 2.5 %near_kernel.1.near_ref = bf16[32,32,128]{2,1,0:T(8,128)(2,1)S(1)} custom-call(bf16[32,64,128]{2,1,0:T(8,128)(2,1)S(1)} %left.1.left_ref, bf16[32,64,128]{2,1,0:T(8,128)(2,1)S(1)} %collective-permute-done.2.right_ref), custom_call_target="tpu_custom_call" | custom-call | tf_op jit(solution)/shard_map/near_kernel/pallas_call | solution.py:301
  83.3 10.1 %collective-permute-done.1.right_ref = bf16[32,64,128]{2,1,0:T(8,128)(2,1)S(1)} collective-permute-done((bf16[32,64,128]{2,1,0:T(8,128)(2,1)S(1)}, bf16[32,64,128]{2,1,0:T(8,128)(2,1)S(1)}, u32[]{:S(2)}, u32[]{:S(2)}) %collective-permute-start.1) | collective-permute-done | bytes 524320 | tf_op jit(solution)/shard_map/ppermute | solution.py:314
  93.4 3.4 %far_kernel.1 = bf16[2,32,32,128]{3,2,1,0:T(8,128)(2,1)} custom-call(bf16[32,64,128]{2,1,0:T(8,128)(2,1)S(1)} %left.1.left_ref, bf16[32,64,128]{2,1,0:T(8,128)(2,1)S(1)} %collective-permute-done.1.right_ref, bf16[32,32,128]{2,1,0:T(8,128)(2,1)S(1)} %near_kernel.1.near_ref), custom_call_target="tpu_custom_call" | custom-call | tf_op jit(solution)/shard_map/far_kernel/pallas_call | solution.py:301
  (1 shorter events, 0.0 us)
Async XLA Ops:
  8.0 9.6 %collective-permute-start = (bf16[32,128]{1,0:T(8,128)(2,1)}, bf16[32,128]{1,0:T(8,128)(2,1)S(1)}, u32[]{:S(2)}, u32[]{:S(2)}) collective-permute-start(bf16[32,128]{1,0:T(8,128)(2,1)} %get-tuple-element.7), channel_id=1, source_target_pairs={{0,1},{1,0},{2,3},{3,2},{4,5},{5,4},{6,7},{7,6},{8,9},{9,8},{10,11... | collective-permute-start | bytes 24584 | tf_op jit(solution)/shard_map/ppermute | solution.py:319
  43.4 1.2 %copy-start = (f32[16,128,128]{2,1,0:T(8,128)S(1)}, f32[16,128,128]{2,1,0:T(8,128)}, u32[]{:S(2)}) copy-start(f32[16,128,128]{2,1,0:T(8,128)} %get-tuple-element.8.block_ref) | copy-start | bytes 3145732
  65.0 15.8 %collective-permute-start.2 = (bf16[32,64,128]{2,1,0:T(8,128)(2,1)S(1)}, bf16[32,64,128]{2,1,0:T(8,128)(2,1)S(1)}, u32[]{:S(2)}, u32[]{:S(2)}) collective-permute-start(bf16[32,64,128]{2,1,0:T(8,128)(2,1)S(1)} %gather.1.right_ref), channel_id=1, source_target_pairs={{0,1},{1,2},{2,3},{3,4},{4,5},{5,6},{6,7},{7,8},{8,9},{9,10},{10,1... | collective-permute-start | bytes 1572872 | tf_op jit(solution)/shard_map/ppermute | solution.py:314
  68.4 25.0 %collective-permute-start.1 = (bf16[32,64,128]{2,1,0:T(8,128)(2,1)S(1)}, bf16[32,64,128]{2,1,0:T(8,128)(2,1)S(1)}, u32[]{:S(2)}, u32[]{:S(2)}) collective-permute-start(bf16[32,64,128]{2,1,0:T(8,128)(2,1)S(1)} %gather.1.right_ref), channel_id=1, source_target_pairs={{0,2},{1,3},{2,4},{3,5},{4,6},{5,7},{6,8},{7,9},{8,10},{9,11},{10,... | collective-permute-start | bytes 1572872 | tf_op jit(solution)/shard_map/ppermute | solution.py:314

commit v3 on v2

--- a/solution.py
+++ b/solution.py
@@ -19,6 +19,7 @@
 SPAN = 9216
 ROWS = SEG * PAIRS
 LANES = 128
+CHIPS = 8
 BF16 = jnp.bfloat16
 F32 = jnp.float32
 
@@ -37,6 +38,12 @@
 
 def lane_index(rows):
     return lax.broadcasted_iota(jnp.int32, (rows, LANES), 1)
+
+
+def relative(band):
+    mine = lax.axis_index("freq")
+    place = (band // 8 + mine // 8) % 2 * 4 + ((band // 2) % 4 - (mine // 2) % 4 + 4) % 4
+    return (band + mine) % 2 == 0, place
 
 
 def cut_windows(offset_ref, order_ref, traces_ref, wave_ref):
@@ -72,7 +79,7 @@
 
 
 def spectra_kernel(
-    offset_hbm, order_hbm, pilot_hbm, traces_hbm, table_hbm, block_ref, guide_ref,
+    offset_hbm, order_hbm, pilot_hbm, traces_hbm, table_hbm, same_ref, other_ref, guide_ref,
     offset_ref, order_ref, pilot_ref, traces_ref, table_ref, wave_ref, power_ref, sems, table_sems,
 ):
     small = [
@@ -124,6 +131,7 @@
                     real * real + imag * imag, lax.rem(place - channel + LANES, LANES), 1
                 )
                 power_ref[...] = jnp.where(lane % 32 == place, power, power_ref[...])
+            lines = []
             for seg in range(SEG):
                 line = None
                 for side in range(2):
@@ -133,19 +141,35 @@
                         if group != seg:
                             part = pltpu.roll(part, (group - seg) * 32 % LANES, 1)
                         line = part if line is None else jnp.where(lane // 32 == group, part, line)
-                block_ref[band, seg * PAIRS : (seg + 1) * PAIRS, :] = line
+                lines.append(line)
+            value = jnp.concatenate(lines, axis=0).astype(BF16)
+            same_core, place = relative(band)
+
+            @pl.when(same_core)
+            def _():
+                same_ref[place] = value
+
+            @pl.when(jnp.logical_not(same_core))
+            def _():
+                other_ref[place] = value
+
     mine = pilot_ref[0] // CH == lax.axis_index("rgrp")
     guide_ref[...] = jnp.where(mine, jnp.sqrt(power_ref[...]), 0.0).astype(BF16)
 
 
 def spectra_of(offsets, order, pilot, traces, table):
     vmem = pl.BlockSpec(memory_space=pltpu.VMEM)
+    offsets, order, traces, table = (
+        pltpu.with_memory_space_constraint(value, pltpu.HBM)
+        for value in (offsets, order, traces, table)
+    )
     return pl.pallas_call(
         spectra_kernel,
         in_specs=[pl.BlockSpec(memory_space=pl.ANY)] * 5,
-        out_specs=[vmem, vmem],
+        out_specs=[vmem, vmem, vmem],
         out_shape=[
-            jax.ShapeDtypeStruct((BANDS, ROWS, LANES), F32),
+            jax.ShapeDtypeStruct((CHIPS, ROWS, LANES), BF16),
+            jax.ShapeDtypeStruct((CHIPS, ROWS, LANES), BF16),
             jax.ShapeDtypeStruct((PAIRS, LANES), BF16),
         ],
         scratch_shapes=[
@@ -159,28 +183,29 @@
             pltpu.SemaphoreType.DMA((4,)),
             pltpu.SemaphoreType.DMA((4,)),
         ],
-        compiler_params=pltpu.CompilerParams(vmem_limit_bytes=56 * 1024 * 1024),
+        compiler_params=pltpu.CompilerParams(vmem_limit_bytes=16 * 1024 * 1024),
         name="spectra",
     )(offsets, order, pilot, traces, table)
 
 
-def whiten_kernel(guides_ref, block_ref, white_ref, value_ref, guide_ref):
+def level_kernel(guides_ref, same_ref, other_ref, note_ref, guide_ref, turned_ref):
     guide = guides_ref[0].astype(F32)
     for line in range(1, 16):
         guide = guide + guides_ref[line].astype(F32)
     guide_ref[...] = guide
-    lane = lane_index(PAIRS)
-    even = (lane // 32) % 2 == 0
+    turned_ref[...] = jnp.transpose(jnp.concatenate([guide] * (LANES // PAIRS), axis=0))
+    even = (lane_index(PAIRS) // 32) % 2 == 0
     totals = [jnp.zeros((PAIRS, LANES), F32) for _ in range(SEG)]
     for band in range(BANDS):
+        same_core, place = relative(band)
         for seg in range(SEG):
             first = 32 * seg + 2 * band
             rows = slice(seg * PAIRS, (seg + 1) * PAIRS)
             weight = jnp.where(
                 even, guide_ref[:, first : first + 1], guide_ref[:, first + 1 : first + 2]
             )
-            value = block_ref[band, rows, :] * weight
-            value_ref[band, rows, :] = value
+            block = jnp.where(same_core, same_ref[place, rows, :], other_ref[place, rows, :])
+            value = block.astype(F32) * weight
             totals[seg] = totals[seg] + value * value
     levels = []
     for seg in range(SEG):
@@ -189,31 +214,56 @@
         total = total + pltpu.roll(total, 64, 1)
         total = total + pltpu.roll(total, 32, 1)
         levels.append((total * (0.1 / (64.0 * BANDS)) + 1e-06)[:1])
+    level = jnp.concatenate(levels, axis=0)
+    low = lane_index(SEG) < PAIRS
     for band in range(BANDS):
-        for seg in range(SEG):
-            rows = slice(seg * PAIRS, (seg + 1) * PAIRS)
-            value = value_ref[band, rows, :]
-            energy = value * value
-            energy = energy + pltpu.roll(energy, 64, 1)
-            white_ref[band, rows, :] = (value * lax.rsqrt(energy + levels[seg])).astype(BF16)
-
-
-def whitened_of(guides, blocks):
-    vmem = pl.BlockSpec(memory_space=pltpu.VMEM)
-    return pl.pallas_call(
-        whiten_kernel,
-        in_specs=[vmem, vmem],
+        even_rows = turned_ref[pl.ds(2 * band, SEG, stride=32), :]
+        odd_rows = turned_ref[pl.ds(2 * band + 1, SEG, stride=32), :]
+        power = jnp.where(low, even_rows, odd_rows)
+        note_ref[band] = jnp.concatenate([power, level, power, level], axis=0).astype(BF16)
+
+
+def notes_of(guides, same, other):
+    vmem = pl.BlockSpec(memory_space=pltpu.VMEM)
+    return pl.pallas_call(
+        level_kernel,
+        in_specs=[vmem] * 3,
         out_specs=vmem,
-        out_shape=jax.ShapeDtypeStruct((BANDS, ROWS, LANES), BF16),
-        scratch_shapes=[pltpu.VMEM((BANDS, ROWS, LANES), F32), pltpu.VMEM((PAIRS, LANES), F32)],
+        out_shape=jax.ShapeDtypeStruct((BANDS, 16, LANES), BF16),
+        scratch_shapes=[pltpu.VMEM((PAIRS, LANES), F32), pltpu.VMEM((LANES, LANES), F32)],
         compiler_params=pltpu.CompilerParams(vmem_limit_bytes=32 * 1024 * 1024),
-        name="whiten",
-    )(guides, blocks)
-
-
-def gather_kernel(band_ref, right_ref, wide_ref):
-    for window in range(BANDS):
-        wide_ref[window * ROWS : (window + 1) * ROWS, :] = band_ref[window].astype(F32)
+        name="level",
+    )(guides, same, other)
+
+
+def merge_kernel(same_ref, other_ref, *out_refs):
+    for k, out_ref in enumerate(out_refs):
+        out_ref[0] = same_ref[k + 1]
+        out_ref[1] = other_ref[k + 1]
+
+
+def merged_of(same, other):
+    vmem = pl.BlockSpec(memory_space=pltpu.VMEM)
+    return pl.pallas_call(
+        merge_kernel,
+        in_specs=[vmem] * 2,
+        out_specs=[vmem] * (CHIPS - 1),
+        out_shape=[jax.ShapeDtypeStruct((2, ROWS, LANES), BF16)] * (CHIPS - 1),
+        compiler_params=pltpu.CompilerParams(vmem_limit_bytes=32 * 1024 * 1024),
+        name="merge",
+    )(same, other)
+
+
+def gather_kernel(same_ref, other_ref, *refs):
+    part_refs, right_ref, wide_ref = refs[:-2], refs[-2], refs[-1]
+    for place in range(CHIPS):
+        for core in range(2):
+            if place == 0:
+                part = (same_ref, other_ref)[core][0]
+            else:
+                part = part_refs[place - 1][core]
+            window = 2 * place + core
+            wide_ref[window * ROWS : (window + 1) * ROWS, :] = part.astype(F32)
 
     def bin_pair(pair, carry):
         right_ref[pair] = wide_ref[pl.ds(pair, BANDS * SEG, stride=PAIRS), :].astype(BF16)
@@ -222,45 +272,75 @@
     lax.fori_loop(0, PAIRS, bin_pair, 0, unroll=4)
 
 
-def gathered_of(banded):
+def gathered_of(same, other, parts):
     vmem = pl.BlockSpec(memory_space=pltpu.VMEM)
     return pl.pallas_call(
         gather_kernel,
-        in_specs=[vmem],
+        in_specs=[vmem] * (1 + CHIPS),
         out_specs=vmem,
         out_shape=jax.ShapeDtypeStruct((PAIRS, BANDS * SEG, LANES), BF16),
         scratch_shapes=[pltpu.VMEM((BANDS * ROWS, LANES), F32)],
         compiler_params=pltpu.CompilerParams(vmem_limit_bytes=32 * 1024 * 1024),
         name="gather",
-    )(banded)
-
-
-def left_kernel(right_ref, left_ref):
-    def bin_pair(pair, carry):
-        turned = jnp.transpose(right_ref[pair].astype(F32))
+    )(same, other, *parts)
+
+
+def note_rows(note_ref, first, wide_ref):
+    mine = lax.axis_index("freq")
+    for place in range(CHIPS):
+        for core in range(2):
+            chip = (mine // 8 + place // 4) % 2 * 4 + ((mine // 2) % 4 - place % 4 + 4) % 4
+            window = 2 * chip + (mine + core) % 2
+            at = (2 * place + core) * SEG
+            wide_ref[at : at + SEG, :] = note_ref[window].astype(F32)[first : first + SEG]
+
+
+def whitened(value, level):
+    energy = value * value
+    energy = energy + pltpu.roll(energy, 64, 1)
+    return value * lax.rsqrt(energy + level)
+
+
+def left_kernel(right_ref, note_ref, left_ref, power_ref, level_ref, wide_ref):
+    note_rows(note_ref, SEG, level_ref)
+    note_rows(note_ref, 0, wide_ref)
+    level = level_ref[...]
+    even = (lane_index(BANDS * SEG) // 32) % 2 == 0
+    for pair in range(PAIRS):
+        power = jnp.where(
+            even, wide_ref[:, pair : pair + 1], wide_ref[:, PAIRS + pair : PAIRS + pair + 1]
+        )
+        power_ref[pair] = power.astype(BF16)
+        white = whitened(right_ref[pair].astype(F32) * power, level)
+        turned = jnp.transpose(white)
         left_ref[pair] = jnp.concatenate([turned[:64], turned[64:]], axis=1).astype(BF16)
-        return carry
-
-    lax.fori_loop(0, PAIRS, bin_pair, 0, unroll=4)
-
-
-def left_of(right):
-    vmem = pl.BlockSpec(memory_space=pltpu.VMEM)
+
+
+def left_of(right, note):
+    vmem = pl.BlockSpec(memory_space=pltpu.VMEM)
+    rows = pltpu.VMEM((BANDS * SEG, LANES), F32)
     return pl.pallas_call(
         left_kernel,
-        in_specs=[vmem],
-        out_specs=vmem,
-        out_shape=jax.ShapeDtypeStruct((PAIRS, 2 * CH, LANES), BF16),
+        in_specs=[vmem] * 2,
+        out_specs=[vmem] * 2,
+        out_shape=[
+            jax.ShapeDtypeStruct((PAIRS, 2 * CH, LANES), BF16),
+            jax.ShapeDtypeStruct((PAIRS, BANDS * SEG, LANES), BF16),
+        ],
+        scratch_shapes=[rows, rows],
         compiler_params=pltpu.CompilerParams(vmem_limit_bytes=32 * 1024 * 1024),
         name="left",
-    )(right)
-
-
-def cross_one(left_ref, right_ref, stack_ref, store):
+    )(right, note)
+
+
+def cross_one(left_ref, power_ref, right_ref, note_ref, stack_ref, level_ref, store):
     side = jnp.where(lane_index(BANDS * SEG) < 64, 1.0, -1.0)
+    note_rows(note_ref, SEG, level_ref)
+    level = level_ref[...]
 
     def bin_pair(pair, carry):
-        right = right_ref[pair].astype(F32)
+        value = right_ref[pair].astype(F32) * power_ref[pair].astype(F32)
+        right = whitened(value, level)
         mix = jnp.concatenate([right * side, pltpu.roll(right, 64, 1)], axis=0).astype(BF16)
         product = jnp.dot(left_ref[pair], mix, preferred_element_type=F32)
         stack_ref[pl.ds(pl.multiple_of(pair * 2 * CH, 2 * CH), 2 * CH), :] = product
@@ -281,19 +361,19 @@
         store(2 * half + 1, jnp.where(low, pltpu.roll(real, 64, 1), imag).astype(BF16))
 
 
-def near_kernel(left_ref, right_ref, out_ref, stack_ref):
+def near_kernel(left_ref, power_ref, right_ref, note_ref, out_ref, stack_ref, level_ref):
     def store(channel, lines):
         out_ref[channel] = lines
 
-    cross_one(left_ref, right_ref, stack_ref, store)
-
-
-def far_kernel(left_ref, right_ref, near_ref, out_ref, stack_ref):
+    cross_one(left_ref, power_ref, right_ref, note_ref, stack_ref, level_ref, store)
+
+
+def far_kernel(left_ref, power_ref, right_ref, note_ref, near_ref, out_ref, stack_ref, level_ref):
     def store(channel, lines):
         out_ref[1, channel] = lines
 
     out_ref[0] = near_ref[...]
-    cross_one(left_ref, right_ref, stack_ref, store)
+    cross_one(left_ref, power_ref, right_ref, note_ref, stack_ref, level_ref, store)
 
 
 def cross_of(kernel, shape, *arrays):
@@ -303,7 +383,10 @@
         in_specs=[vmem] * len(arrays),
         out_specs=vmem,
         out_shape=jax.ShapeDtypeStruct(shape, BF16),
-        scratch_shapes=[pltpu.VMEM((64 * CH, LANES), F32)],
+        scratch_shapes=[
+            pltpu.VMEM((64 * CH, LANES), F32),
+            pltpu.VMEM((BANDS * SEG, LANES), F32),
+        ],
         compiler_params=pltpu.CompilerParams(vmem_limit_bytes=32 * 1024 * 1024),
         name=kernel.__name__,
     )(*arrays)
@@ -314,8 +397,22 @@
     return lax.ppermute(value, "rgrp", pairs)
 
 
+def to_chip(value, place):
+    pairs = []
+    for f in range(BANDS):
+        chip = (f // 8 + place // 4) % 2 * 4 + (f // 2 + place) % 4
+        pairs.append((f, 2 * chip + f % 2))
+    return lax.ppermute(value, "freq", pairs)
+
+
 def local(table, traces, segment_offsets, channel_order, pilot_channel):
-    blocks, guide = spectra_of(segment_offsets, channel_order, pilot_channel, traces, table)
+    same, other, guide = spectra_of(segment_offsets, channel_order, pilot_channel, traces, table)
+    swapped = lax.ppermute(other, "freq", [(f, f ^ 1) for f in range(BANDS)])
+    merged = merged_of(same, swapped)
+    parts = [to_chip(value, place + 1) for place, value in enumerate(merged)]
+    own = gathered_of(same, swapped, parts)
+    near, far = shifted(own, 1), shifted(own, 2)
+
     guide = guide + lax.ppermute(guide, "rgrp", [(g, g ^ 1) for g in range(32)])
     lines = [[2 * z + side for z in range(16)] for side in range(2)]
     guides = lax.all_to_all(
@@ -326,13 +423,13 @@
         tiled=True,
         axis_index_groups=lines,
     )
-    white = whitened_of(guides, blocks)
-    banded = lax.all_to_all(white, "freq", split_axis=0, concat_axis=0, tiled=True)
-    own = gathered_of(banded)
-    near, far = shifted(own, 1), shifted(own, 2)
-    left = left_of(own)
-    first = cross_of(near_kernel, (CH, CH, LANES), left, near)
-    return cross_of(far_kernel, (2, CH, CH, LANES), left, far, first)
+    notes = notes_of(guides, same, other)
+    note = lax.all_to_all(notes, "freq", split_axis=0, concat_axis=0, tiled=True)
+    left, power = left_of(own, note)
+    first = cross_of(near_kernel, (CH, CH, LANES), left, power, near, shifted(note, 1))
+    return cross_of(
+        far_kernel, (2, CH, CH, LANES), left, power, far, shifted(note, 2), first
+    )
 
 
 def solution(mesh):

time: 97.1 us -> 111 us (1.14)
  the two profiles are of different devices: /device:TPU:8 before, /device:TPU:1 now
where the time goes in v3:
time: 111 us; the launch traced here: 110 us
  starting transfers between devices  57.3 us (52%)
  Pallas kernels  25.5 us (23%)
  blocking collectives  17.4 us (16%)
  waiting for transfers between devices  8.29 us (7%)
    ppermute x7, starting transfers between devices, to_chip(): return lax.ppermute(value, 'freq', pairs)  22.6 us
    all_to_all x1, blocking collectives, local(): lax.all_to_all(notes, 'freq', split_axis=0, concat_axis=0, tiled=True)  17.4 us
    all_to_all x1, starting transfers between devices, local(): lax.all_to_all(jnp.broadcast_to(guide, (16, PAIRS, LANES)), 'rgrp', split...  12.9 us
    ppermute x4, starting transfers between devices, shifted(): return lax.ppermute(value, 'rgrp', pairs)  11.1 us
    pallas_call x1, Pallas kernels, spectra_of(): pl.pallas_call(spectra_kernel, in_specs=[pl.BlockSpec(memory_space=pl.ANY...  8.87 us
    ppermute x1, starting transfers between devices, local(): swapped = lax.ppermute(other, 'freq', [(f, f ^ 1) for f in range(BANDS)])  8.79 us
    pallas_call x2, Pallas kernels, cross_of(): pl.pallas_call(kernel, in_specs=[vmem] * len(arrays), out_specs=vmem, out...  7.41 us
    pallas_call x1, Pallas kernels, left_of(): pl.pallas_call(left_kernel, in_specs=[vmem] * 2, out_specs=[vmem] * 2, ou...  7.4 us
  transfers between devices with their start and end apart: 14, of which 3 were waited for; matrix products, arithmetic and copies ran while one was open for 1% of the time, Pallas kernels for 11%

profile of v3, /device:TPU:1, one launch (start us, length us, event | category | flops | bytes accessed | tf_op | source)
XLA Modules:
  0.0 110.1 jit_solution(9205843496416923667)
XLA Ops:
  0.7 8.9 %spectra.1 = (bf16[8,128,128]{2,1,0:T(8,128)(2,1)S(1)}, bf16[8,128,128]{2,1,0:T(8,128)(2,1)S(1)}, bf16[32,128]{1,0:T(8,128)(2,1)S(1)}) custom-call(s32[4]{0:T(128)} %offset_hbm.1, s32[1,32]{1,0:T(1,128)} %order_hbm.1, s32[1]{0:T(128)S(6)} %copy.6.pilot_hbm, bf16[32,9216]{1,0:T(8,128)(2,1)} %traces_hbm.1, bf16[16,2,64,1024]{3,2,1,0:T(8,128)(2,1)} %constant.2.clone.table_hbm), custom_call_target="tpu_custom_call" | custom-call | tf_op jit(solution)/shard_map/spectra/pallas_call | solution.py:166
  9.5 8.8 %collective-permute-start = (bf16[8,128,128]{2,1,0:T(8,128)(2,1)S(1)}, bf16[8,128,128]{2,1,0:T(8,128)(2,1)S(1)}, u32[]{:S(2)}, u32[]{:S(2)}) collective-permute-start(bf16[8,128,128]{2,1,0:T(8,128)(2,1)S(1)} %get-tuple-element.18.other_ref), channel_id=1, source_target_pairs={{0,32},{32,0},{64,96},{96,64},{128,160},{160,128},{192,224},{224,1... | collective-permute-start | bytes 786440 | tf_op jit(solution)/shard_map/ppermute | solution.py:410
  18.3 1.1 %collective-permute-done.other_ref = bf16[8,128,128]{2,1,0:T(8,128)(2,1)S(1)} collective-permute-done((bf16[8,128,128]{2,1,0:T(8,128)(2,1)S(1)}, bf16[8,128,128]{2,1,0:T(8,128)(2,1)S(1)}, u32[]{:S(2)}, u32[]{:S(2)}) %collective-permute-start) | collective-permute-done | bytes 262176 | tf_op jit(solution)/shard_map/ppermute | solution.py:410
  19.5 1.9 %collective-permute-start.1 = (bf16[2,128,128]{2,1,0:T(8,128)(2,1)S(1)}, bf16[2,128,128]{2,1,0:T(8,128)(2,1)S(1)}, u32[]{:S(2)}, u32[]{:S(2)}) collective-permute-start(bf16[2,128,128]{2,1,0:T(8,128)(2,1)S(1)} %get-tuple-element.19), channel_id=1, source_target_pairs={{0,64},{32,96},{64,128},{96,160},{128,192},{160,224},{192,0},{224,... | collective-permute-start | bytes 196616 | tf_op jit(solution)/shard_map/ppermute | solution.py:405
  21.4 1.9 %collective-permute-start.2 = (bf16[2,128,128]{2,1,0:T(8,128)(2,1)S(1)}, bf16[2,128,128]{2,1,0:T(8,128)(2,1)S(1)}, u32[]{:S(2)}, u32[]{:S(2)}) collective-permute-start(bf16[2,128,128]{2,1,0:T(8,128)(2,1)S(1)} %get-tuple-element.20), channel_id=1, source_target_pairs={{0,128},{32,160},{64,192},{96,224},{128,0},{160,32},{192,64},{224,... | collective-permute-start | bytes 196616 | tf_op jit(solution)/shard_map/ppermute | solution.py:405
  23.4 1.9 %collective-permute-start.8 = (bf16[32,128]{1,0:T(8,128)(2,1)S(1)}, bf16[32,128]{1,0:T(8,128)(2,1)S(1)}, u32[]{:S(2)}, u32[]{:S(2)}) collective-permute-start(bf16[32,128]{1,0:T(8,128)(2,1)S(1)} %get-tuple-element.26), channel_id=1, source_target_pairs={{0,1},{1,0},{2,3},{3,2},{4,5},{5,4},{6,7},{7,6},{8,9},{9,8},{10,11... | collective-permute-start | bytes 24584 | tf_op jit(solution)/shard_map/ppermute | solution.py:416
  25.3 2.8 %collective-permute-done.8 = bf16[32,128]{1,0:T(8,128)(2,1)S(1)} collective-permute-done((bf16[32,128]{1,0:T(8,128)(2,1)S(1)}, bf16[32,128]{1,0:T(8,128)(2,1)S(1)}, u32[]{:S(2)}, u32[]{:S(2)}) %collective-permute-start.8) | collective-permute-done | bytes 8224 | tf_op jit(solution)/shard_map/ppermute | solution.py:416
  28.1 0.7 broadcast_in_dim.3
  28.7 12.9 %all-to-all-start = ((bf16[16,32,128]{2,1,0:T(8,128)(2,1)}), bf16[16,32,128]{2,1,0:T(8,128)(2,1)S(1)}, u32[]{:S(2)}, u32[]{:S(2)}) async-start(bf16[16,32,128]{2,1,0:T(8,128)(2,1)} %broadcast_in_dim.3), calls=%async_computation | async-start | bytes 262144 | tf_op jit(solution)/shard_map/all_to_all | solution.py:418
  41.6 3.1 %collective-permute-start.3 = (bf16[2,128,128]{2,1,0:T(8,128)(2,1)S(1)}, bf16[2,128,128]{2,1,0:T(8,128)(2,1)S(1)}, u32[]{:S(2)}, u32[]{:S(2)}) collective-permute-start(bf16[2,128,128]{2,1,0:T(8,128)(2,1)S(1)} %get-tuple-element.21), channel_id=1, source_target_pairs={{0,192},{32,224},{64,0},{96,32},{128,64},{160,96},{192,128},{224,1... | collective-permute-start | bytes 196616 | tf_op jit(solution)/shard_map/ppermute | solution.py:405
  44.7 4.8 %collective-permute-start.4 = (bf16[2,128,128]{2,1,0:T(8,128)(2,1)S(1)}, bf16[2,128,128]{2,1,0:T(8,128)(2,1)S(1)}, u32[]{:S(2)}, u32[]{:S(2)}) collective-permute-start(bf16[2,128,128]{2,1,0:T(8,128)(2,1)S(1)} %get-tuple-element.22), channel_id=1, source_target_pairs={{0,256},{32,288},{64,320},{96,352},{128,384},{160,416},{192,448},{... | collective-permute-start | bytes 196616 | tf_op jit(solution)/shard_map/ppermute | solution.py:405
  49.5 2.0 %collective-permute-start.5 = (bf16[2,128,128]{2,1,0:T(8,128)(2,1)S(1)}, bf16[2,128,128]{2,1,0:T(8,128)(2,1)S(1)}, u32[]{:S(2)}, u32[]{:S(2)}) collective-permute-start(bf16[2,128,128]{2,1,0:T(8,128)(2,1)S(1)} %get-tuple-element.23), channel_id=1, source_target_pairs={{0,320},{32,352},{64,384},{96,416},{128,448},{160,480},{192,256},{... | collective-permute-start | bytes 196616 | tf_op jit(solution)/shard_map/ppermute | solution.py:405
  51.5 0.0 collective-permute-done.1.refs_0_
  51.5 5.4 %collective-permute-start.6 = (bf16[2,128,128]{2,1,0:T(8,128)(2,1)S(1)}, bf16[2,128,128]{2,1,0:T(8,128)(2,1)S(1)}, u32[]{:S(2)}, u32[]{:S(2)}) collective-permute-start(bf16[2,128,128]{2,1,0:T(8,128)(2,1)S(1)} %get-tuple-element.24), channel_id=1, source_target_pairs={{0,384},{32,416},{64,448},{96,480},{128,256},{160,288},{192,320},{... | collective-permute-start | bytes 196616 | tf_op jit(solution)/shard_map/ppermute | solution.py:405
  57.0 0.0 collective-permute-done.2.refs_1_
  57.0 3.4 %collective-permute-start.7 = (bf16[2,128,128]{2,1,0:T(8,128)(2,1)S(1)}, bf16[2,128,128]{2,1,0:T(8,128)(2,1)S(1)}, u32[]{:S(2)}, u32[]{:S(2)}) collective-permute-start(bf16[2,128,128]{2,1,0:T(8,128)(2,1)S(1)} %get-tuple-element.25), channel_id=1, source_target_pairs={{0,448},{32,480},{64,256},{96,288},{128,320},{160,352},{192,384},{... | collective-permute-start | bytes 196616 | tf_op jit(solution)/shard_map/ppermute | solution.py:405
  60.4 0.0 collective-permute-done.3.refs_2_
  60.4 0.0 collective-permute-done.4.refs_3_
  60.4 0.0 collective-permute-done.5.refs_4_
  60.5 0.0 collective-permute-done.6.refs_5_
  60.5 4.3 %collective-permute-done.7.refs_6_ = bf16[2,128,128]{2,1,0:T(8,128)(2,1)S(1)} collective-permute-done((bf16[2,128,128]{2,1,0:T(8,128)(2,1)S(1)}, bf16[2,128,128]{2,1,0:T(8,128)(2,1)S(1)}, u32[]{:S(2)}, u32[]{:S(2)}) %collective-permute-start.7) | collective-permute-done | bytes 65568 | tf_op jit(solution)/shard_map/ppermute | solution.py:405
  64.8 0.8 gather.1.right_ref
  65.6 2.3 %collective-permute-start.11 = (bf16[32,64,128]{2,1,0:T(8,128)(2,1)S(1)}, bf16[32,64,128]{2,1,0:T(8,128)(2,1)S(1)}, u32[]{:S(2)}, u32[]{:S(2)}) collective-permute-start(bf16[32,64,128]{2,1,0:T(8,128)(2,1)S(1)} %gather.1.right_ref), channel_id=1, source_target_pairs={{0,1},{1,2},{2,3},{3,4},{4,5},{5,6},{6,7},{7,8},{8,9},{9,10},{10,1... | collective-permute-start | bytes 1572872 | tf_op jit(solution)/shard_map/ppermute | solution.py:397
  68.0 3.1 %collective-permute-start.9 = (bf16[32,64,128]{2,1,0:T(8,128)(2,1)S(1)}, bf16[32,64,128]{2,1,0:T(8,128)(2,1)S(1)}, u32[]{:S(2)}, u32[]{:S(2)}) collective-permute-start(bf16[32,64,128]{2,1,0:T(8,128)(2,1)S(1)} %gather.1.right_ref), channel_id=1, source_target_pairs={{0,2},{1,3},{2,4},{3,5},{4,6},{5,7},{6,8},{7,9},{8,10},{9,11},{10,... | collective-permute-start | bytes 1572872 | tf_op jit(solution)/shard_map/ppermute | solution.py:397
  71.1 0.0 all-to-all-done.guides_ref
  71.1 1.0 level.1
  72.1 17.4 %all_to_all.10.note_ref = bf16[16,16,128]{2,1,0:T(8,128)(2,1)S(1)} all-to-all(bf16[16,16,128]{2,1,0:T(8,128)(2,1)S(1)} %level.1), channel_id=1, replica_groups=mesh['freq'=16,'rgrp'=32] {'freq'}, dimensions={0} | all-to-all | bytes 131072 | tf_op jit(solution)/shard_map/all_to_all | solution.py:427
  89.6 2.6 %collective-permute-start.12 = (bf16[16,16,128]{2,1,0:T(8,128)(2,1)S(1)}, bf16[16,16,128]{2,1,0:T(8,128)(2,1)S(1)}, u32[]{:S(2)}, u32[]{:S(2)}) collective-permute-start(bf16[16,16,128]{2,1,0:T(8,128)(2,1)S(1)} %all_to_all.10.note_ref), channel_id=1, source_target_pairs={{0,1},{1,2},{2,3},{3,4},{4,5},{5,6},{6,7},{7,8},{8,9},{9,10},{10,1... | collective-permute-start | bytes 196616 | tf_op jit(solution)/shard_map/ppermute | solution.py:397
  92.2 3.1 %collective-permute-start.10 = (bf16[16,16,128]{2,1,0:T(8,128)(2,1)S(1)}, bf16[16,16,128]{2,1,0:T(8,128)(2,1)S(1)}, u32[]{:S(2)}, u32[]{:S(2)}) collective-permute-start(bf16[16,16,128]{2,1,0:T(8,128)(2,1)S(1)} %all_to_all.10.note_ref), channel_id=1, source_target_pairs={{0,2},{1,3},{2,4},{3,5},{4,6},{5,7},{6,8},{7,9},{8,10},{9,11},{10,... | collective-permute-start | bytes 196616 | tf_op jit(solution)/shard_map/ppermute | solution.py:397
  95.3 7.4 %left.1 = (bf16[32,64,128]{2,1,0:T(8,128)(2,1)S(1)}, bf16[32,64,128]{2,1,0:T(8,128)(2,1)S(1)}) custom-call(bf16[32,64,128]{2,1,0:T(8,128)(2,1)S(1)} %gather.1.right_ref, bf16[16,16,128]{2,1,0:T(8,128)(2,1)S(1)} %all_to_all.10.note_ref), custom_call_target="tpu_custom_call" | custom-call | tf_op jit(solution)/shard_map/left/pallas_call | solution.py:322
  102.7 0.0 collective-permute-done.12.note_ref
  102.7 0.0 collective-permute-done.11.right_ref
  102.7 3.3 %near_kernel.1.near_ref = bf16[32,32,128]{2,1,0:T(8,128)(2,1)S(1)} custom-call(bf16[32,64,128]{2,1,0:T(8,128)(2,1)S(1)} %get-tuple-element.27.left_ref, bf16[32,64,128]{2,1,0:T(8,128)(2,1)S(1)} %get-tuple-element.28.power_ref, bf16[32,64,128]{2,1,0:T(8,128)(2,1)S(1)} %collective-permute-done.11.right_ref, ...), custom_call_target="tpu_custom_call" | custom-call | tf_op jit(solution)/shard_map/near_kernel/pallas_call | solution.py:381
  106.0 0.0 collective-permute-done.10.note_ref
  106.0 0.0 collective-permute-done.9.right_ref
  106.0 4.1 %far_kernel.1 = bf16[2,32,32,128]{3,2,1,0:T(8,128)(2,1)} custom-call(bf16[32,64,128]{2,1,0:T(8,128)(2,1)S(1)} %get-tuple-element.27.left_ref, bf16[32,64,128]{2,1,0:T(8,128)(2,1)S(1)} %get-tuple-element.28.power_ref, bf16[32,64,128]{2,1,0:T(8,128)(2,1)S(1)} %collective-permute-done.9.right_ref, bf16[16,16,128]{2,1,0:T(8,128)(2,1)S(1)} %collective-permute-done.10.note_ref, ...), custom_call_target="tpu_custom_call" | custom-call | tf_op jit(solution)/shard_map/far_kernel/pallas_call | solution.py:381
  (2 shorter events, 0.0 us)
Async XLA Ops:
  9.5 9.9 %collective-permute-start = (bf16[8,128,128]{2,1,0:T(8,128)(2,1)S(1)}, bf16[8,128,128]{2,1,0:T(8,128)(2,1)S(1)}, u32[]{:S(2)}, u32[]{:S(2)}) collective-permute-start(bf16[8,128,128]{2,1,0:T(8,128)(2,1)S(1)} %get-tuple-element.18.other_ref), channel_id=1, source_target_pairs={{0,32},{32,0},{64,96},{96,64},{128,160},{160,128},{192,224},{224,1... | collective-permute-start | bytes 786440 | tf_op jit(solution)/shard_map/ppermute | solution.py:410
  19.5 32.0 %collective-permute-start.1 = (bf16[2,128,128]{2,1,0:T(8,128)(2,1)S(1)}, bf16[2,128,128]{2,1,0:T(8,128)(2,1)S(1)}, u32[]{:S(2)}, u32[]{:S(2)}) collective-permute-start(bf16[2,128,128]{2,1,0:T(8,128)(2,1)S(1)} %get-tuple-element.19), channel_id=1, source_target_pairs={{0,64},{32,96},{64,128},{96,160},{128,192},{160,224},{192,0},{224,... | collective-permute-start | bytes 196616 | tf_op jit(solution)/shard_map/ppermute | solution.py:405
  21.4 35.5 %collective-permute-start.2 = (bf16[2,128,128]{2,1,0:T(8,128)(2,1)S(1)}, bf16[2,128,128]{2,1,0:T(8,128)(2,1)S(1)}, u32[]{:S(2)}, u32[]{:S(2)}) collective-permute-start(bf16[2,128,128]{2,1,0:T(8,128)(2,1)S(1)} %get-tuple-element.20), channel_id=1, source_target_pairs={{0,128},{32,160},{64,192},{96,224},{128,0},{160,32},{192,64},{224,... | collective-permute-start | bytes 196616 | tf_op jit(solution)/shard_map/ppermute | solution.py:405
  23.4 4.7 %collective-permute-start.8 = (bf16[32,128]{1,0:T(8,128)(2,1)S(1)}, bf16[32,128]{1,0:T(8,128)(2,1)S(1)}, u32[]{:S(2)}, u32[]{:S(2)}) collective-permute-start(bf16[32,128]{1,0:T(8,128)(2,1)S(1)} %get-tuple-element.26), channel_id=1, source_target_pairs={{0,1},{1,0},{2,3},{3,2},{4,5},{5,4},{6,7},{7,6},{8,9},{9,8},{10,11... | collective-permute-start | bytes 24584 | tf_op jit(solution)/shard_map/ppermute | solution.py:416
  28.7 42.4 %all-to-all-start = ((bf16[16,32,128]{2,1,0:T(8,128)(2,1)}), bf16[16,32,128]{2,1,0:T(8,128)(2,1)S(1)}, u32[]{:S(2)}, u32[]{:S(2)}) async-start(bf16[16,32,128]{2,1,0:T(8,128)(2,1)} %broadcast_in_dim.3), calls=%async_computation | async-start | bytes 262144 | tf_op jit(solution)/shard_map/all_to_all | solution.py:418
  41.6 18.8 %collective-permute-start.3 = (bf16[2,128,128]{2,1,0:T(8,128)(2,1)S(1)}, bf16[2,128,128]{2,1,0:T(8,128)(2,1)S(1)}, u32[]{:S(2)}, u32[]{:S(2)}) collective-permute-start(bf16[2,128,128]{2,1,0:T(8,128)(2,1)S(1)} %get-tuple-element.21), channel_id=1, source_target_pairs={{0,192},{32,224},{64,0},{96,32},{128,64},{160,96},{192,128},{224,1... | collective-permute-start | bytes 196616 | tf_op jit(solution)/shard_map/ppermute | solution.py:405
  44.7 15.7 %collective-permute-start.4 = (bf16[2,128,128]{2,1,0:T(8,128)(2,1)S(1)}, bf16[2,128,128]{2,1,0:T(8,128)(2,1)S(1)}, u32[]{:S(2)}, u32[]{:S(2)}) collective-permute-start(bf16[2,128,128]{2,1,0:T(8,128)(2,1)S(1)} %get-tuple-element.22), channel_id=1, source_target_pairs={{0,256},{32,288},{64,320},{96,352},{128,384},{160,416},{192,448},{... | collective-permute-start | bytes 196616 | tf_op jit(solution)/shard_map/ppermute | solution.py:405
  49.5 10.9 %collective-permute-start.5 = (bf16[2,128,128]{2,1,0:T(8,128)(2,1)S(1)}, bf16[2,128,128]{2,1,0:T(8,128)(2,1)S(1)}, u32[]{:S(2)}, u32[]{:S(2)}) collective-permute-start(bf16[2,128,128]{2,1,0:T(8,128)(2,1)S(1)} %get-tuple-element.23), channel_id=1, source_target_pairs={{0,320},{32,352},{64,384},{96,416},{128,448},{160,480},{192,256},{... | collective-permute-start | bytes 196616 | tf_op jit(solution)/shard_map/ppermute | solution.py:405
  51.5 8.9 %collective-permute-start.6 = (bf16[2,128,128]{2,1,0:T(8,128)(2,1)S(1)}, bf16[2,128,128]{2,1,0:T(8,128)(2,1)S(1)}, u32[]{:S(2)}, u32[]{:S(2)}) collective-permute-start(bf16[2,128,128]{2,1,0:T(8,128)(2,1)S(1)} %get-tuple-element.24), channel_id=1, source_target_pairs={{0,384},{32,416},{64,448},{96,480},{128,256},{160,288},{192,320},{... | collective-permute-start | bytes 196616 | tf_op jit(solution)/shard_map/ppermute | solution.py:405
  57.0 7.8 %collective-permute-start.7 = (bf16[2,128,128]{2,1,0:T(8,128)(2,1)S(1)}, bf16[2,128,128]{2,1,0:T(8,128)(2,1)S(1)}, u32[]{:S(2)}, u32[]{:S(2)}) collective-permute-start(bf16[2,128,128]{2,1,0:T(8,128)(2,1)S(1)} %get-tuple-element.25), channel_id=1, source_target_pairs={{0,448},{32,480},{64,256},{96,288},{128,320},{160,352},{192,384},{... | collective-permute-start | bytes 196616 | tf_op jit(solution)/shard_map/ppermute | solution.py:405
  65.6 37.1 %collective-permute-start.11 = (bf16[32,64,128]{2,1,0:T(8,128)(2,1)S(1)}, bf16[32,64,128]{2,1,0:T(8,128)(2,1)S(1)}, u32[]{:S(2)}, u32[]{:S(2)}) collective-permute-start(bf16[32,64,128]{2,1,0:T(8,128)(2,1)S(1)} %gather.1.right_ref), channel_id=1, source_target_pairs={{0,1},{1,2},{2,3},{3,4},{4,5},{5,6},{6,7},{7,8},{8,9},{9,10},{10,1... | collective-permute-start | bytes 1572872 | tf_op jit(solution)/shard_map/ppermute | solution.py:397
  68.0 38.1 %collective-permute-start.9 = (bf16[32,64,128]{2,1,0:T(8,128)(2,1)S(1)}, bf16[32,64,128]{2,1,0:T(8,128)(2,1)S(1)}, u32[]{:S(2)}, u32[]{:S(2)}) collective-permute-start(bf16[32,64,128]{2,1,0:T(8,128)(2,1)S(1)} %gather.1.right_ref), channel_id=1, source_target_pairs={{0,2},{1,3},{2,4},{3,5},{4,6},{5,7},{6,8},{7,9},{8,10},{9,11},{10,... | collective-permute-start | bytes 1572872 | tf_op jit(solution)/shard_map/ppermute | solution.py:397
  89.6 13.1 %collective-permute-start.12 = (bf16[16,16,128]{2,1,0:T(8,128)(2,1)S(1)}, bf16[16,16,128]{2,1,0:T(8,128)(2,1)S(1)}, u32[]{:S(2)}, u32[]{:S(2)}) collective-permute-start(bf16[16,16,128]{2,1,0:T(8,128)(2,1)S(1)} %all_to_all.10.note_ref), channel_id=1, source_target_pairs={{0,1},{1,2},{2,3},{3,4},{4,5},{5,6},{6,7},{7,8},{8,9},{9,10},{10,1... | collective-permute-start | bytes 196616 | tf_op jit(solution)/shard_map/ppermute | solution.py:397
  92.2 13.8 %collective-permute-start.10 = (bf16[16,16,128]{2,1,0:T(8,128)(2,1)S(1)}, bf16[16,16,128]{2,1,0:T(8,128)(2,1)S(1)}, u32[]{:S(2)}, u32[]{:S(2)}) collective-permute-start(bf16[16,16,128]{2,1,0:T(8,128)(2,1)S(1)} %all_to_all.10.note_ref), channel_id=1, source_target_pairs={{0,2},{1,3},{2,4},{3,5},{4,6},{5,7},{6,8},{7,9},{8,10},{9,11},{10,... | collective-permute-start | bytes 196616 | tf_op jit(solution)/shard_map/ppermute | solution.py:397

commit v4 on v2

v4 whole, which is shorter than its diff:
```python
import functools
import math

import jax
import jax.numpy as jnp
import ml_dtypes
import numpy as np
from jax import lax
from jax.experimental import pallas as pl
from jax.experimental.pallas import tpu as pltpu
from jax.sharding import PartitionSpec as P

L = 2048
HALF = 1024
BANDS = 16
SEG = 4
CH = 32
PAIRS = 32
SPAN = 9216
HALVES = 2
FEW = 16
ROWS = SEG * FEW
LANES = 128
BF16 = jnp.bfloat16
F32 = jnp.float32


def half_table():
    band, parity, pair = np.ogrid[:BANDS, :2, :PAIRS]
    which_bin = 64 * band + 2 * pair + parity + 1
    sample = np.arange(HALF)
    residue = (which_bin[..., None] * sample) % L
    phase_angle = residue.astype(np.float32) * np.float32(2.0 * math.pi / L)
    factor = np.float32(1.0 / math.sqrt(L))
    cosine = np.cos(phase_angle) * factor
    sine = -np.sin(phase_angle) * factor
    return np.concatenate([cosine, sine], axis=2).astype(ml_dtypes.bfloat16)


def lane_index(rows):
    return lax.broadcasted_iota(jnp.int32, (rows, LANES), 1)


def cut_windows(offset_ref, order_ref, traces_ref, wave_ref):
    lane = lane_index(CH)
    row = lax.broadcasted_iota(jnp.int32, (CH, CH), 0)
    picked = jnp.zeros((CH, CH), jnp.int32)
    for channel in range(CH):
        picked = jnp.where(row == channel, order_ref[0, channel], picked)
    chosen = (lax.broadcasted_iota(jnp.int32, (CH, CH), 1) == picked).astype(F32).astype(BF16)
    tiles = L // LANES
    for seg in range(SEG):
        start = seg * L + offset_ref[seg]
        base = jnp.minimum((start // LANES) * LANES, SPAN - (L + LANES))
        base = pl.multiple_of(base, LANES)
        rest = start - base
        turn = lax.rem(LANES - rest, LANES)
        rolled = []
        for tile in range(tiles + 1):
            part = traces_ref[:, pl.ds(pl.multiple_of(base + tile * LANES, LANES), LANES)]
            rolled.append(pltpu.roll(part.astype(F32), turn, 1))
        window = [
            jnp.where(lane < LANES - rest, rolled[tile], rolled[tile + 1]) for tile in range(tiles)
        ]
        rows = pl.ds(seg * CH, CH)
        for parity in range(2):
            sign = -1.0 if parity == 0 else 1.0
            folded = jnp.concatenate(
                [window[t] + sign * window[t + tiles // 2] for t in range(tiles // 2)], axis=1
            ).astype(BF16)
            wave_ref[parity, rows, :] = jnp.dot(
                chosen, folded, preferred_element_type=F32
            ).astype(BF16)


def spectra_kernel(
    offset_hbm, order_hbm, pilot_hbm, traces_hbm, table_hbm, block_ref, guide_ref,
    offset_ref, order_ref, pilot_ref, traces_ref, table_ref, wave_ref, power_ref, sems, table_sems,
):
    small = [
        pltpu.make_async_copy(source, target, sems.at[k])
        for k, (source, target) in enumerate(
            (
                (offset_hbm, offset_ref),
                (order_hbm, order_ref),
                (pilot_hbm, pilot_ref),
                (traces_hbm, traces_ref),
            )
        )
    ]
    for copy in small:
        copy.start()
    for part in range(4):
        pltpu.make_async_copy(
            table_hbm.at[pl.ds(4 * part, 4)], table_ref.at[pl.ds(4 * part, 4)], table_sems.at[part]
        ).start()
    power_ref[...] = jnp.zeros_like(power_ref)
    for copy in small:
        copy.wait()
    cut_windows(offset_ref, order_ref, traces_ref, wave_ref)

    lane = lane_index(PAIRS)
    channel = lax.rem(pilot_ref[0], CH)
    for quarter in range(4):
        pltpu.make_async_copy(
            table_hbm.at[pl.ds(4 * quarter, 4)],
            table_ref.at[pl.ds(4 * quarter, 4)],
            table_sems.at[quarter],
        ).wait()
        for local_band in range(4):
            band = quarter * 4 + local_band
            parts = {}
            for parity in range(2):
                product = lax.dot_general(
                    table_ref[band, parity],
                    wave_ref[parity],
                    (((1,), (1,)), ((), ())),
                    preferred_element_type=F32,
                )
                for side in range(2):
                    parts[side, parity] = product[side * PAIRS : (side + 1) * PAIRS]
                real = parts[0, parity].astype(BF16).astype(F32)
                imag = parts[1, parity].astype(BF16).astype(F32)
                place = 2 * band + parity
                power = pltpu.roll(
                    real * real + imag * imag, lax.rem(place - channel + LANES, LANES), 1
                )
                power_ref[...] = jnp.where(lane % 32 == place, power, power_ref[...])
            for seg in range(SEG):
                line = None
                for side in range(2):
                    for parity in range(2):
                        group = side * 2 + parity
                        part = parts[side, parity]
                        if group != seg:
                            part = pltpu.roll(part, (group - seg) * 32 % LANES, 1)
                        line = part if line is None else jnp.where(lane // 32 == group, part, line)
                line = line.astype(BF16)
                for half in range(HALVES):
                    block_ref[band, half, seg * FEW : (seg + 1) * FEW, :] = line[
                        half * FEW : (half + 1) * FEW
                    ]
    mine = pilot_ref[0] // CH == lax.axis_index("rgrp")
    guide_ref[...] = jnp.where(mine, jnp.sqrt(power_ref[...]), 0.0).astype(BF16)


def spectra_of(offsets, order, pilot, traces, table):
    vmem = pl.BlockSpec(memory_space=pltpu.VMEM)
    offsets, order, traces, table = (
        pltpu.with_memory_space_constraint(value, pltpu.HBM)
        for value in (offsets, order, traces, table)
    )
    return pl.pallas_call(
        spectra_kernel,
        in_specs=[pl.BlockSpec(memory_space=pl.ANY)] * 5,
        out_specs=[vmem, vmem],
        out_shape=[
            jax.ShapeDtypeStruct((BANDS, HALVES, SEG * FEW, LANES), BF16),
            jax.ShapeDtypeStruct((PAIRS, LANES), BF16),
        ],
        scratch_shapes=[
            pltpu.SMEM((SEG,), jnp.int32),
            pltpu.SMEM((1, CH), jnp.int32),
            pltpu.SMEM((1,), jnp.int32),
            pltpu.VMEM((CH, SPAN), BF16),
            pltpu.VMEM((BANDS, 2, 2 * PAIRS, HALF), BF16),
            pltpu.VMEM((2, SEG * CH, HALF), BF16),
            pltpu.VMEM((PAIRS, LANES), F32),
            pltpu.SemaphoreType.DMA((4,)),
            pltpu.SemaphoreType.DMA((4,)),
        ],
        compiler_params=pltpu.CompilerParams(vmem_limit_bytes=16 * 1024 * 1024),
        name="spectra",
    )(offsets, order, pilot, traces, table)


def whiten_kernel(guides_ref, own_ref, far_ref, white_ref, value_ref, guide_ref):
    guide = guides_ref[0].astype(F32)
    for line in range(1, 16):
        guide = guide + guides_ref[line].astype(F32)
    guide_ref[...] = guide
    even = (lane_index(PAIRS) // 32) % 2 == 0
    blocks = (own_ref, far_ref)
    totals = [[jnp.zeros((FEW, LANES), F32) for _ in range(SEG)] for _ in blocks]
    for band in range(BANDS):
        for seg in range(SEG):
            first = 32 * seg + 2 * band
            rows = slice(seg * FEW, (seg + 1) * FEW)
            weight = jnp.where(
                even, guide_ref[:, first : first + 1], guide_ref[:, first + 1 : first + 2]
            )
            for half in range(HALVES):
                part = weight[half * FEW : (half + 1) * FEW]
                for k, block_ref in enumerate(blocks):
                    value = block_ref[band, half, rows, :].astype(F32) * part
                    value_ref[band * HALVES + half, k, rows, :] = value
                    totals[k][seg] = totals[k][seg] + value * value
    for k in range(len(blocks)):
        for seg in range(SEG):
            total = jnp.sum(totals[k][seg], axis=0, keepdims=True)
            total = jnp.broadcast_to(total, (8, LANES))
            total = total + pltpu.roll(total, 64, 1)
            total = total + pltpu.roll(total, 32, 1)
            level = (total * (0.1 / (64.0 * BANDS)) + 1e-06)[:1]
            rows = slice(seg * FEW, (seg + 1) * FEW)
            for place in range(BANDS * HALVES):
                value = value_ref[place, k, rows, :]
                energy = value * value
                energy = energy + pltpu.roll(energy, 64, 1)
                white_ref[place, k, rows, :] = (value * lax.rsqrt(energy + level)).astype(BF16)


def whitened_of(guides, own, far):
    vmem = pl.BlockSpec(memory_space=pltpu.VMEM)
    shape = (BANDS * HALVES, 2, ROWS, LANES)
    return pl.pallas_call(
        whiten_kernel,
        in_specs=[vmem] * 3,
        out_specs=vmem,
        out_shape=jax.ShapeDtypeStruct(shape, BF16),
        scratch_shapes=[pltpu.VMEM(shape, F32), pltpu.VMEM((PAIRS, LANES), F32)],
        compiler_params=pltpu.CompilerParams(vmem_limit_bytes=32 * 1024 * 1024),
        name="whiten",
    )(guides, own, far)


def gather_kernel(parts_ref, block_ref, wide_ref):
    for place in range(BANDS * HALVES):
        for k in range(2):
            at = (place * 2 + k) * ROWS
            wide_ref[at : at + ROWS, :] = parts_ref[place, k].astype(F32)

    def bin_pair(pair, carry):
        for which in range(4):
            rows = [
                wide_ref[pl.ds(which * ROWS + seg * FEW + pair, BANDS, stride=4 * ROWS), :]
                for seg in range(SEG)
            ]
            block_ref[pair, which] = jnp.concatenate(rows, axis=0).astype(BF16)
        return carry

    lax.fori_loop(0, FEW, bin_pair, 0, unroll=2)


def gathered_of(parts):
    vmem = pl.BlockSpec(memory_space=pltpu.VMEM)
    return pl.pallas_call(
        gather_kernel,
        in_specs=[vmem],
        out_specs=vmem,
        out_shape=jax.ShapeDtypeStruct((FEW, 4, BANDS * SEG, LANES), BF16),
        scratch_shapes=[pltpu.VMEM((BANDS * HALVES * 2 * ROWS, LANES), F32)],
        compiler_params=pltpu.CompilerParams(vmem_limit_bytes=32 * 1024 * 1024),
        name="gather",
    )(parts)


def cross_kernel(mine, block_ref, out_ref, near_ref, far_ref):
    side = lax.axis_index("rgrp") % 2
    left_side = side if mine else 1 - side
    sign = jnp.where(lane_index(BANDS * SEG) < 64, 1.0, -1.0)

    def bin_pair(pair, carry):
        turned = jnp.transpose(block_ref[pair, 2 * left_side].astype(F32))
        left = jnp.concatenate([turned[:64], turned[64:]], axis=1).astype(BF16)
        for which, stack_ref in ((3 * (1 - left_side), near_ref), (2 * left_side + 1, far_ref)):
            right = block_ref[pair, which].astype(F32)
            mix = jnp.concatenate([right * sign, pltpu.roll(right, 64, 1)], axis=0).astype(BF16)
            product = jnp.dot(left, mix, preferred_element_type=F32)
            stack_ref[pl.ds(pl.multiple_of(pair * 2 * CH, 2 * CH), 2 * CH), :] = product
        return carry

    lax.fori_loop(0, FEW, bin_pair, 0, unroll=4)

    lane = lane_index(CH)
    even = lane % 2 == 0
    for first in range(0, CH, 4):
        pieces = {}
        for back, stack_ref in enumerate((near_ref, far_ref)):
            rows = [stack_ref[pl.ds(first + k, 2 * FEW, stride=CH), :] for k in range(4)]
            turned = jnp.transpose(jnp.concatenate(rows, axis=0)) * 0.125
            pieces[back] = jnp.where(even, turned[:32], turned[32:64])
            pieces[2 + back] = jnp.where(even, turned[64:96], turned[96:])
        for k in range(4):
            line = None
            for group in range(4):
                part = pieces[group]
                if group != k:
                    part = pltpu.roll(part, (group - k) * 32 % LANES, 1)
                line = part if line is None else jnp.where(lane // 32 == group, part, line)
            out_ref[first + k] = line.astype(BF16)


def cross_of(mine, blocks):
    vmem = pl.BlockSpec(memory_space=pltpu.VMEM)
    stack = pltpu.VMEM((2 * FEW * CH, LANES), F32)
    return pl.pallas_call(
        functools.partial(cross_kernel, mine),
        in_specs=[vmem],
        out_specs=vmem,
        out_shape=jax.ShapeDtypeStruct((CH, CH, LANES), BF16),
        scratch_shapes=[stack, stack],
        compiler_params=pltpu.CompilerParams(vmem_limit_bytes=32 * 1024 * 1024),
        cost_estimate=pl.CostEstimate(flops=2**28, bytes_accessed=2**23, transcendentals=0),
        name="cross_mine" if mine else "cross_other",
    )(blocks)


def merge_kernel(own_ref, other_ref, out_ref):
    first = lax.axis_index("rgrp") % 2 == 0
    even = (lane_index(CH) // 32) % 2 == 0

    def channel(i, carry):
        own = own_ref[i].astype(F32)
        other = other_ref[i].astype(F32)
        low = jnp.where(first, own, other)
        high = jnp.where(first, other, own)
        out_ref[0, i] = jnp.where(even, low, pltpu.roll(high, 32, 1)).astype(BF16)
        out_ref[1, i] = jnp.where(even, pltpu.roll(low, 96, 1), high).astype(BF16)
        return carry

    lax.fori_loop(0, CH, channel, 0, unroll=4)


def merged_of(own, other):
    vmem = pl.BlockSpec(memory_space=pltpu.VMEM)
    return pl.pallas_call(
        merge_kernel,
        in_specs=[vmem] * 2,
        out_specs=vmem,
        out_shape=jax.ShapeDtypeStruct((2, CH, CH, LANES), BF16),
        compiler_params=pltpu.CompilerParams(vmem_limit_bytes=32 * 1024 * 1024),
        name="merge",
    )(own, other)


def beside(value):
    return lax.ppermute(value, "rgrp", [(g, g ^ 1) for g in range(32)])


def local(table, traces, segment_offsets, channel_order, pilot_channel):
    own, guide = spectra_of(segment_offsets, channel_order, pilot_channel, traces, table)
    far = lax.ppermute(own, "rgrp", [(g, (g + 2) % 32) for g in range(32)])
    guide = guide + beside(guide)
    lines = [[2 * z + side for z in range(16)] for side in range(2)]
    guides = lax.all_to_all(
        jnp.broadcast_to(guide, (16, PAIRS, LANES)),
        "rgrp",
        split_axis=0,
        concat_axis=0,
        tiled=True,
        axis_index_groups=lines,
    )
    white = whitened_of(guides, own, far)
    planes = [[32 * f + 2 * z + side for f in range(BANDS) for side in range(2)] for z in range(16)]
    parts = lax.all_to_all(
        white, ("freq", "rgrp"), split_axis=0, concat_axis=0, tiled=True, axis_index_groups=planes
    )
    blocks = gathered_of(parts)
    other = beside(cross_of(False, blocks))
    return merged_of(cross_of(True, blocks), other)


def solution(mesh):
    table = half_table()
    specs = (P(), P("rgrp", "freq"), P("freq"), P("rgrp", None), P())
    inner = jax.shard_map(
        local, mesh=mesh, in_specs=specs, out_specs=P(None, "rgrp", None, "freq"), check_vma=False
    )

    def run(traces, segment_offsets, channel_order, pilot_channel):
        return inner(jnp.asarray(table), traces, segment_offsets, channel_order, pilot_channel)

    return run
```

time: 97.1 us -> 85.8 us (0.88)
  the two profiles are of different devices: /device:TPU:8 before, /device:TPU:1 now
where the time goes in v4:
time: 85.8 us; the launch traced here: 85.6 us
  blocking collectives  54.1 us (63%)
  Pallas kernels  16.1 us (19%)
  starting transfers between devices  9.49 us (11%)
  waiting for transfers between devices  5.15 us (6%)
    all_to_all x1, blocking collectives, local(): lax.all_to_all(white, ('freq', 'rgrp'), split_axis=0, concat_axis=0, tile...  28 us
    all_to_all x1, blocking collectives, local(): lax.all_to_all(jnp.broadcast_to(guide, (16, PAIRS, LANES)), 'rgrp', split...  26.1 us
    pallas_call x1, Pallas kernels, spectra_of(): pl.pallas_call(spectra_kernel, in_specs=[pl.BlockSpec(memory_space=pl.ANY...  6.25 us
    pallas_call x2, Pallas kernels, cross_of(): pl.pallas_call(functools.partial(cross_kernel, mine), in_specs=[vmem], ou...  5.49 us
    ppermute x2, waiting for transfers between devices, beside(): return lax.ppermute(value, 'rgrp', [(g, g ^ 1) for g in range(32)])  5.14 us
    ppermute x2, starting transfers between devices, beside(): return lax.ppermute(value, 'rgrp', [(g, g ^ 1) for g in range(32)])  5.13 us
    ppermute x1, starting transfers between devices, local(): far = lax.ppermute(own, 'rgrp', [(g, (g + 2) % 32) for g in range(32)])  4.37 us
  transfers between devices with their start and end apart: 3, of which 2 were waited for; matrix products, arithmetic and copies ran while one was open for 0% of the time, Pallas kernels for 3%

profile of v4, /device:TPU:1, one launch (start us, length us, event | category | flops | bytes accessed | tf_op | source)
XLA Modules:
  0.0 85.6 jit_solution(1518692299859356569)
XLA Ops:
  0.7 6.2 %spectra.1 = (bf16[16,2,64,128]{3,2,1,0:T(8,128)(2,1)S(1)}, bf16[32,128]{1,0:T(8,128)(2,1)S(1)}) custom-call(s32[4]{0:T(128)} %offset_hbm.1, s32[1,32]{1,0:T(1,128)} %order_hbm.1, s32[1]{0:T(128)S(6)} %copy.6.pilot_hbm, bf16[32,9216]{1,0:T(8,128)(2,1)} %traces_hbm.1, bf16[16,2,64,1024]{3,2,1,0:T(8,128)(2,1)} %constant.2.clone.table_hbm), custom_call_target="tpu_custom_call" | custom-call | tf_op jit(solution)/shard_map/spectra/pallas_call | solution.py:153
  6.9 4.4 %collective-permute-start.1 = (bf16[16,2,64,128]{3,2,1,0:T(8,128)(2,1)S(1)}, bf16[16,2,64,128]{3,2,1,0:T(8,128)(2,1)S(1)}, u32[]{:S(2)}, u32[]{:S(2)}) collective-permute-start(bf16[16,2,64,128]{3,2,1,0:T(8,128)(2,1)S(1)} %get-tuple-element.8.own_ref), channel_id=1, source_target_pairs={{0,2},{1,3},{2,4},{3,5},{4,6},{5,7},{6,8},{7,9},{8,10},{9,11},{10,... | collective-permute-start | bytes 1572872 | tf_op jit(solution)/shard_map/ppermute | solution.py:343
  11.3 3.2 %collective-permute-start = (bf16[32,128]{1,0:T(8,128)(2,1)S(1)}, bf16[32,128]{1,0:T(8,128)(2,1)S(1)}, u32[]{:S(2)}, u32[]{:S(2)}) collective-permute-start(bf16[32,128]{1,0:T(8,128)(2,1)S(1)} %get-tuple-element.7), channel_id=1, source_target_pairs={{0,1},{1,0},{2,3},{3,2},{4,5},{5,4},{6,7},{7,6},{8,9},{9,8},{10,11... | collective-permute-start | bytes 24584 | tf_op jit(solution)/shard_map/ppermute | solution.py:338
  14.5 1.2 %collective-permute-done = bf16[32,128]{1,0:T(8,128)(2,1)S(1)} collective-permute-done((bf16[32,128]{1,0:T(8,128)(2,1)S(1)}, bf16[32,128]{1,0:T(8,128)(2,1)S(1)}, u32[]{:S(2)}, u32[]{:S(2)}) %collective-permute-start) | collective-permute-done | bytes 8224 | tf_op jit(solution)/shard_map/ppermute | solution.py:338
  15.7 26.1 %all_to_all.10.guides_ref = bf16[16,32,128]{2,1,0:T(8,128)(2,1)S(1)} all-to-all(bf16[16,32,128]{2,1,0:T(8,128)(2,1)S(1)} %broadcast_in_dim.3), channel_id=1, replica_groups={{0,2,4,6,8,10,12,14,16,18,20,22,24,26,28,30},{1,3,5,7,9,11,13,15,17,19,..., dimensions={0} | all-to-all | bytes 262144 | tf_op jit(solution)/shard_map/all_to_all | solution.py:346
  41.8 0.0 collective-permute-done.1.far_ref
  41.8 1.5 %whiten.1 = bf16[32,2,64,128]{3,2,1,0:T(8,128)(2,1)S(1)} custom-call(bf16[16,32,128]{2,1,0:T(8,128)(2,1)S(1)} %all_to_all.10.guides_ref, bf16[16,2,64,128]{3,2,1,0:T(8,128)(2,1)S(1)} %get-tuple-element.8.own_ref, bf16[16,2,64,128]{3,2,1,0:T(8,128)(2,1)S(1)} %collective-permute-done.1.far_ref), custom_call_target="tpu_custom_call" | custom-call | tf_op jit(solution)/shard_map/whiten/pallas_call | solution.py:216
  43.4 28.0 %all_to_all.11.parts_ref = bf16[32,2,64,128]{3,2,1,0:T(8,128)(2,1)S(1)} all-to-all(bf16[32,2,64,128]{3,2,1,0:T(8,128)(2,1)S(1)} %whiten.1), channel_id=1, replica_groups={{0,1,32,33,64,65,96,97,128,129,160,161,192,193,224,225,256,257,288,289,..., dimensions={0} | all-to-all | bytes 2097152 | tf_op jit(solution)/shard_map/all_to_all | solution.py:356
  71.3 1.3 %gather.1.block_ref = bf16[16,4,64,128]{3,2,1,0:T(8,128)(2,1)S(1)} custom-call(bf16[32,2,64,128]{3,2,1,0:T(8,128)(2,1)S(1)} %all_to_all.11.parts_ref), custom_call_target="tpu_custom_call" | custom-call | tf_op jit(solution)/shard_map/gather/pallas_call | solution.py:247
  72.7 2.7 %cross_other.1 = bf16[32,32,128]{2,1,0:T(8,128)(2,1)S(1)} custom-call(bf16[16,4,64,128]{3,2,1,0:T(8,128)(2,1)S(1)} %gather.1.block_ref), custom_call_target="tpu_custom_call" | custom-call | flops 268435456 | bytes 8388608 | tf_op jit(solution)/shard_map/cross_other/pallas_call | solution.py:297
  75.4 1.9 %collective-permute-start.2 = (bf16[32,32,128]{2,1,0:T(8,128)(2,1)S(1)}, bf16[32,32,128]{2,1,0:T(8,128)(2,1)S(1)}, u32[]{:S(2)}, u32[]{:S(2)}) collective-permute-start(bf16[32,32,128]{2,1,0:T(8,128)(2,1)S(1)} %cross_other.1), channel_id=1, source_target_pairs={{0,1},{1,0},{2,3},{3,2},{4,5},{5,4},{6,7},{7,6},{8,9},{9,8},{10,11... | collective-permute-start | bytes 786440 | tf_op jit(solution)/shard_map/ppermute | solution.py:338
  77.4 2.7 %cross_mine.1.own_ref = bf16[32,32,128]{2,1,0:T(8,128)(2,1)S(1)} custom-call(bf16[16,4,64,128]{3,2,1,0:T(8,128)(2,1)S(1)} %gather.1.block_ref), custom_call_target="tpu_custom_call" | custom-call | flops 268435456 | bytes 8388608 | tf_op jit(solution)/shard_map/cross_mine/pallas_call | solution.py:297
  80.1 4.0 %collective-permute-done.2.other_ref = bf16[32,32,128]{2,1,0:T(8,128)(2,1)S(1)} collective-permute-done((bf16[32,32,128]{2,1,0:T(8,128)(2,1)S(1)}, bf16[32,32,128]{2,1,0:T(8,128)(2,1)S(1)}, u32[]{:S(2)}, u32[]{:S(2)}) %collective-permute-start.2) | collective-permute-done | bytes 262176 | tf_op jit(solution)/shard_map/ppermute | solution.py:338
  84.1 1.5 %merge.1 = bf16[2,32,32,128]{3,2,1,0:T(8,128)(2,1)} custom-call(bf16[32,32,128]{2,1,0:T(8,128)(2,1)S(1)} %cross_mine.1.own_ref, bf16[32,32,128]{2,1,0:T(8,128)(2,1)S(1)} %collective-permute-done.2.other_ref), custom_call_target="tpu_custom_call" | custom-call | tf_op jit(solution)/shard_map/merge/pallas_call | solution.py:327
  (2 shorter events, 0.0 us)
Async XLA Ops:
  6.9 34.9 %collective-permute-start.1 = (bf16[16,2,64,128]{3,2,1,0:T(8,128)(2,1)S(1)}, bf16[16,2,64,128]{3,2,1,0:T(8,128)(2,1)S(1)}, u32[]{:S(2)}, u32[]{:S(2)}) collective-permute-start(bf16[16,2,64,128]{3,2,1,0:T(8,128)(2,1)S(1)} %get-tuple-element.8.own_ref), channel_id=1, source_target_pairs={{0,2},{1,3},{2,4},{3,5},{4,6},{5,7},{6,8},{7,9},{8,10},{9,11},{10,... | collective-permute-start | bytes 1572872 | tf_op jit(solution)/shard_map/ppermute | solution.py:343
  11.3 4.4 %collective-permute-start = (bf16[32,128]{1,0:T(8,128)(2,1)S(1)}, bf16[32,128]{1,0:T(8,128)(2,1)S(1)}, u32[]{:S(2)}, u32[]{:S(2)}) collective-permute-start(bf16[32,128]{1,0:T(8,128)(2,1)S(1)} %get-tuple-element.7), channel_id=1, source_target_pairs={{0,1},{1,0},{2,3},{3,2},{4,5},{5,4},{6,7},{7,6},{8,9},{9,8},{10,11... | collective-permute-start | bytes 24584 | tf_op jit(solution)/shard_map/ppermute | solution.py:338
  75.4 8.6 %collective-permute-start.2 = (bf16[32,32,128]{2,1,0:T(8,128)(2,1)S(1)}, bf16[32,32,128]{2,1,0:T(8,128)(2,1)S(1)}, u32[]{:S(2)}, u32[]{:S(2)}) collective-permute-start(bf16[32,32,128]{2,1,0:T(8,128)(2,1)S(1)} %cross_other.1), channel_id=1, source_target_pairs={{0,1},{1,0},{2,3},{3,2},{4,5},{5,4},{6,7},{7,6},{8,9},{9,8},{10,11... | collective-permute-start | bytes 786440 | tf_op jit(solution)/shard_map/ppermute | solution.py:338

commit v5 on v4

--- a/solution.py
+++ b/solution.py
@@ -11,7 +11,8 @@
 from jax.sharding import PartitionSpec as P
 
 L = 2048
-HALF = 1024
+QUARTER = 512
+PARTS = 1
 BANDS = 16
 SEG = 4
 CH = 32
@@ -20,28 +21,28 @@
 HALVES = 2
 FEW = 16
 ROWS = SEG * FEW
+PITCH = 4 * ROWS + 8
 LANES = 128
 BF16 = jnp.bfloat16
 F32 = jnp.float32
 
 
-def half_table():
-    band, parity, pair = np.ogrid[:BANDS, :2, :PAIRS]
-    which_bin = 64 * band + 2 * pair + parity + 1
-    sample = np.arange(HALF)
+def quarter_table():
+    part, parity, band, pair = np.ogrid[:PARTS, :2, : BANDS // PARTS, :PAIRS]
+    which_bin = 64 * (part * (BANDS // PARTS) + band) + 2 * pair + parity + 1
+    sample = np.arange(QUARTER)
     residue = (which_bin[..., None] * sample) % L
     phase_angle = residue.astype(np.float32) * np.float32(2.0 * math.pi / L)
     factor = np.float32(1.0 / math.sqrt(L))
-    cosine = np.cos(phase_angle) * factor
-    sine = -np.sin(phase_angle) * factor
-    return np.concatenate([cosine, sine], axis=2).astype(ml_dtypes.bfloat16)
+    both = np.stack([np.cos(phase_angle) * factor, np.sin(phase_angle) * factor], axis=3)
+    return both.reshape(PARTS, 2, -1, QUARTER).astype(ml_dtypes.bfloat16)
 
 
 def lane_index(rows):
     return lax.broadcasted_iota(jnp.int32, (rows, LANES), 1)
 
 
-def cut_windows(offset_ref, order_ref, traces_ref, wave_ref):
+def cut_windows(offset_ref, order_ref, traces_ref, wide_ref, wave_ref):
     lane = lane_index(CH)
     row = lax.broadcasted_iota(jnp.int32, (CH, CH), 0)
     picked = jnp.zeros((CH, CH), jnp.int32)
@@ -62,63 +63,72 @@
         window = [
             jnp.where(lane < LANES - rest, rolled[tile], rolled[tile + 1]) for tile in range(tiles)
         ]
-        rows = pl.ds(seg * CH, CH)
-        for parity in range(2):
-            sign = -1.0 if parity == 0 else 1.0
-            folded = jnp.concatenate(
-                [window[t] + sign * window[t + tiles // 2] for t in range(tiles // 2)], axis=1
-            ).astype(BF16)
-            wave_ref[parity, rows, :] = jnp.dot(
-                chosen, folded, preferred_element_type=F32
-            ).astype(BF16)
+        quarter = tiles // 4
+        first, second, third, fourth = (
+            jnp.concatenate(window[k * quarter : (k + 1) * quarter], axis=1) for k in range(4)
+        )
+        even, odd = first + third, second + fourth
+        mixes = (first - third, second - fourth, even - odd, even + odd)
+        for k, mix in enumerate(mixes):
+            mix = jnp.dot(chosen, mix.astype(BF16), preferred_element_type=F32)
+            at = (k % 2) * LANES + seg * CH
+            wide_ref[k // 2, at : at + CH, :] = mix
+    for parity in range(2):
+        wave_ref[parity] = jnp.transpose(wide_ref[parity]).astype(BF16)
 
 
 def spectra_kernel(
     offset_hbm, order_hbm, pilot_hbm, traces_hbm, table_hbm, block_ref, guide_ref,
-    offset_ref, order_ref, pilot_ref, traces_ref, table_ref, wave_ref, power_ref, sems, table_sems,
+    offset_ref, order_ref, pilot_ref, traces_ref, table_ref, wide_ref, wave_ref,
+    power_ref, sems, table_sems,
 ):
     small = [
         pltpu.make_async_copy(source, target, sems.at[k])
         for k, (source, target) in enumerate(
             (
+                (traces_hbm, traces_ref),
                 (offset_hbm, offset_ref),
                 (order_hbm, order_ref),
                 (pilot_hbm, pilot_ref),
-                (traces_hbm, traces_ref),
             )
         )
     ]
     for copy in small:
         copy.start()
-    for part in range(4):
-        pltpu.make_async_copy(
-            table_hbm.at[pl.ds(4 * part, 4)], table_ref.at[pl.ds(4 * part, 4)], table_sems.at[part]
-        ).start()
+    table = [
+        pltpu.make_async_copy(table_hbm.at[part], table_ref.at[part], table_sems.at[part])
+        for part in range(PARTS)
+    ]
+    for copy in table:
+        copy.start()
     power_ref[...] = jnp.zeros_like(power_ref)
     for copy in small:
         copy.wait()
-    cut_windows(offset_ref, order_ref, traces_ref, wave_ref)
+    cut_windows(offset_ref, order_ref, traces_ref, wide_ref, wave_ref)
 
     lane = lane_index(PAIRS)
     channel = lax.rem(pilot_ref[0], CH)
-    for quarter in range(4):
-        pltpu.make_async_copy(
-            table_hbm.at[pl.ds(4 * quarter, 4)],
-            table_ref.at[pl.ds(4 * quarter, 4)],
-            table_sems.at[quarter],
-        ).wait()
-        for local_band in range(4):
-            band = quarter * 4 + local_band
+    odd_pair = lax.broadcasted_iota(jnp.int32, (PAIRS, LANES), 0) % 2 == 1
+    flip = jnp.where(odd_pair, -1.0, 1.0)
+    for slab in range(PARTS):
+        table[slab].wait()
+        products = [
+            jnp.dot(table_ref[slab, parity], wave_ref[parity], preferred_element_type=F32)
+            for parity in range(2)
+        ]
+        for local_band in range(BANDS // PARTS):
+            band = slab * (BANDS // PARTS) + local_band
+            at = 2 * PAIRS * local_band
             parts = {}
+            cosine = products[0][at : at + PAIRS]
+            sine = products[0][at + PAIRS : at + 2 * PAIRS]
+            parts[0, 0] = cosine[:, :LANES] - flip * sine[:, LANES:]
+            parts[1, 0] = -sine[:, :LANES] - flip * cosine[:, LANES:]
+            cosine = products[1][at : at + PAIRS]
+            sine = products[1][at + PAIRS : at + 2 * PAIRS]
+            parts[0, 1] = jnp.where(odd_pair, cosine[:, LANES:], cosine[:, :LANES])
+            parts[1, 1] = -jnp.where(odd_pair, sine[:, LANES:], sine[:, :LANES])
             for parity in range(2):
-                product = lax.dot_general(
-                    table_ref[band, parity],
-                    wave_ref[parity],
-                    (((1,), (1,)), ((), ())),
-                    preferred_element_type=F32,
-                )
-                for side in range(2):
-                    parts[side, parity] = product[side * PAIRS : (side + 1) * PAIRS]
                 real = parts[0, parity].astype(BF16).astype(F32)
                 imag = parts[1, parity].astype(BF16).astype(F32)
                 place = 2 * band + parity
@@ -163,11 +173,12 @@
             pltpu.SMEM((1, CH), jnp.int32),
             pltpu.SMEM((1,), jnp.int32),
             pltpu.VMEM((CH, SPAN), BF16),
-            pltpu.VMEM((BANDS, 2, 2 * PAIRS, HALF), BF16),
-            pltpu.VMEM((2, SEG * CH, HALF), BF16),
+            pltpu.VMEM((PARTS, 2, 2 * PAIRS * BANDS // PARTS, QUARTER), BF16),
+            pltpu.VMEM((2, 2 * LANES, QUARTER), F32),
+            pltpu.VMEM((2, QUARTER, 2 * LANES), BF16),
             pltpu.VMEM((PAIRS, LANES), F32),
             pltpu.SemaphoreType.DMA((4,)),
-            pltpu.SemaphoreType.DMA((4,)),
+            pltpu.SemaphoreType.DMA((PARTS,)),
         ],
         compiler_params=pltpu.CompilerParams(vmem_limit_bytes=16 * 1024 * 1024),
         name="spectra",
@@ -224,53 +235,31 @@
     )(guides, own, far)
 
 
-def gather_kernel(parts_ref, block_ref, wide_ref):
-    for place in range(BANDS * HALVES):
-        for k in range(2):
-            at = (place * 2 + k) * ROWS
-            wide_ref[at : at + ROWS, :] = parts_ref[place, k].astype(F32)
-
-    def bin_pair(pair, carry):
+def gather_rows(parts_ref, block_ref, wide_ref):
+    for window in range(BANDS):
+        for which in range(4):
+            at = window * PITCH + which * ROWS
+            part = parts_ref[window * HALVES + which // 2, which % 2]
+            wide_ref[at : at + ROWS, :] = part.astype(F32)
+    for pair in range(FEW):
         for which in range(4):
             rows = [
-                wide_ref[pl.ds(which * ROWS + seg * FEW + pair, BANDS, stride=4 * ROWS), :]
+                wide_ref[pl.ds(which * ROWS + seg * FEW + pair, BANDS, stride=PITCH), :]
                 for seg in range(SEG)
             ]
             block_ref[pair, which] = jnp.concatenate(rows, axis=0).astype(BF16)
-        return carry
-
-    lax.fori_loop(0, FEW, bin_pair, 0, unroll=2)
-
-
-def gathered_of(parts):
-    vmem = pl.BlockSpec(memory_space=pltpu.VMEM)
-    return pl.pallas_call(
-        gather_kernel,
-        in_specs=[vmem],
-        out_specs=vmem,
-        out_shape=jax.ShapeDtypeStruct((FEW, 4, BANDS * SEG, LANES), BF16),
-        scratch_shapes=[pltpu.VMEM((BANDS * HALVES * 2 * ROWS, LANES), F32)],
-        compiler_params=pltpu.CompilerParams(vmem_limit_bytes=32 * 1024 * 1024),
-        name="gather",
-    )(parts)
-
-
-def cross_kernel(mine, block_ref, out_ref, near_ref, far_ref):
-    side = lax.axis_index("rgrp") % 2
-    left_side = side if mine else 1 - side
+
+
+def cross_rows(left_side, block_ref, out_ref, near_ref, far_ref):
     sign = jnp.where(lane_index(BANDS * SEG) < 64, 1.0, -1.0)
-
-    def bin_pair(pair, carry):
+    for pair in range(FEW):
         turned = jnp.transpose(block_ref[pair, 2 * left_side].astype(F32))
         left = jnp.concatenate([turned[:64], turned[64:]], axis=1).astype(BF16)
         for which, stack_ref in ((3 * (1 - left_side), near_ref), (2 * left_side + 1, far_ref)):
             right = block_ref[pair, which].astype(F32)
             mix = jnp.concatenate([right * sign, pltpu.roll(right, 64, 1)], axis=0).astype(BF16)
             product = jnp.dot(left, mix, preferred_element_type=F32)
-            stack_ref[pl.ds(pl.multiple_of(pair * 2 * CH, 2 * CH), 2 * CH), :] = product
-        return carry
-
-    lax.fori_loop(0, FEW, bin_pair, 0, unroll=4)
+            stack_ref[pair * 2 * CH : (pair + 1) * 2 * CH, :] = product
 
     lane = lane_index(CH)
     even = lane % 2 == 0
@@ -291,18 +280,43 @@
             out_ref[first + k] = line.astype(BF16)
 
 
-def cross_of(mine, blocks):
-    vmem = pl.BlockSpec(memory_space=pltpu.VMEM)
-    stack = pltpu.VMEM((2 * FEW * CH, LANES), F32)
-    return pl.pallas_call(
-        functools.partial(cross_kernel, mine),
+def other_kernel(parts_ref, out_ref, block_ref, wide_ref, near_ref, far_ref):
+    gather_rows(parts_ref, block_ref, wide_ref)
+    cross_rows(1 - lax.axis_index("rgrp") % 2, block_ref, out_ref, near_ref, far_ref)
+
+
+def mine_kernel(block_ref, out_ref, near_ref, far_ref):
+    cross_rows(lax.axis_index("rgrp") % 2, block_ref, out_ref, near_ref, far_ref)
+
+
+STACK = pltpu.VMEM((2 * FEW * CH, LANES), F32)
+CROSS = jax.ShapeDtypeStruct((CH, CH, LANES), BF16)
+
+
+def other_of(parts):
+    vmem = pl.BlockSpec(memory_space=pltpu.VMEM)
+    return pl.pallas_call(
+        other_kernel,
+        in_specs=[vmem],
+        out_specs=[vmem, vmem],
+        out_shape=[CROSS, jax.ShapeDtypeStruct((FEW, 4, BANDS * SEG, LANES), BF16)],
+        scratch_shapes=[pltpu.VMEM((BANDS * PITCH, LANES), F32), STACK, STACK],
+        compiler_params=pltpu.CompilerParams(vmem_limit_bytes=32 * 1024 * 1024),
+        name="cross_other",
+    )(parts)
+
+
+def mine_of(blocks):
+    vmem = pl.BlockSpec(memory_space=pltpu.VMEM)
+    return pl.pallas_call(
+        mine_kernel,
         in_specs=[vmem],
         out_specs=vmem,
-        out_shape=jax.ShapeDtypeStruct((CH, CH, LANES), BF16),
-        scratch_shapes=[stack, stack],
+        out_shape=CROSS,
+        scratch_shapes=[STACK, STACK],
         compiler_params=pltpu.CompilerParams(vmem_limit_bytes=32 * 1024 * 1024),
         cost_estimate=pl.CostEstimate(flops=2**28, bytes_accessed=2**23, transcendentals=0),
-        name="cross_mine" if mine else "cross_other",
+        name="cross_mine",
     )(blocks)
 
 
@@ -319,7 +333,7 @@
         out_ref[1, i] = jnp.where(even, pltpu.roll(low, 96, 1), high).astype(BF16)
         return carry
 
-    lax.fori_loop(0, CH, channel, 0, unroll=4)
+    lax.fori_loop(0, CH, channel, 0, unroll=CH)
 
 
 def merged_of(own, other):
@@ -356,13 +370,13 @@
     parts = lax.all_to_all(
         white, ("freq", "rgrp"), split_axis=0, concat_axis=0, tiled=True, axis_index_groups=planes
     )
-    blocks = gathered_of(parts)
-    other = beside(cross_of(False, blocks))
-    return merged_of(cross_of(True, blocks), other)
+    other, blocks = other_of(parts)
+    other = beside(other)
+    return merged_of(mine_of(blocks), other)
 
 
 def solution(mesh):
-    table = half_table()
+    table = quarter_table()
     specs = (P(), P("rgrp", "freq"), P("freq"), P("rgrp", None), P())
     inner = jax.shard_map(
         local, mesh=mesh, in_specs=specs, out_specs=P(None, "rgrp", None, "freq"), check_vma=False

time: 85.8 us -> 79.9 us (0.931)
  Pallas kernels: 16.1 us -> 8.89 us
  waiting for transfers between devices: 5.15 us -> 6.37 us
    pallas_call x3 -> x2, Pallas kernels: 6.82 us -> 3.43 us  [the longest x1 1.9 us: other_of(): pl.pallas_call(other_kernel, in_specs=[vmem], out_specs=[vmem, vmem], out...]
    pallas_call x1, Pallas kernels: 6.25 us -> 2.9 us  [spectra_of(): pl.pallas_call(spectra_kernel, in_specs=[pl.BlockSpec(memory_space=pl.ANY...]
    ppermute x2, waiting for transfers between devices: 5.14 us -> 6.37 us  [beside(): return lax.ppermute(value, 'rgrp', [(g, g ^ 1) for g in range(32)])]
  transfers between devices with their start and end apart: 3 -> 3, of which waited for: 2 -> 2; matrix products, arithmetic and copies ran while one was open for 0% -> 0% of each run, Pallas kernels for 3% -> 2%
where the time goes in v5:
time: 79.9 us; the launch traced here: 79.6 us
  blocking collectives  54.1 us (68%)
  starting transfers between devices  9.5 us (12%)
  Pallas kernels  8.89 us (11%)
  waiting for transfers between devices  6.37 us (8%)
    all_to_all x1, blocking collectives, local(): lax.all_to_all(white, ('freq', 'rgrp'), split_axis=0, concat_axis=0, tile...  28 us
    all_to_all x1, blocking collectives, local(): lax.all_to_all(jnp.broadcast_to(guide, (16, PAIRS, LANES)), 'rgrp', split...  26.1 us
    ppermute x2, waiting for transfers between devices, beside(): return lax.ppermute(value, 'rgrp', [(g, g ^ 1) for g in range(32)])  6.37 us
    ppermute x2, starting transfers between devices, beside(): return lax.ppermute(value, 'rgrp', [(g, g ^ 1) for g in range(32)])  5.12 us
    ppermute x1, starting transfers between devices, local(): far = lax.ppermute(own, 'rgrp', [(g, (g + 2) % 32) for g in range(32)])  4.38 us
    pallas_call x1, Pallas kernels, spectra_of(): pl.pallas_call(spectra_kernel, in_specs=[pl.BlockSpec(memory_space=pl.ANY...  2.9 us
    pallas_call x1, Pallas kernels, other_of(): pl.pallas_call(other_kernel, in_specs=[vmem], out_specs=[vmem, vmem], out...  1.9 us
  transfers between devices with their start and end apart: 3, of which 2 were waited for; matrix products, arithmetic and copies ran while one was open for 0% of the time, Pallas kernels for 2%

profile of v5, /device:TPU:1, one launch (start us, length us, event | category | flops | bytes accessed | tf_op | source)
XLA Modules:
  0.0 79.6 jit_solution(4953535236000154638)
XLA Ops:
  0.7 2.9 %spectra.1 = (bf16[16,2,64,128]{3,2,1,0:T(8,128)(2,1)S(1)}, bf16[32,128]{1,0:T(8,128)(2,1)S(1)}) custom-call(s32[4]{0:T(128)} %offset_hbm.1, s32[1,32]{1,0:T(1,128)} %order_hbm.1, s32[1]{0:T(128)S(6)} %copy.6.pilot_hbm, bf16[32,9216]{1,0:T(8,128)(2,1)} %traces_hbm.1, bf16[1,2,1024,512]{3,2,1,0:T(8,128)(2,1)} %constant.2.clone.table_hbm), custom_call_target="tpu_custom_call" | custom-call | tf_op jit(solution)/shard_map/spectra/pallas_call | solution.py:163
  3.6 4.4 %collective-permute-start.1 = (bf16[16,2,64,128]{3,2,1,0:T(8,128)(2,1)S(1)}, bf16[16,2,64,128]{3,2,1,0:T(8,128)(2,1)S(1)}, u32[]{:S(2)}, u32[]{:S(2)}) collective-permute-start(bf16[16,2,64,128]{3,2,1,0:T(8,128)(2,1)S(1)} %get-tuple-element.10.own_ref), channel_id=1, source_target_pairs={{0,2},{1,3},{2,4},{3,5},{4,6},{5,7},{6,8},{7,9},{8,10},{9,11},{10,... | collective-permute-start | bytes 1572872 | tf_op jit(solution)/shard_map/ppermute | solution.py:357
  7.9 3.2 %collective-permute-start = (bf16[32,128]{1,0:T(8,128)(2,1)S(1)}, bf16[32,128]{1,0:T(8,128)(2,1)S(1)}, u32[]{:S(2)}, u32[]{:S(2)}) collective-permute-start(bf16[32,128]{1,0:T(8,128)(2,1)S(1)} %get-tuple-element.9), channel_id=1, source_target_pairs={{0,1},{1,0},{2,3},{3,2},{4,5},{5,4},{6,7},{7,6},{8,9},{9,8},{10,11... | collective-permute-start | bytes 24584 | tf_op jit(solution)/shard_map/ppermute | solution.py:352
  11.2 1.2 %collective-permute-done = bf16[32,128]{1,0:T(8,128)(2,1)S(1)} collective-permute-done((bf16[32,128]{1,0:T(8,128)(2,1)S(1)}, bf16[32,128]{1,0:T(8,128)(2,1)S(1)}, u32[]{:S(2)}, u32[]{:S(2)}) %collective-permute-start) | collective-permute-done | bytes 8224 | tf_op jit(solution)/shard_map/ppermute | solution.py:352
  12.4 26.1 %all_to_all.10.guides_ref = bf16[16,32,128]{2,1,0:T(8,128)(2,1)S(1)} all-to-all(bf16[16,32,128]{2,1,0:T(8,128)(2,1)S(1)} %broadcast_in_dim.3), channel_id=1, replica_groups={{0,2,4,6,8,10,12,14,16,18,20,22,24,26,28,30},{1,3,5,7,9,11,13,15,17,19,..., dimensions={0} | all-to-all | bytes 262144 | tf_op jit(solution)/shard_map/all_to_all | solution.py:360
  38.5 0.0 collective-permute-done.1.far_ref
  38.5 1.5 %whiten.1 = bf16[32,2,64,128]{3,2,1,0:T(8,128)(2,1)S(1)} custom-call(bf16[16,32,128]{2,1,0:T(8,128)(2,1)S(1)} %all_to_all.10.guides_ref, bf16[16,2,64,128]{3,2,1,0:T(8,128)(2,1)S(1)} %get-tuple-element.10.own_ref, bf16[16,2,64,128]{3,2,1,0:T(8,128)(2,1)S(1)} %collective-permute-done.1.far_ref), custom_call_target="tpu_custom_call" | custom-call | tf_op jit(solution)/shard_map/whiten/pallas_call | solution.py:227
  40.0 28.0 %all_to_all.11.parts_ref = bf16[32,2,64,128]{3,2,1,0:T(8,128)(2,1)S(1)} all-to-all(bf16[32,2,64,128]{3,2,1,0:T(8,128)(2,1)S(1)} %whiten.1), channel_id=1, replica_groups={{0,1,32,33,64,65,96,97,128,129,160,161,192,193,224,225,256,257,288,289,..., dimensions={0} | all-to-all | bytes 2097152 | tf_op jit(solution)/shard_map/all_to_all | solution.py:370
  68.1 1.9 %cross_other.1 = (bf16[32,32,128]{2,1,0:T(8,128)(2,1)S(1)}, bf16[16,4,64,128]{3,2,1,0:T(8,128)(2,1)S(1)}) custom-call(bf16[32,2,64,128]{3,2,1,0:T(8,128)(2,1)S(1)} %all_to_all.11.parts_ref), custom_call_target="tpu_custom_call" | custom-call | tf_op jit(solution)/shard_map/cross_other/pallas_call | solution.py:298
  70.0 1.9 %collective-permute-start.2 = (bf16[32,32,128]{2,1,0:T(8,128)(2,1)S(1)}, bf16[32,32,128]{2,1,0:T(8,128)(2,1)S(1)}, u32[]{:S(2)}, u32[]{:S(2)}) collective-permute-start(bf16[32,32,128]{2,1,0:T(8,128)(2,1)S(1)} %get-tuple-element.12), channel_id=1, source_target_pairs={{0,1},{1,0},{2,3},{3,2},{4,5},{5,4},{6,7},{7,6},{8,9},{9,8},{10,11... | collective-permute-start | bytes 786440 | tf_op jit(solution)/shard_map/ppermute | solution.py:352
  71.9 1.5 %cross_mine.1.own_ref = bf16[32,32,128]{2,1,0:T(8,128)(2,1)S(1)} custom-call(bf16[16,4,64,128]{3,2,1,0:T(8,128)(2,1)S(1)} %get-tuple-element.11.block_ref), custom_call_target="tpu_custom_call" | custom-call | flops 268435456 | bytes 8388608 | tf_op jit(solution)/shard_map/cross_mine/pallas_call | solution.py:311
  73.4 5.2 %collective-permute-done.2.other_ref = bf16[32,32,128]{2,1,0:T(8,128)(2,1)S(1)} collective-permute-done((bf16[32,32,128]{2,1,0:T(8,128)(2,1)S(1)}, bf16[32,32,128]{2,1,0:T(8,128)(2,1)S(1)}, u32[]{:S(2)}, u32[]{:S(2)}) %collective-permute-start.2) | collective-permute-done | bytes 262176 | tf_op jit(solution)/shard_map/ppermute | solution.py:352
  78.6 1.0 %merge.1 = bf16[2,32,32,128]{3,2,1,0:T(8,128)(2,1)} custom-call(bf16[32,32,128]{2,1,0:T(8,128)(2,1)S(1)} %cross_mine.1.own_ref, bf16[32,32,128]{2,1,0:T(8,128)(2,1)S(1)} %collective-permute-done.2.other_ref), custom_call_target="tpu_custom_call" | custom-call | tf_op jit(solution)/shard_map/merge/pallas_call | solution.py:341
  (2 shorter events, 0.0 us)
Async XLA Ops:
  3.6 34.9 %collective-permute-start.1 = (bf16[16,2,64,128]{3,2,1,0:T(8,128)(2,1)S(1)}, bf16[16,2,64,128]{3,2,1,0:T(8,128)(2,1)S(1)}, u32[]{:S(2)}, u32[]{:S(2)}) collective-permute-start(bf16[16,2,64,128]{3,2,1,0:T(8,128)(2,1)S(1)} %get-tuple-element.10.own_ref), channel_id=1, source_target_pairs={{0,2},{1,3},{2,4},{3,5},{4,6},{5,7},{6,8},{7,9},{8,10},{9,11},{10,... | collective-permute-start | bytes 1572872 | tf_op jit(solution)/shard_map/ppermute | solution.py:357
  7.9 4.4 %collective-permute-start = (bf16[32,128]{1,0:T(8,128)(2,1)S(1)}, bf16[32,128]{1,0:T(8,128)(2,1)S(1)}, u32[]{:S(2)}, u32[]{:S(2)}) collective-permute-start(bf16[32,128]{1,0:T(8,128)(2,1)S(1)} %get-tuple-element.9), channel_id=1, source_target_pairs={{0,1},{1,0},{2,3},{3,2},{4,5},{5,4},{6,7},{7,6},{8,9},{9,8},{10,11... | collective-permute-start | bytes 24584 | tf_op jit(solution)/shard_map/ppermute | solution.py:352
  70.0 8.6 %collective-permute-start.2 = (bf16[32,32,128]{2,1,0:T(8,128)(2,1)S(1)}, bf16[32,32,128]{2,1,0:T(8,128)(2,1)S(1)}, u32[]{:S(2)}, u32[]{:S(2)}) collective-permute-start(bf16[32,32,128]{2,1,0:T(8,128)(2,1)S(1)} %get-tuple-element.12), channel_id=1, source_target_pairs={{0,1},{1,0},{2,3},{3,2},{4,5},{5,4},{6,7},{7,6},{8,9},{9,8},{10,11... | collective-permute-start | bytes 786440 | tf_op jit(solution)/shard_map/ppermute | solution.py:352

commit v6 on v5

--- a/solution.py
+++ b/solution.py
@@ -185,11 +185,26 @@
     )(offsets, order, pilot, traces, table)
 
 
-def whiten_kernel(guides_ref, own_ref, far_ref, white_ref, value_ref, guide_ref):
+def total_kernel(guides_ref, guide_ref):
     guide = guides_ref[0].astype(F32)
     for line in range(1, 16):
         guide = guide + guides_ref[line].astype(F32)
     guide_ref[...] = guide
+
+
+def total_of(guides):
+    vmem = pl.BlockSpec(memory_space=pltpu.VMEM)
+    return pl.pallas_call(
+        total_kernel,
+        in_specs=[vmem],
+        out_specs=vmem,
+        out_shape=jax.ShapeDtypeStruct((PAIRS, LANES), F32),
+        cost_estimate=pl.CostEstimate(flops=2**28, bytes_accessed=2**17, transcendentals=0),
+        name="total",
+    )(guides)
+
+
+def whiten_kernel(guide_ref, own_ref, far_ref, white_ref, value_ref):
     even = (lane_index(PAIRS) // 32) % 2 == 0
     blocks = (own_ref, far_ref)
     totals = [[jnp.zeros((FEW, LANES), F32) for _ in range(SEG)] for _ in blocks]
@@ -229,7 +244,7 @@
         in_specs=[vmem] * 3,
         out_specs=vmem,
         out_shape=jax.ShapeDtypeStruct(shape, BF16),
-        scratch_shapes=[pltpu.VMEM(shape, F32), pltpu.VMEM((PAIRS, LANES), F32)],
+        scratch_shapes=[pltpu.VMEM(shape, F32)],
         compiler_params=pltpu.CompilerParams(vmem_limit_bytes=32 * 1024 * 1024),
         name="whiten",
     )(guides, own, far)
@@ -365,7 +380,7 @@
         tiled=True,
         axis_index_groups=lines,
     )
-    white = whitened_of(guides, own, far)
+    white = whitened_of(total_of(guides), own, far)
     planes = [[32 * f + 2 * z + side for f in range(BANDS) for side in range(2)] for z in range(16)]
     parts = lax.all_to_all(
         white, ("freq", "rgrp"), split_axis=0, concat_axis=0, tiled=True, axis_index_groups=planes

time: 79.9 us -> 80 us (level)
  Pallas kernels: 8.89 us -> 10.4 us
  blocking collectives: 54.1 us -> 52.9 us
  waiting for transfers between devices: 6.37 us -> 5.19 us
    pallas_call x0 -> x1, Pallas kernels: none -> 1.53 us  [total_of(): pl.pallas_call(total_kernel, in_specs=[vmem], out_specs=vmem, out_shape=j...]
    ppermute x2, waiting for transfers between devices: 6.37 us -> 5.19 us  [beside(): return lax.ppermute(value, 'rgrp', [(g, g ^ 1) for g in range(32)])]
    all_to_all x1, blocking collectives: 28 us -> 27.1 us  [local(): lax.all_to_all(white, ('freq', 'rgrp'), split_axis=0, concat_axis=0, tile...]
    ppermute x2, starting transfers between devices: 5.12 us -> 5.96 us  [beside(): return lax.ppermute(value, 'rgrp', [(g, g ^ 1) for g in range(32)])]
    ppermute x1, starting transfers between devices: 4.38 us -> 3.54 us  [local(): far = lax.ppermute(own, 'rgrp', [(g, (g + 2) % 32) for g in range(32)])]
  transfers between devices with their start and end apart: 3 -> 3, of which waited for: 2 -> 1; matrix products, arithmetic and copies ran while one was open for 0% -> 0% of each run, Pallas kernels for 2% -> 4%
where the time goes in v6:
time: 80 us; the launch traced here: 79.4 us
  blocking collectives  52.9 us (66%)
  Pallas kernels  10.4 us (13%)
  starting transfers between devices  9.5 us (12%)
  waiting for transfers between devices  5.19 us (6%)
    all_to_all x1, blocking collectives, local(): lax.all_to_all(white, ('freq', 'rgrp'), split_axis=0, concat_axis=0, tile...  27.1 us
    all_to_all x1, blocking collectives, local(): lax.all_to_all(jnp.broadcast_to(guide, (16, PAIRS, LANES)), 'rgrp', split...  25.7 us
    ppermute x2, starting transfers between devices, beside(): return lax.ppermute(value, 'rgrp', [(g, g ^ 1) for g in range(32)])  5.96 us
    ppermute x2, waiting for transfers between devices, beside(): return lax.ppermute(value, 'rgrp', [(g, g ^ 1) for g in range(32)])  5.19 us
    ppermute x1, starting transfers between devices, local(): far = lax.ppermute(own, 'rgrp', [(g, (g + 2) % 32) for g in range(32)])  3.54 us
    pallas_call x1, Pallas kernels, spectra_of(): pl.pallas_call(spectra_kernel, in_specs=[pl.BlockSpec(memory_space=pl.ANY...  2.9 us
    pallas_call x1, Pallas kernels, other_of(): pl.pallas_call(other_kernel, in_specs=[vmem], out_specs=[vmem, vmem], out...  1.9 us
  transfers between devices with their start and end apart: 3, of which 1 were waited for; matrix products, arithmetic and copies ran while one was open for 0% of the time, Pallas kernels for 4%

profile of v6, /device:TPU:1, one launch (start us, length us, event | category | flops | bytes accessed | tf_op | source)
XLA Modules:
  0.0 79.4 jit_solution(3231061566687605115)
XLA Ops:
  0.7 2.9 %spectra.1 = (bf16[16,2,64,128]{3,2,1,0:T(8,128)(2,1)S(1)}, bf16[32,128]{1,0:T(8,128)(2,1)S(1)}) custom-call(s32[4]{0:T(128)} %offset_hbm.1, s32[1,32]{1,0:T(1,128)} %order_hbm.1, s32[1]{0:T(128)S(6)} %copy.6.pilot_hbm, bf16[32,9216]{1,0:T(8,128)(2,1)} %traces_hbm.1, bf16[1,2,1024,512]{3,2,1,0:T(8,128)(2,1)} %constant.2.clone.table_hbm), custom_call_target="tpu_custom_call" | custom-call | tf_op jit(solution)/shard_map/spectra/pallas_call | solution.py:163
  3.6 4.0 %collective-permute-start = (bf16[32,128]{1,0:T(8,128)(2,1)S(1)}, bf16[32,128]{1,0:T(8,128)(2,1)S(1)}, u32[]{:S(2)}, u32[]{:S(2)}) collective-permute-start(bf16[32,128]{1,0:T(8,128)(2,1)S(1)} %get-tuple-element.9), channel_id=1, source_target_pairs={{0,1},{1,0},{2,3},{3,2},{4,5},{5,4},{6,7},{7,6},{8,9},{9,8},{10,11... | collective-permute-start | bytes 24584 | tf_op jit(solution)/shard_map/ppermute | solution.py:367
  7.6 3.5 %collective-permute-start.1 = (bf16[16,2,64,128]{3,2,1,0:T(8,128)(2,1)S(1)}, bf16[16,2,64,128]{3,2,1,0:T(8,128)(2,1)S(1)}, u32[]{:S(2)}, u32[]{:S(2)}) collective-permute-start(bf16[16,2,64,128]{3,2,1,0:T(8,128)(2,1)S(1)} %get-tuple-element.10.own_ref), channel_id=1, source_target_pairs={{0,2},{1,3},{2,4},{3,5},{4,6},{5,7},{6,8},{7,9},{8,10},{9,11},{10,... | collective-permute-start | bytes 1572872 | tf_op jit(solution)/shard_map/ppermute | solution.py:372
  11.2 0.0 collective-permute-done
  11.2 25.7 %all_to_all.10.guides_ref = bf16[16,32,128]{2,1,0:T(8,128)(2,1)} all-to-all(bf16[16,32,128]{2,1,0:T(8,128)(2,1)S(1)} %broadcast_in_dim.3), channel_id=1, replica_groups={{0,2,4,6,8,10,12,14,16,18,20,22,24,26,28,30},{1,3,5,7,9,11,13,15,17,19,..., dimensions={0} | all-to-all | bytes 262144 | tf_op jit(solution)/shard_map/all_to_all | solution.py:375
  36.9 1.5 %total.1.guide_ref = f32[32,128]{1,0:T(8,128)} custom-call(bf16[16,32,128]{2,1,0:T(8,128)(2,1)} %all_to_all.10.guides_ref), custom_call_target="tpu_custom_call" | custom-call | flops 268435456 | bytes 131072 | tf_op jit(solution)/shard_map/total/pallas_call | solution.py:197
  38.5 0.0 collective-permute-done.1.far_ref
  38.5 0.0 copy-start
  38.5 0.7 copy-done
  39.2 1.5 %whiten.1 = bf16[32,2,64,128]{3,2,1,0:T(8,128)(2,1)S(1)} custom-call(f32[32,128]{1,0:T(8,128)S(1)} %copy-done, bf16[16,2,64,128]{3,2,1,0:T(8,128)(2,1)S(1)} %get-tuple-element.10.own_ref, bf16[16,2,64,128]{3,2,1,0:T(8,128)(2,1)S(1)} %collective-permute-done.1.far_ref), custom_call_target="tpu_custom_call" | custom-call | tf_op jit(solution)/shard_map/whiten/pallas_call | solution.py:242
  40.7 27.1 %all_to_all.11.parts_ref = bf16[32,2,64,128]{3,2,1,0:T(8,128)(2,1)S(1)} all-to-all(bf16[32,2,64,128]{3,2,1,0:T(8,128)(2,1)S(1)} %whiten.1), channel_id=1, replica_groups={{0,1,32,33,64,65,96,97,128,129,160,161,192,193,224,225,256,257,288,289,..., dimensions={0} | all-to-all | bytes 2097152 | tf_op jit(solution)/shard_map/all_to_all | solution.py:385
  67.9 1.9 %cross_other.1 = (bf16[32,32,128]{2,1,0:T(8,128)(2,1)S(1)}, bf16[16,4,64,128]{3,2,1,0:T(8,128)(2,1)S(1)}) custom-call(bf16[32,2,64,128]{3,2,1,0:T(8,128)(2,1)S(1)} %all_to_all.11.parts_ref), custom_call_target="tpu_custom_call" | custom-call | tf_op jit(solution)/shard_map/cross_other/pallas_call | solution.py:313
  69.8 1.9 %collective-permute-start.2 = (bf16[32,32,128]{2,1,0:T(8,128)(2,1)S(1)}, bf16[32,32,128]{2,1,0:T(8,128)(2,1)S(1)}, u32[]{:S(2)}, u32[]{:S(2)}) collective-permute-start(bf16[32,32,128]{2,1,0:T(8,128)(2,1)S(1)} %get-tuple-element.12), channel_id=1, source_target_pairs={{0,1},{1,0},{2,3},{3,2},{4,5},{5,4},{6,7},{7,6},{8,9},{9,8},{10,11... | collective-permute-start | bytes 786440 | tf_op jit(solution)/shard_map/ppermute | solution.py:367
  71.7 1.5 %cross_mine.1.own_ref = bf16[32,32,128]{2,1,0:T(8,128)(2,1)S(1)} custom-call(bf16[16,4,64,128]{3,2,1,0:T(8,128)(2,1)S(1)} %get-tuple-element.11.block_ref), custom_call_target="tpu_custom_call" | custom-call | flops 268435456 | bytes 8388608 | tf_op jit(solution)/shard_map/cross_mine/pallas_call | solution.py:326
  73.2 5.2 %collective-permute-done.2.other_ref = bf16[32,32,128]{2,1,0:T(8,128)(2,1)S(1)} collective-permute-done((bf16[32,32,128]{2,1,0:T(8,128)(2,1)S(1)}, bf16[32,32,128]{2,1,0:T(8,128)(2,1)S(1)}, u32[]{:S(2)}, u32[]{:S(2)}) %collective-permute-start.2) | collective-permute-done | bytes 262176 | tf_op jit(solution)/shard_map/ppermute | solution.py:367
  78.4 1.0 %merge.1 = bf16[2,32,32,128]{3,2,1,0:T(8,128)(2,1)} custom-call(bf16[32,32,128]{2,1,0:T(8,128)(2,1)S(1)} %cross_mine.1.own_ref, bf16[32,32,128]{2,1,0:T(8,128)(2,1)S(1)} %collective-permute-done.2.other_ref), custom_call_target="tpu_custom_call" | custom-call | tf_op jit(solution)/shard_map/merge/pallas_call | solution.py:356
  (2 shorter events, 0.0 us)
Async XLA Ops:
  3.6 7.6 %collective-permute-start = (bf16[32,128]{1,0:T(8,128)(2,1)S(1)}, bf16[32,128]{1,0:T(8,128)(2,1)S(1)}, u32[]{:S(2)}, u32[]{:S(2)}) collective-permute-start(bf16[32,128]{1,0:T(8,128)(2,1)S(1)} %get-tuple-element.9), channel_id=1, source_target_pairs={{0,1},{1,0},{2,3},{3,2},{4,5},{5,4},{6,7},{7,6},{8,9},{9,8},{10,11... | collective-permute-start | bytes 24584 | tf_op jit(solution)/shard_map/ppermute | solution.py:367
  7.6 30.9 %collective-permute-start.1 = (bf16[16,2,64,128]{3,2,1,0:T(8,128)(2,1)S(1)}, bf16[16,2,64,128]{3,2,1,0:T(8,128)(2,1)S(1)}, u32[]{:S(2)}, u32[]{:S(2)}) collective-permute-start(bf16[16,2,64,128]{3,2,1,0:T(8,128)(2,1)S(1)} %get-tuple-element.10.own_ref), channel_id=1, source_target_pairs={{0,2},{1,3},{2,4},{3,5},{4,6},{5,7},{6,8},{7,9},{8,10},{9,11},{10,... | collective-permute-start | bytes 1572872 | tf_op jit(solution)/shard_map/ppermute | solution.py:372
  38.5 0.7 copy-start
  69.8 8.6 %collective-permute-start.2 = (bf16[32,32,128]{2,1,0:T(8,128)(2,1)S(1)}, bf16[32,32,128]{2,1,0:T(8,128)(2,1)S(1)}, u32[]{:S(2)}, u32[]{:S(2)}) collective-permute-start(bf16[32,32,128]{2,1,0:T(8,128)(2,1)S(1)} %get-tuple-element.12), channel_id=1, source_target_pairs={{0,1},{1,0},{2,3},{3,2},{4,5},{5,4},{6,7},{7,6},{8,9},{9,8},{10,11... | collective-permute-start | bytes 786440 | tf_op jit(solution)/shard_map/ppermute | solution.py:367

commit v7 on v6

--- a/solution.py
+++ b/solution.py
@@ -199,6 +199,7 @@
         in_specs=[vmem],
         out_specs=vmem,
         out_shape=jax.ShapeDtypeStruct((PAIRS, LANES), F32),
+        compiler_params=pltpu.CompilerParams(vmem_limit_bytes=32 * 1024 * 1024),
         cost_estimate=pl.CostEstimate(flops=2**28, bytes_accessed=2**17, transcendentals=0),
         name="total",
     )(guides)

time: 80 us -> 77.6 us (0.970)
  Pallas kernels: 10.4 us -> 8.89 us
    pallas_call x1, Pallas kernels: 1.53 us -> 0.02 us  [total_of(): pl.pallas_call(total_kernel, in_specs=[vmem], out_specs=vmem, out_shape=j...]
  transfers between devices with their start and end apart: 3 -> 3, of which waited for: 1 -> 1; matrix products, arithmetic and copies ran while one was open for 0% -> 0% of each run, Pallas kernels for 4% -> 2%
where the time goes in v7:
time: 77.6 us; the launch traced here: 77.1 us
  blocking collectives  52.8 us (68%)
  starting transfers between devices  9.5 us (12%)
  Pallas kernels  8.89 us (11%)
  waiting for transfers between devices  5.19 us (7%)
    all_to_all x1, blocking collectives, local(): lax.all_to_all(white, ('freq', 'rgrp'), split_axis=0, concat_axis=0, tile...  27.1 us
    all_to_all x1, blocking collectives, local(): lax.all_to_all(jnp.broadcast_to(guide, (16, PAIRS, LANES)), 'rgrp', split...  25.6 us
    ppermute x2, starting transfers between devices, beside(): return lax.ppermute(value, 'rgrp', [(g, g ^ 1) for g in range(32)])  5.96 us
    ppermute x2, waiting for transfers between devices, beside(): return lax.ppermute(value, 'rgrp', [(g, g ^ 1) for g in range(32)])  5.19 us
    ppermute x1, starting transfers between devices, local(): far = lax.ppermute(own, 'rgrp', [(g, (g + 2) % 32) for g in range(32)])  3.54 us
    pallas_call x1, Pallas kernels, spectra_of(): pl.pallas_call(spectra_kernel, in_specs=[pl.BlockSpec(memory_space=pl.ANY...  2.9 us
    pallas_call x1, Pallas kernels, other_of(): pl.pallas_call(other_kernel, in_specs=[vmem], out_specs=[vmem, vmem], out...  1.9 us
  transfers between devices with their start and end apart: 3, of which 1 were waited for; matrix products, arithmetic and copies ran while one was open for 0% of the time, Pallas kernels for 2%

profile of v7, /device:TPU:1, one launch (start us, length us, event | category | flops | bytes accessed | tf_op | source)
XLA Modules:
  0.0 77.1 jit_solution(12201400638423954349)
XLA Ops:
  0.7 2.9 %spectra.1 = (bf16[16,2,64,128]{3,2,1,0:T(8,128)(2,1)S(1)}, bf16[32,128]{1,0:T(8,128)(2,1)S(1)}) custom-call(s32[4]{0:T(128)} %offset_hbm.1, s32[1,32]{1,0:T(1,128)} %order_hbm.1, s32[1]{0:T(128)S(6)} %copy.6.pilot_hbm, bf16[32,9216]{1,0:T(8,128)(2,1)} %traces_hbm.1, bf16[1,2,1024,512]{3,2,1,0:T(8,128)(2,1)} %constant.2.clone.table_hbm), custom_call_target="tpu_custom_call" | custom-call | tf_op jit(solution)/shard_map/spectra/pallas_call | solution.py:163
  3.6 4.0 %collective-permute-start = (bf16[32,128]{1,0:T(8,128)(2,1)S(1)}, bf16[32,128]{1,0:T(8,128)(2,1)S(1)}, u32[]{:S(2)}, u32[]{:S(2)}) collective-permute-start(bf16[32,128]{1,0:T(8,128)(2,1)S(1)} %get-tuple-element.9), channel_id=1, source_target_pairs={{0,1},{1,0},{2,3},{3,2},{4,5},{5,4},{6,7},{7,6},{8,9},{9,8},{10,11... | collective-permute-start | bytes 24584 | tf_op jit(solution)/shard_map/ppermute | solution.py:368
  7.6 3.5 %collective-permute-start.1 = (bf16[16,2,64,128]{3,2,1,0:T(8,128)(2,1)S(1)}, bf16[16,2,64,128]{3,2,1,0:T(8,128)(2,1)S(1)}, u32[]{:S(2)}, u32[]{:S(2)}) collective-permute-start(bf16[16,2,64,128]{3,2,1,0:T(8,128)(2,1)S(1)} %get-tuple-element.10.own_ref), channel_id=1, source_target_pairs={{0,2},{1,3},{2,4},{3,5},{4,6},{5,7},{6,8},{7,9},{8,10},{9,11},{10,... | collective-permute-start | bytes 1572872 | tf_op jit(solution)/shard_map/ppermute | solution.py:373
  11.2 0.0 collective-permute-done
  11.2 25.6 %all_to_all.10.guides_ref = bf16[16,32,128]{2,1,0:T(8,128)(2,1)S(1)} all-to-all(bf16[16,32,128]{2,1,0:T(8,128)(2,1)S(1)} %broadcast_in_dim.3), channel_id=1, replica_groups={{0,2,4,6,8,10,12,14,16,18,20,22,24,26,28,30},{1,3,5,7,9,11,13,15,17,19,..., dimensions={0} | all-to-all | bytes 262144 | tf_op jit(solution)/shard_map/all_to_all | solution.py:376
  36.9 0.0 collective-permute-done.1.far_ref
  36.9 1.5 %whiten.1 = bf16[32,2,64,128]{3,2,1,0:T(8,128)(2,1)S(1)} custom-call(f32[32,128]{1,0:T(8,128)S(1)} %total.1.guide_ref, bf16[16,2,64,128]{3,2,1,0:T(8,128)(2,1)S(1)} %get-tuple-element.10.own_ref, bf16[16,2,64,128]{3,2,1,0:T(8,128)(2,1)S(1)} %collective-permute-done.1.far_ref), custom_call_target="tpu_custom_call" | custom-call | tf_op jit(solution)/shard_map/whiten/pallas_call | solution.py:243
  38.4 27.1 %all_to_all.11.parts_ref = bf16[32,2,64,128]{3,2,1,0:T(8,128)(2,1)S(1)} all-to-all(bf16[32,2,64,128]{3,2,1,0:T(8,128)(2,1)S(1)} %whiten.1), channel_id=1, replica_groups={{0,1,32,33,64,65,96,97,128,129,160,161,192,193,224,225,256,257,288,289,..., dimensions={0} | all-to-all | bytes 2097152 | tf_op jit(solution)/shard_map/all_to_all | solution.py:386
  65.5 1.9 %cross_other.1 = (bf16[32,32,128]{2,1,0:T(8,128)(2,1)S(1)}, bf16[16,4,64,128]{3,2,1,0:T(8,128)(2,1)S(1)}) custom-call(bf16[32,2,64,128]{3,2,1,0:T(8,128)(2,1)S(1)} %all_to_all.11.parts_ref), custom_call_target="tpu_custom_call" | custom-call | tf_op jit(solution)/shard_map/cross_other/pallas_call | solution.py:314
  67.4 1.9 %collective-permute-start.2 = (bf16[32,32,128]{2,1,0:T(8,128)(2,1)S(1)}, bf16[32,32,128]{2,1,0:T(8,128)(2,1)S(1)}, u32[]{:S(2)}, u32[]{:S(2)}) collective-permute-start(bf16[32,32,128]{2,1,0:T(8,128)(2,1)S(1)} %get-tuple-element.12), channel_id=1, source_target_pairs={{0,1},{1,0},{2,3},{3,2},{4,5},{5,4},{6,7},{7,6},{8,9},{9,8},{10,11... | collective-permute-start | bytes 786440 | tf_op jit(solution)/shard_map/ppermute | solution.py:368
  69.4 1.5 %cross_mine.1.own_ref = bf16[32,32,128]{2,1,0:T(8,128)(2,1)S(1)} custom-call(bf16[16,4,64,128]{3,2,1,0:T(8,128)(2,1)S(1)} %get-tuple-element.11.block_ref), custom_call_target="tpu_custom_call" | custom-call | flops 268435456 | bytes 8388608 | tf_op jit(solution)/shard_map/cross_mine/pallas_call | solution.py:327
  70.9 5.2 %collective-permute-done.2.other_ref = bf16[32,32,128]{2,1,0:T(8,128)(2,1)S(1)} collective-permute-done((bf16[32,32,128]{2,1,0:T(8,128)(2,1)S(1)}, bf16[32,32,128]{2,1,0:T(8,128)(2,1)S(1)}, u32[]{:S(2)}, u32[]{:S(2)}) %collective-permute-start.2) | collective-permute-done | bytes 262176 | tf_op jit(solution)/shard_map/ppermute | solution.py:368
  76.1 1.0 %merge.1 = bf16[2,32,32,128]{3,2,1,0:T(8,128)(2,1)} custom-call(bf16[32,32,128]{2,1,0:T(8,128)(2,1)S(1)} %cross_mine.1.own_ref, bf16[32,32,128]{2,1,0:T(8,128)(2,1)S(1)} %collective-permute-done.2.other_ref), custom_call_target="tpu_custom_call" | custom-call | tf_op jit(solution)/shard_map/merge/pallas_call | solution.py:357
  (3 shorter events, 0.0 us)
Async XLA Ops:
  3.6 7.6 %collective-permute-start = (bf16[32,128]{1,0:T(8,128)(2,1)S(1)}, bf16[32,128]{1,0:T(8,128)(2,1)S(1)}, u32[]{:S(2)}, u32[]{:S(2)}) collective-permute-start(bf16[32,128]{1,0:T(8,128)(2,1)S(1)} %get-tuple-element.9), channel_id=1, source_target_pairs={{0,1},{1,0},{2,3},{3,2},{4,5},{5,4},{6,7},{7,6},{8,9},{9,8},{10,11... | collective-permute-start | bytes 24584 | tf_op jit(solution)/shard_map/ppermute | solution.py:368
  7.6 29.3 %collective-permute-start.1 = (bf16[16,2,64,128]{3,2,1,0:T(8,128)(2,1)S(1)}, bf16[16,2,64,128]{3,2,1,0:T(8,128)(2,1)S(1)}, u32[]{:S(2)}, u32[]{:S(2)}) collective-permute-start(bf16[16,2,64,128]{3,2,1,0:T(8,128)(2,1)S(1)} %get-tuple-element.10.own_ref), channel_id=1, source_target_pairs={{0,2},{1,3},{2,4},{3,5},{4,6},{5,7},{6,8},{7,9},{8,10},{9,11},{10,... | collective-permute-start | bytes 1572872 | tf_op jit(solution)/shard_map/ppermute | solution.py:373
  67.4 8.6 %collective-permute-start.2 = (bf16[32,32,128]{2,1,0:T(8,128)(2,1)S(1)}, bf16[32,32,128]{2,1,0:T(8,128)(2,1)S(1)}, u32[]{:S(2)}, u32[]{:S(2)}) collective-permute-start(bf16[32,32,128]{2,1,0:T(8,128)(2,1)S(1)} %get-tuple-element.12), channel_id=1, source_target_pairs={{0,1},{1,0},{2,3},{3,2},{4,5},{5,4},{6,7},{7,6},{8,9},{9,8},{10,11... | collective-permute-start | bytes 786440 | tf_op jit(solution)/shard_map/ppermute | solution.py:368

commit v8 on v7

--- a/solution.py
+++ b/solution.py
@@ -206,18 +206,22 @@
 
 
 def whiten_kernel(guide_ref, own_ref, far_ref, white_ref, value_ref):
-    even = (lane_index(PAIRS) // 32) % 2 == 0
+    guide = guide_ref[...]
+    place = lane_index(PAIRS) // 2
+    parity = lax.broadcasted_iota(jnp.int32, (LANES, LANES), 0) % 2
+    spread = (parity == (lane_index(LANES) // 32) % 2).astype(F32).astype(BF16)
     blocks = (own_ref, far_ref)
     totals = [[jnp.zeros((FEW, LANES), F32) for _ in range(SEG)] for _ in blocks]
     for band in range(BANDS):
+        picked = [jnp.where(place == seg * BANDS + band, guide, 0.0) for seg in range(SEG)]
+        weight = jnp.dot(
+            jnp.concatenate(picked, axis=0).astype(BF16), spread, preferred_element_type=F32
+        )
         for seg in range(SEG):
-            first = 32 * seg + 2 * band
             rows = slice(seg * FEW, (seg + 1) * FEW)
-            weight = jnp.where(
-                even, guide_ref[:, first : first + 1], guide_ref[:, first + 1 : first + 2]
-            )
             for half in range(HALVES):
-                part = weight[half * FEW : (half + 1) * FEW]
+                at = seg * PAIRS + half * FEW
+                part = weight[at : at + FEW]
                 for k, block_ref in enumerate(blocks):
                     value = block_ref[band, half, rows, :].astype(F32) * part
                     value_ref[band * HALVES + half, k, rows, :] = value

time: 77.6 us -> 77.1 us (level)
  no operation moved by 1% of the time
where the time goes in v8:
time: 77.1 us; the launch traced here: 76.6 us
  blocking collectives  52.8 us (68%)
  starting transfers between devices  9.5 us (12%)
  Pallas kernels  8.41 us (11%)
  waiting for transfers between devices  5.19 us (7%)
    all_to_all x1, blocking collectives, local(): lax.all_to_all(white, ('freq', 'rgrp'), split_axis=0, concat_axis=0, tile...  27.1 us
    all_to_all x1, blocking collectives, local(): lax.all_to_all(jnp.broadcast_to(guide, (16, PAIRS, LANES)), 'rgrp', split...  25.6 us
    ppermute x2, starting transfers between devices, beside(): return lax.ppermute(value, 'rgrp', [(g, g ^ 1) for g in range(32)])  5.96 us
    ppermute x2, waiting for transfers between devices, beside(): return lax.ppermute(value, 'rgrp', [(g, g ^ 1) for g in range(32)])  5.19 us
    ppermute x1, starting transfers between devices, local(): far = lax.ppermute(own, 'rgrp', [(g, (g + 2) % 32) for g in range(32)])  3.54 us
    pallas_call x1, Pallas kernels, spectra_of(): pl.pallas_call(spectra_kernel, in_specs=[pl.BlockSpec(memory_space=pl.ANY...  2.9 us
    pallas_call x1, Pallas kernels, other_of(): pl.pallas_call(other_kernel, in_specs=[vmem], out_specs=[vmem, vmem], out...  1.9 us
  transfers between devices with their start and end apart: 3, of which 1 were waited for; matrix products, arithmetic and copies ran while one was open for 0% of the time, Pallas kernels for 2%

profile of v8, /device:TPU:1, one launch (start us, length us, event | category | flops | bytes accessed | tf_op | source)
XLA Modules:
  0.0 76.6 jit_solution(5867061959421768749)
XLA Ops:
  0.7 2.9 %spectra.1 = (bf16[16,2,64,128]{3,2,1,0:T(8,128)(2,1)S(1)}, bf16[32,128]{1,0:T(8,128)(2,1)S(1)}) custom-call(s32[4]{0:T(128)} %offset_hbm.1, s32[1,32]{1,0:T(1,128)} %order_hbm.1, s32[1]{0:T(128)S(6)} %copy.6.pilot_hbm, bf16[32,9216]{1,0:T(8,128)(2,1)} %traces_hbm.1, bf16[1,2,1024,512]{3,2,1,0:T(8,128)(2,1)} %constant.2.clone.table_hbm), custom_call_target="tpu_custom_call" | custom-call | tf_op jit(solution)/shard_map/spectra/pallas_call | solution.py:163
  3.6 4.0 %collective-permute-start = (bf16[32,128]{1,0:T(8,128)(2,1)S(1)}, bf16[32,128]{1,0:T(8,128)(2,1)S(1)}, u32[]{:S(2)}, u32[]{:S(2)}) collective-permute-start(bf16[32,128]{1,0:T(8,128)(2,1)S(1)} %get-tuple-element.9), channel_id=1, source_target_pairs={{0,1},{1,0},{2,3},{3,2},{4,5},{5,4},{6,7},{7,6},{8,9},{9,8},{10,11... | collective-permute-start | bytes 24584 | tf_op jit(solution)/shard_map/ppermute | solution.py:372
  7.6 3.5 %collective-permute-start.1 = (bf16[16,2,64,128]{3,2,1,0:T(8,128)(2,1)S(1)}, bf16[16,2,64,128]{3,2,1,0:T(8,128)(2,1)S(1)}, u32[]{:S(2)}, u32[]{:S(2)}) collective-permute-start(bf16[16,2,64,128]{3,2,1,0:T(8,128)(2,1)S(1)} %get-tuple-element.10.own_ref), channel_id=1, source_target_pairs={{0,2},{1,3},{2,4},{3,5},{4,6},{5,7},{6,8},{7,9},{8,10},{9,11},{10,... | collective-permute-start | bytes 1572872 | tf_op jit(solution)/shard_map/ppermute | solution.py:377
  11.2 0.0 collective-permute-done
  11.2 25.6 %all_to_all.10.guides_ref = bf16[16,32,128]{2,1,0:T(8,128)(2,1)S(1)} all-to-all(bf16[16,32,128]{2,1,0:T(8,128)(2,1)S(1)} %broadcast_in_dim.3), channel_id=1, replica_groups={{0,2,4,6,8,10,12,14,16,18,20,22,24,26,28,30},{1,3,5,7,9,11,13,15,17,19,..., dimensions={0} | all-to-all | bytes 262144 | tf_op jit(solution)/shard_map/all_to_all | solution.py:380
  36.9 0.0 collective-permute-done.1.far_ref
  36.9 1.0 %whiten.1 = bf16[32,2,64,128]{3,2,1,0:T(8,128)(2,1)S(1)} custom-call(f32[32,128]{1,0:T(8,128)S(1)} %total.1.guide_ref, bf16[16,2,64,128]{3,2,1,0:T(8,128)(2,1)S(1)} %get-tuple-element.10.own_ref, bf16[16,2,64,128]{3,2,1,0:T(8,128)(2,1)S(1)} %collective-permute-done.1.far_ref), custom_call_target="tpu_custom_call" | custom-call | tf_op jit(solution)/shard_map/whiten/pallas_call | solution.py:247
  37.9 27.1 %all_to_all.11.parts_ref = bf16[32,2,64,128]{3,2,1,0:T(8,128)(2,1)S(1)} all-to-all(bf16[32,2,64,128]{3,2,1,0:T(8,128)(2,1)S(1)} %whiten.1), channel_id=1, replica_groups={{0,1,32,33,64,65,96,97,128,129,160,161,192,193,224,225,256,257,288,289,..., dimensions={0} | all-to-all | bytes 2097152 | tf_op jit(solution)/shard_map/all_to_all | solution.py:390
  65.1 1.9 %cross_other.1 = (bf16[32,32,128]{2,1,0:T(8,128)(2,1)S(1)}, bf16[16,4,64,128]{3,2,1,0:T(8,128)(2,1)S(1)}) custom-call(bf16[32,2,64,128]{3,2,1,0:T(8,128)(2,1)S(1)} %all_to_all.11.parts_ref), custom_call_target="tpu_custom_call" | custom-call | tf_op jit(solution)/shard_map/cross_other/pallas_call | solution.py:318
  67.0 1.9 %collective-permute-start.2 = (bf16[32,32,128]{2,1,0:T(8,128)(2,1)S(1)}, bf16[32,32,128]{2,1,0:T(8,128)(2,1)S(1)}, u32[]{:S(2)}, u32[]{:S(2)}) collective-permute-start(bf16[32,32,128]{2,1,0:T(8,128)(2,1)S(1)} %get-tuple-element.12), channel_id=1, source_target_pairs={{0,1},{1,0},{2,3},{3,2},{4,5},{5,4},{6,7},{7,6},{8,9},{9,8},{10,11... | collective-permute-start | bytes 786440 | tf_op jit(solution)/shard_map/ppermute | solution.py:372
  68.9 1.5 %cross_mine.1.own_ref = bf16[32,32,128]{2,1,0:T(8,128)(2,1)S(1)} custom-call(bf16[16,4,64,128]{3,2,1,0:T(8,128)(2,1)S(1)} %get-tuple-element.11.block_ref), custom_call_target="tpu_custom_call" | custom-call | flops 268435456 | bytes 8388608 | tf_op jit(solution)/shard_map/cross_mine/pallas_call | solution.py:331
  70.4 5.2 %collective-permute-done.2.other_ref = bf16[32,32,128]{2,1,0:T(8,128)(2,1)S(1)} collective-permute-done((bf16[32,32,128]{2,1,0:T(8,128)(2,1)S(1)}, bf16[32,32,128]{2,1,0:T(8,128)(2,1)S(1)}, u32[]{:S(2)}, u32[]{:S(2)}) %collective-permute-start.2) | collective-permute-done | bytes 262176 | tf_op jit(solution)/shard_map/ppermute | solution.py:372
  75.6 1.0 %merge.1 = bf16[2,32,32,128]{3,2,1,0:T(8,128)(2,1)} custom-call(bf16[32,32,128]{2,1,0:T(8,128)(2,1)S(1)} %cross_mine.1.own_ref, bf16[32,32,128]{2,1,0:T(8,128)(2,1)S(1)} %collective-permute-done.2.other_ref), custom_call_target="tpu_custom_call" | custom-call | tf_op jit(solution)/shard_map/merge/pallas_call | solution.py:361
  (3 shorter events, 0.0 us)
Async XLA Ops:
  3.6 7.6 %collective-permute-start = (bf16[32,128]{1,0:T(8,128)(2,1)S(1)}, bf16[32,128]{1,0:T(8,128)(2,1)S(1)}, u32[]{:S(2)}, u32[]{:S(2)}) collective-permute-start(bf16[32,128]{1,0:T(8,128)(2,1)S(1)} %get-tuple-element.9), channel_id=1, source_target_pairs={{0,1},{1,0},{2,3},{3,2},{4,5},{5,4},{6,7},{7,6},{8,9},{9,8},{10,11... | collective-permute-start | bytes 24584 | tf_op jit(solution)/shard_map/ppermute | solution.py:372
  7.6 29.3 %collective-permute-start.1 = (bf16[16,2,64,128]{3,2,1,0:T(8,128)(2,1)S(1)}, bf16[16,2,64,128]{3,2,1,0:T(8,128)(2,1)S(1)}, u32[]{:S(2)}, u32[]{:S(2)}) collective-permute-start(bf16[16,2,64,128]{3,2,1,0:T(8,128)(2,1)S(1)} %get-tuple-element.10.own_ref), channel_id=1, source_target_pairs={{0,2},{1,3},{2,4},{3,5},{4,6},{5,7},{6,8},{7,9},{8,10},{9,11},{10,... | collective-permute-start | bytes 1572872 | tf_op jit(solution)/shard_map/ppermute | solution.py:377
  67.0 8.6 %collective-permute-start.2 = (bf16[32,32,128]{2,1,0:T(8,128)(2,1)S(1)}, bf16[32,32,128]{2,1,0:T(8,128)(2,1)S(1)}, u32[]{:S(2)}, u32[]{:S(2)}) collective-permute-start(bf16[32,32,128]{2,1,0:T(8,128)(2,1)S(1)} %get-tuple-element.12), channel_id=1, source_target_pairs={{0,1},{1,0},{2,3},{3,2},{4,5},{5,4},{6,7},{7,6},{8,9},{9,8},{10,11... | collective-permute-start | bytes 786440 | tf_op jit(solution)/shard_map/ppermute | solution.py:372

commit v9 on v8

--- a/solution.py
+++ b/solution.py
@@ -63,18 +63,21 @@
         window = [
             jnp.where(lane < LANES - rest, rolled[tile], rolled[tile + 1]) for tile in range(tiles)
         ]
-        quarter = tiles // 4
+        ordered = jnp.dot(
+            chosen, jnp.concatenate(window, axis=1).astype(BF16), preferred_element_type=F32
+        )
         first, second, third, fourth = (
-            jnp.concatenate(window[k * quarter : (k + 1) * quarter], axis=1) for k in range(4)
+            ordered[:, k * QUARTER : (k + 1) * QUARTER] for k in range(4)
         )
         even, odd = first + third, second + fourth
-        mixes = (first - third, second - fourth, even - odd, even + odd)
-        for k, mix in enumerate(mixes):
-            mix = jnp.dot(chosen, mix.astype(BF16), preferred_element_type=F32)
+        for k, mix in enumerate((first - third, second - fourth, even - odd, even + odd)):
             at = (k % 2) * LANES + seg * CH
             wide_ref[k // 2, at : at + CH, :] = mix
     for parity in range(2):
-        wave_ref[parity] = jnp.transpose(wide_ref[parity]).astype(BF16)
+        mix = jnp.transpose(wide_ref[parity])
+        high = mix.astype(BF16)
+        wave_ref[parity, 0] = high
+        wave_ref[parity, 1] = (mix - high.astype(F32)).astype(BF16)
 
 
 def spectra_kernel(
@@ -113,7 +116,8 @@
     for slab in range(PARTS):
         table[slab].wait()
         products = [
-            jnp.dot(table_ref[slab, parity], wave_ref[parity], preferred_element_type=F32)
+            jnp.dot(table_ref[slab, parity], wave_ref[parity, 0], preferred_element_type=F32)
+            + jnp.dot(table_ref[slab, parity], wave_ref[parity, 1], preferred_element_type=F32)
             for parity in range(2)
         ]
         for local_band in range(BANDS // PARTS):
@@ -175,7 +179,7 @@
             pltpu.VMEM((CH, SPAN), BF16),
             pltpu.VMEM((PARTS, 2, 2 * PAIRS * BANDS // PARTS, QUARTER), BF16),
             pltpu.VMEM((2, 2 * LANES, QUARTER), F32),
-            pltpu.VMEM((2, QUARTER, 2 * LANES), BF16),
+            pltpu.VMEM((2, 2, QUARTER, 2 * LANES), BF16),
             pltpu.VMEM((PAIRS, LANES), F32),
             pltpu.SemaphoreType.DMA((4,)),
             pltpu.SemaphoreType.DMA((PARTS,)),

time: 77.1 us -> 77.6 us (level)
  no operation moved by 1% of the time
where the time goes in v9:
time: 77.6 us; the launch traced here: 77.2 us
  blocking collectives  52.8 us (68%)
  starting transfers between devices  9.5 us (12%)
  Pallas kernels  8.95 us (12%)
  waiting for transfers between devices  5.19 us (7%)
    all_to_all x1, blocking collectives, local(): lax.all_to_all(white, ('freq', 'rgrp'), split_axis=0, concat_axis=0, tile...  27.1 us
    all_to_all x1, blocking collectives, local(): lax.all_to_all(jnp.broadcast_to(guide, (16, PAIRS, LANES)), 'rgrp', split...  25.6 us
    ppermute x2, starting transfers between devices, beside(): return lax.ppermute(value, 'rgrp', [(g, g ^ 1) for g in range(32)])  5.96 us
    ppermute x2, waiting for transfers between devices, beside(): return lax.ppermute(value, 'rgrp', [(g, g ^ 1) for g in range(32)])  5.19 us
    ppermute x1, starting transfers between devices, local(): far = lax.ppermute(own, 'rgrp', [(g, (g + 2) % 32) for g in range(32)])  3.55 us
    pallas_call x1, Pallas kernels, spectra_of(): pl.pallas_call(spectra_kernel, in_specs=[pl.BlockSpec(memory_space=pl.ANY...  3.43 us
    pallas_call x1, Pallas kernels, other_of(): pl.pallas_call(other_kernel, in_specs=[vmem], out_specs=[vmem, vmem], out...  1.9 us
  transfers between devices with their start and end apart: 3, of which 1 were waited for; matrix products, arithmetic and copies ran while one was open for 0% of the time, Pallas kernels for 2%

profile of v9, /device:TPU:1, one launch (start us, length us, event | category | flops | bytes accessed | tf_op | source)
XLA Modules:
  0.0 77.2 jit_solution(17169404454866237131)
XLA Ops:
  0.7 3.4 %spectra.1 = (bf16[16,2,64,128]{3,2,1,0:T(8,128)(2,1)S(1)}, bf16[32,128]{1,0:T(8,128)(2,1)S(1)}) custom-call(s32[4]{0:T(128)} %offset_hbm.1, s32[1,32]{1,0:T(1,128)} %order_hbm.1, s32[1]{0:T(128)S(6)} %copy.6.pilot_hbm, bf16[32,9216]{1,0:T(8,128)(2,1)} %traces_hbm.1, bf16[1,2,1024,512]{3,2,1,0:T(8,128)(2,1)} %constant.2.clone.table_hbm), custom_call_target="tpu_custom_call" | custom-call | tf_op jit(solution)/shard_map/spectra/pallas_call | solution.py:167
  4.1 4.0 %collective-permute-start = (bf16[32,128]{1,0:T(8,128)(2,1)S(1)}, bf16[32,128]{1,0:T(8,128)(2,1)S(1)}, u32[]{:S(2)}, u32[]{:S(2)}) collective-permute-start(bf16[32,128]{1,0:T(8,128)(2,1)S(1)} %get-tuple-element.9), channel_id=1, source_target_pairs={{0,1},{1,0},{2,3},{3,2},{4,5},{5,4},{6,7},{7,6},{8,9},{9,8},{10,11... | collective-permute-start | bytes 24584 | tf_op jit(solution)/shard_map/ppermute | solution.py:376
  8.1 3.5 %collective-permute-start.1 = (bf16[16,2,64,128]{3,2,1,0:T(8,128)(2,1)S(1)}, bf16[16,2,64,128]{3,2,1,0:T(8,128)(2,1)S(1)}, u32[]{:S(2)}, u32[]{:S(2)}) collective-permute-start(bf16[16,2,64,128]{3,2,1,0:T(8,128)(2,1)S(1)} %get-tuple-element.10.own_ref), channel_id=1, source_target_pairs={{0,2},{1,3},{2,4},{3,5},{4,6},{5,7},{6,8},{7,9},{8,10},{9,11},{10,... | collective-permute-start | bytes 1572872 | tf_op jit(solution)/shard_map/ppermute | solution.py:381
  11.7 0.0 collective-permute-done
  11.7 25.6 %all_to_all.10.guides_ref = bf16[16,32,128]{2,1,0:T(8,128)(2,1)S(1)} all-to-all(bf16[16,32,128]{2,1,0:T(8,128)(2,1)S(1)} %broadcast_in_dim.3), channel_id=1, replica_groups={{0,2,4,6,8,10,12,14,16,18,20,22,24,26,28,30},{1,3,5,7,9,11,13,15,17,19,..., dimensions={0} | all-to-all | bytes 262144 | tf_op jit(solution)/shard_map/all_to_all | solution.py:384
  37.4 0.0 collective-permute-done.1.far_ref
  37.4 1.0 %whiten.1 = bf16[32,2,64,128]{3,2,1,0:T(8,128)(2,1)S(1)} custom-call(f32[32,128]{1,0:T(8,128)S(1)} %total.1.guide_ref, bf16[16,2,64,128]{3,2,1,0:T(8,128)(2,1)S(1)} %get-tuple-element.10.own_ref, bf16[16,2,64,128]{3,2,1,0:T(8,128)(2,1)S(1)} %collective-permute-done.1.far_ref), custom_call_target="tpu_custom_call" | custom-call | tf_op jit(solution)/shard_map/whiten/pallas_call | solution.py:251
  38.5 27.1 %all_to_all.11.parts_ref = bf16[32,2,64,128]{3,2,1,0:T(8,128)(2,1)S(1)} all-to-all(bf16[32,2,64,128]{3,2,1,0:T(8,128)(2,1)S(1)} %whiten.1), channel_id=1, replica_groups={{0,1,32,33,64,65,96,97,128,129,160,161,192,193,224,225,256,257,288,289,..., dimensions={0} | all-to-all | bytes 2097152 | tf_op jit(solution)/shard_map/all_to_all | solution.py:394
  65.6 1.9 %cross_other.1 = (bf16[32,32,128]{2,1,0:T(8,128)(2,1)S(1)}, bf16[16,4,64,128]{3,2,1,0:T(8,128)(2,1)S(1)}) custom-call(bf16[32,2,64,128]{3,2,1,0:T(8,128)(2,1)S(1)} %all_to_all.11.parts_ref), custom_call_target="tpu_custom_call" | custom-call | tf_op jit(solution)/shard_map/cross_other/pallas_call | solution.py:322
  67.5 1.9 %collective-permute-start.2 = (bf16[32,32,128]{2,1,0:T(8,128)(2,1)S(1)}, bf16[32,32,128]{2,1,0:T(8,128)(2,1)S(1)}, u32[]{:S(2)}, u32[]{:S(2)}) collective-permute-start(bf16[32,32,128]{2,1,0:T(8,128)(2,1)S(1)} %get-tuple-element.12), channel_id=1, source_target_pairs={{0,1},{1,0},{2,3},{3,2},{4,5},{5,4},{6,7},{7,6},{8,9},{9,8},{10,11... | collective-permute-start | bytes 786440 | tf_op jit(solution)/shard_map/ppermute | solution.py:376
  69.4 1.5 %cross_mine.1.own_ref = bf16[32,32,128]{2,1,0:T(8,128)(2,1)S(1)} custom-call(bf16[16,4,64,128]{3,2,1,0:T(8,128)(2,1)S(1)} %get-tuple-element.11.block_ref), custom_call_target="tpu_custom_call" | custom-call | flops 268435456 | bytes 8388608 | tf_op jit(solution)/shard_map/cross_mine/pallas_call | solution.py:335
  71.0 5.2 %collective-permute-done.2.other_ref = bf16[32,32,128]{2,1,0:T(8,128)(2,1)S(1)} collective-permute-done((bf16[32,32,128]{2,1,0:T(8,128)(2,1)S(1)}, bf16[32,32,128]{2,1,0:T(8,128)(2,1)S(1)}, u32[]{:S(2)}, u32[]{:S(2)}) %collective-permute-start.2) | collective-permute-done | bytes 262176 | tf_op jit(solution)/shard_map/ppermute | solution.py:376
  76.1 1.0 %merge.1 = bf16[2,32,32,128]{3,2,1,0:T(8,128)(2,1)} custom-call(bf16[32,32,128]{2,1,0:T(8,128)(2,1)S(1)} %cross_mine.1.own_ref, bf16[32,32,128]{2,1,0:T(8,128)(2,1)S(1)} %collective-permute-done.2.other_ref), custom_call_target="tpu_custom_call" | custom-call | tf_op jit(solution)/shard_map/merge/pallas_call | solution.py:365
  (3 shorter events, 0.0 us)
Async XLA Ops:
  4.1 7.6 %collective-permute-start = (bf16[32,128]{1,0:T(8,128)(2,1)S(1)}, bf16[32,128]{1,0:T(8,128)(2,1)S(1)}, u32[]{:S(2)}, u32[]{:S(2)}) collective-permute-start(bf16[32,128]{1,0:T(8,128)(2,1)S(1)} %get-tuple-element.9), channel_id=1, source_target_pairs={{0,1},{1,0},{2,3},{3,2},{4,5},{5,4},{6,7},{7,6},{8,9},{9,8},{10,11... | collective-permute-start | bytes 24584 | tf_op jit(solution)/shard_map/ppermute | solution.py:376
  8.1 29.3 %collective-permute-start.1 = (bf16[16,2,64,128]{3,2,1,0:T(8,128)(2,1)S(1)}, bf16[16,2,64,128]{3,2,1,0:T(8,128)(2,1)S(1)}, u32[]{:S(2)}, u32[]{:S(2)}) collective-permute-start(bf16[16,2,64,128]{3,2,1,0:T(8,128)(2,1)S(1)} %get-tuple-element.10.own_ref), channel_id=1, source_target_pairs={{0,2},{1,3},{2,4},{3,5},{4,6},{5,7},{6,8},{7,9},{8,10},{9,11},{10,... | collective-permute-start | bytes 1572872 | tf_op jit(solution)/shard_map/ppermute | solution.py:381
  67.5 8.6 %collective-permute-start.2 = (bf16[32,32,128]{2,1,0:T(8,128)(2,1)S(1)}, bf16[32,32,128]{2,1,0:T(8,128)(2,1)S(1)}, u32[]{:S(2)}, u32[]{:S(2)}) collective-permute-start(bf16[32,32,128]{2,1,0:T(8,128)(2,1)S(1)} %get-tuple-element.12), channel_id=1, source_target_pairs={{0,1},{1,0},{2,3},{3,2},{4,5},{5,4},{6,7},{7,6},{8,9},{9,8},{10,11... | collective-permute-start | bytes 786440 | tf_op jit(solution)/shard_map/ppermute | solution.py:376

commit v10 on v9

--- a/solution.py
+++ b/solution.py
@@ -259,37 +259,38 @@
     )(guides, own, far)
 
 
-def gather_rows(parts_ref, block_ref, wide_ref):
+def spread_rows(parts_ref, wide_ref):
     for window in range(BANDS):
         for which in range(4):
             at = window * PITCH + which * ROWS
             part = parts_ref[window * HALVES + which // 2, which % 2]
             wide_ref[at : at + ROWS, :] = part.astype(F32)
-    for pair in range(FEW):
-        for which in range(4):
-            rows = [
-                wide_ref[pl.ds(which * ROWS + seg * FEW + pair, BANDS, stride=PITCH), :]
-                for seg in range(SEG)
-            ]
-            block_ref[pair, which] = jnp.concatenate(rows, axis=0).astype(BF16)
-
-
-def cross_rows(left_side, block_ref, out_ref, near_ref, far_ref):
+
+
+def gathered_row(pair, which, wide_ref):
+    rows = [
+        wide_ref[pl.ds(which * ROWS + seg * FEW + pair, BANDS, stride=PITCH), :]
+        for seg in range(SEG)
+    ]
+    return jnp.concatenate(rows, axis=0)
+
+
+def stack_pair(pair, left, rights, stack_refs):
     sign = jnp.where(lane_index(BANDS * SEG) < 64, 1.0, -1.0)
-    for pair in range(FEW):
-        turned = jnp.transpose(block_ref[pair, 2 * left_side].astype(F32))
-        left = jnp.concatenate([turned[:64], turned[64:]], axis=1).astype(BF16)
-        for which, stack_ref in ((3 * (1 - left_side), near_ref), (2 * left_side + 1, far_ref)):
-            right = block_ref[pair, which].astype(F32)
-            mix = jnp.concatenate([right * sign, pltpu.roll(right, 64, 1)], axis=0).astype(BF16)
-            product = jnp.dot(left, mix, preferred_element_type=F32)
-            stack_ref[pair * 2 * CH : (pair + 1) * 2 * CH, :] = product
-
+    turned = jnp.transpose(left)
+    left = jnp.concatenate([turned[:64], turned[64:]], axis=1).astype(BF16)
+    for right, stack_ref in zip(rights, stack_refs):
+        mix = jnp.concatenate([right * sign, pltpu.roll(right, 64, 1)], axis=0).astype(BF16)
+        product = jnp.dot(left, mix, preferred_element_type=F32)
+        stack_ref[pair * 2 * CH : (pair + 1) * 2 * CH, :] = product
+
+
+def unstack(out_ref, stack_refs):
     lane = lane_index(CH)
     even = lane % 2 == 0
     for first in range(0, CH, 4):
         pieces = {}
-        for back, stack_ref in enumerate((near_ref, far_ref)):
+        for back, stack_ref in enumerate(stack_refs):
             rows = [stack_ref[pl.ds(first + k, 2 * FEW, stride=CH), :] for k in range(4)]
             turned = jnp.transpose(jnp.concatenate(rows, axis=0)) * 0.125
             pieces[back] = jnp.where(even, turned[:32], turned[32:64])
@@ -305,12 +306,25 @@
 
 
 def other_kernel(parts_ref, out_ref, block_ref, wide_ref, near_ref, far_ref):
-    gather_rows(parts_ref, block_ref, wide_ref)
-    cross_rows(1 - lax.axis_index("rgrp") % 2, block_ref, out_ref, near_ref, far_ref)
+    spread_rows(parts_ref, wide_ref)
+    first = lax.axis_index("rgrp") % 2 == 0
+    for pair in range(FEW):
+        a, a_far, b, b_far = (gathered_row(pair, which, wide_ref) for which in range(4))
+        left, near, far = (
+            jnp.where(first, b, a), jnp.where(first, a, b_far), jnp.where(first, b_far, a_far)
+        )
+        stack_pair(pair, left, (near, far), (near_ref, far_ref))
+        block_ref[pair, 0] = jnp.where(first, a, b).astype(BF16)
+        block_ref[pair, 1] = jnp.where(first, b_far, a).astype(BF16)
+        block_ref[pair, 2] = jnp.where(first, a_far, b_far).astype(BF16)
+    unstack(out_ref, (near_ref, far_ref))
 
 
 def mine_kernel(block_ref, out_ref, near_ref, far_ref):
-    cross_rows(lax.axis_index("rgrp") % 2, block_ref, out_ref, near_ref, far_ref)
+    for pair in range(FEW):
+        left, near, far = (block_ref[pair, k].astype(F32) for k in range(3))
+        stack_pair(pair, left, (near, far), (near_ref, far_ref))
+    unstack(out_ref, (near_ref, far_ref))
 
 
 STACK = pltpu.VMEM((2 * FEW * CH, LANES), F32)
@@ -323,7 +337,7 @@
         other_kernel,
         in_specs=[vmem],
         out_specs=[vmem, vmem],
-        out_shape=[CROSS, jax.ShapeDtypeStruct((FEW, 4, BANDS * SEG, LANES), BF16)],
+        out_shape=[CROSS, jax.ShapeDtypeStruct((FEW, 3, BANDS * SEG, LANES), BF16)],
         scratch_shapes=[pltpu.VMEM((BANDS * PITCH, LANES), F32), STACK, STACK],
         compiler_params=pltpu.CompilerParams(vmem_limit_bytes=32 * 1024 * 1024),
         name="cross_other",

time: 77.6 us -> 77.6 us (level)
  no operation moved by 1% of the time
where the time goes in v10:
time: 77.6 us; the launch traced here: 77.1 us
  blocking collectives  52.8 us (68%)
  starting transfers between devices  9.5 us (12%)
  Pallas kernels  8.85 us (11%)
  waiting for transfers between devices  5.2 us (7%)
    all_to_all x1, blocking collectives, local(): lax.all_to_all(white, ('freq', 'rgrp'), split_axis=0, concat_axis=0, tile...  27.1 us
    all_to_all x1, blocking collectives, local(): lax.all_to_all(jnp.broadcast_to(guide, (16, PAIRS, LANES)), 'rgrp', split...  25.6 us
    ppermute x2, starting transfers between devices, beside(): return lax.ppermute(value, 'rgrp', [(g, g ^ 1) for g in range(32)])  5.96 us
    ppermute x2, waiting for transfers between devices, beside(): return lax.ppermute(value, 'rgrp', [(g, g ^ 1) for g in range(32)])  5.2 us
    ppermute x1, starting transfers between devices, local(): far = lax.ppermute(own, 'rgrp', [(g, (g + 2) % 32) for g in range(32)])  3.55 us
    pallas_call x1, Pallas kernels, spectra_of(): pl.pallas_call(spectra_kernel, in_specs=[pl.BlockSpec(memory_space=pl.ANY...  3.43 us
    pallas_call x1, Pallas kernels, other_of(): pl.pallas_call(other_kernel, in_specs=[vmem], out_specs=[vmem, vmem], out...  1.82 us
  transfers between devices with their start and end apart: 3, of which 1 were waited for; matrix products, arithmetic and copies ran while one was open for 0% of the time, Pallas kernels for 2%

profile of v10, /device:TPU:1, one launch (start us, length us, event | category | flops | bytes accessed | tf_op | source)
XLA Modules:
  0.0 77.1 jit_solution(17410158101012785763)
XLA Ops:
  0.7 3.4 %spectra.1 = (bf16[16,2,64,128]{3,2,1,0:T(8,128)(2,1)S(1)}, bf16[32,128]{1,0:T(8,128)(2,1)S(1)}) custom-call(s32[4]{0:T(128)} %offset_hbm.1, s32[1,32]{1,0:T(1,128)} %order_hbm.1, s32[1]{0:T(128)S(6)} %copy.6.pilot_hbm, bf16[32,9216]{1,0:T(8,128)(2,1)} %traces_hbm.1, bf16[1,2,1024,512]{3,2,1,0:T(8,128)(2,1)} %constant.2.clone.table_hbm), custom_call_target="tpu_custom_call" | custom-call | tf_op jit(solution)/shard_map/spectra/pallas_call | solution.py:167
  4.1 4.0 %collective-permute-start = (bf16[32,128]{1,0:T(8,128)(2,1)S(1)}, bf16[32,128]{1,0:T(8,128)(2,1)S(1)}, u32[]{:S(2)}, u32[]{:S(2)}) collective-permute-start(bf16[32,128]{1,0:T(8,128)(2,1)S(1)} %get-tuple-element.9), channel_id=1, source_target_pairs={{0,1},{1,0},{2,3},{3,2},{4,5},{5,4},{6,7},{7,6},{8,9},{9,8},{10,11... | collective-permute-start | bytes 24584 | tf_op jit(solution)/shard_map/ppermute | solution.py:390
  8.1 3.5 %collective-permute-start.1 = (bf16[16,2,64,128]{3,2,1,0:T(8,128)(2,1)S(1)}, bf16[16,2,64,128]{3,2,1,0:T(8,128)(2,1)S(1)}, u32[]{:S(2)}, u32[]{:S(2)}) collective-permute-start(bf16[16,2,64,128]{3,2,1,0:T(8,128)(2,1)S(1)} %get-tuple-element.10.own_ref), channel_id=1, source_target_pairs={{0,2},{1,3},{2,4},{3,5},{4,6},{5,7},{6,8},{7,9},{8,10},{9,11},{10,... | collective-permute-start | bytes 1572872 | tf_op jit(solution)/shard_map/ppermute | solution.py:395
  11.7 0.0 collective-permute-done
  11.7 25.6 %all_to_all.10.guides_ref = bf16[16,32,128]{2,1,0:T(8,128)(2,1)S(1)} all-to-all(bf16[16,32,128]{2,1,0:T(8,128)(2,1)S(1)} %broadcast_in_dim.3), channel_id=1, replica_groups={{0,2,4,6,8,10,12,14,16,18,20,22,24,26,28,30},{1,3,5,7,9,11,13,15,17,19,..., dimensions={0} | all-to-all | bytes 262144 | tf_op jit(solution)/shard_map/all_to_all | solution.py:398
  37.4 0.0 collective-permute-done.1.far_ref
  37.4 1.0 %whiten.1 = bf16[32,2,64,128]{3,2,1,0:T(8,128)(2,1)S(1)} custom-call(f32[32,128]{1,0:T(8,128)S(1)} %total.1.guide_ref, bf16[16,2,64,128]{3,2,1,0:T(8,128)(2,1)S(1)} %get-tuple-element.10.own_ref, bf16[16,2,64,128]{3,2,1,0:T(8,128)(2,1)S(1)} %collective-permute-done.1.far_ref), custom_call_target="tpu_custom_call" | custom-call | tf_op jit(solution)/shard_map/whiten/pallas_call | solution.py:251
  38.5 27.1 %all_to_all.11.parts_ref = bf16[32,2,64,128]{3,2,1,0:T(8,128)(2,1)S(1)} all-to-all(bf16[32,2,64,128]{3,2,1,0:T(8,128)(2,1)S(1)} %whiten.1), channel_id=1, replica_groups={{0,1,32,33,64,65,96,97,128,129,160,161,192,193,224,225,256,257,288,289,..., dimensions={0} | all-to-all | bytes 2097152 | tf_op jit(solution)/shard_map/all_to_all | solution.py:408
  65.6 1.8 %cross_other.1 = (bf16[32,32,128]{2,1,0:T(8,128)(2,1)S(1)}, bf16[16,3,64,128]{3,2,1,0:T(8,128)(2,1)S(1)}) custom-call(bf16[32,2,64,128]{3,2,1,0:T(8,128)(2,1)S(1)} %all_to_all.11.parts_ref), custom_call_target="tpu_custom_call" | custom-call | tf_op jit(solution)/shard_map/cross_other/pallas_call | solution.py:336
  67.4 1.9 %collective-permute-start.2 = (bf16[32,32,128]{2,1,0:T(8,128)(2,1)S(1)}, bf16[32,32,128]{2,1,0:T(8,128)(2,1)S(1)}, u32[]{:S(2)}, u32[]{:S(2)}) collective-permute-start(bf16[32,32,128]{2,1,0:T(8,128)(2,1)S(1)} %get-tuple-element.12), channel_id=1, source_target_pairs={{0,1},{1,0},{2,3},{3,2},{4,5},{5,4},{6,7},{7,6},{8,9},{9,8},{10,11... | collective-permute-start | bytes 786440 | tf_op jit(solution)/shard_map/ppermute | solution.py:390
  69.3 1.5 %cross_mine.1.own_ref = bf16[32,32,128]{2,1,0:T(8,128)(2,1)S(1)} custom-call(bf16[16,3,64,128]{3,2,1,0:T(8,128)(2,1)S(1)} %get-tuple-element.11.block_ref), custom_call_target="tpu_custom_call" | custom-call | flops 268435456 | bytes 8388608 | tf_op jit(solution)/shard_map/cross_mine/pallas_call | solution.py:349
  70.9 5.2 %collective-permute-done.2.other_ref = bf16[32,32,128]{2,1,0:T(8,128)(2,1)S(1)} collective-permute-done((bf16[32,32,128]{2,1,0:T(8,128)(2,1)S(1)}, bf16[32,32,128]{2,1,0:T(8,128)(2,1)S(1)}, u32[]{:S(2)}, u32[]{:S(2)}) %collective-permute-start.2) | collective-permute-done | bytes 262176 | tf_op jit(solution)/shard_map/ppermute | solution.py:390
  76.1 1.0 %merge.1 = bf16[2,32,32,128]{3,2,1,0:T(8,128)(2,1)} custom-call(bf16[32,32,128]{2,1,0:T(8,128)(2,1)S(1)} %cross_mine.1.own_ref, bf16[32,32,128]{2,1,0:T(8,128)(2,1)S(1)} %collective-permute-done.2.other_ref), custom_call_target="tpu_custom_call" | custom-call | tf_op jit(solution)/shard_map/merge/pallas_call | solution.py:379
  (3 shorter events, 0.0 us)
Async XLA Ops:
  4.1 7.6 %collective-permute-start = (bf16[32,128]{1,0:T(8,128)(2,1)S(1)}, bf16[32,128]{1,0:T(8,128)(2,1)S(1)}, u32[]{:S(2)}, u32[]{:S(2)}) collective-permute-start(bf16[32,128]{1,0:T(8,128)(2,1)S(1)} %get-tuple-element.9), channel_id=1, source_target_pairs={{0,1},{1,0},{2,3},{3,2},{4,5},{5,4},{6,7},{7,6},{8,9},{9,8},{10,11... | collective-permute-start | bytes 24584 | tf_op jit(solution)/shard_map/ppermute | solution.py:390
  8.1 29.3 %collective-permute-start.1 = (bf16[16,2,64,128]{3,2,1,0:T(8,128)(2,1)S(1)}, bf16[16,2,64,128]{3,2,1,0:T(8,128)(2,1)S(1)}, u32[]{:S(2)}, u32[]{:S(2)}) collective-permute-start(bf16[16,2,64,128]{3,2,1,0:T(8,128)(2,1)S(1)} %get-tuple-element.10.own_ref), channel_id=1, source_target_pairs={{0,2},{1,3},{2,4},{3,5},{4,6},{5,7},{6,8},{7,9},{8,10},{9,11},{10,... | collective-permute-start | bytes 1572872 | tf_op jit(solution)/shard_map/ppermute | solution.py:395
  67.4 8.6 %collective-permute-start.2 = (bf16[32,32,128]{2,1,0:T(8,128)(2,1)S(1)}, bf16[32,32,128]{2,1,0:T(8,128)(2,1)S(1)}, u32[]{:S(2)}, u32[]{:S(2)}) collective-permute-start(bf16[32,32,128]{2,1,0:T(8,128)(2,1)S(1)} %get-tuple-element.12), channel_id=1, source_target_pairs={{0,1},{1,0},{2,3},{3,2},{4,5},{5,4},{6,7},{7,6},{8,9},{9,8},{10,11... | collective-permute-start | bytes 786440 | tf_op jit(solution)/shard_map/ppermute | solution.py:390

commit v11 on v10

--- a/solution.py
+++ b/solution.py
@@ -12,7 +12,6 @@
 
 L = 2048
 QUARTER = 512
-PARTS = 1
 BANDS = 16
 SEG = 4
 CH = 32
@@ -28,14 +27,17 @@
 
 
 def quarter_table():
-    part, parity, band, pair = np.ogrid[:PARTS, :2, : BANDS // PARTS, :PAIRS]
-    which_bin = 64 * (part * (BANDS // PARTS) + band) + 2 * pair + parity + 1
-    sample = np.arange(QUARTER)
-    residue = (which_bin[..., None] * sample) % L
+    place = np.arange(PAIRS)
+    pair = 16 * (place // 16) + 2 * (place % 8) + place // 8 % 2
+    band = 64 * np.arange(BANDS)[:, None]
+    bins = np.stack([band + 2 * pair + 1, band + 2 * pair + 2])
+    residue = (bins[..., None] * np.arange(QUARTER)) % L
     phase_angle = residue.astype(np.float32) * np.float32(2.0 * math.pi / L)
     factor = np.float32(1.0 / math.sqrt(L))
-    both = np.stack([np.cos(phase_angle) * factor, np.sin(phase_angle) * factor], axis=3)
-    return both.reshape(PARTS, 2, -1, QUARTER).astype(ml_dtypes.bfloat16)
+    odd, even = np.stack([np.cos(phase_angle) * factor, np.sin(phase_angle) * factor], axis=2)
+    even = even.reshape(BANDS, 2, 2, 2, 8, QUARTER).transpose(3, 0, 1, 2, 4, 5)
+    rows = [part.reshape(-1, QUARTER) for part in (odd, even)]
+    return np.stack(rows).astype(ml_dtypes.bfloat16)
 
 
 def lane_index(rows):
@@ -76,14 +78,20 @@
     for parity in range(2):
         mix = jnp.transpose(wide_ref[parity])
         high = mix.astype(BF16)
-        wave_ref[parity, 0] = high
-        wave_ref[parity, 1] = (mix - high.astype(F32)).astype(BF16)
+        low = (mix - high.astype(F32)).astype(BF16)
+        if parity == 0:
+            wave_ref[0, 0] = high
+            wave_ref[0, 1] = low
+        else:
+            for k in range(2):
+                lanes = slice(k * LANES, (k + 1) * LANES)
+                wave_ref[1, k] = jnp.concatenate([high[:, lanes], low[:, lanes]], axis=1)
 
 
 def spectra_kernel(
     offset_hbm, order_hbm, pilot_hbm, traces_hbm, table_hbm, block_ref, guide_ref,
     offset_ref, order_ref, pilot_ref, traces_ref, table_ref, wide_ref, wave_ref,
-    power_ref, sems, table_sems,
+    power_ref, sems,
 ):
     small = [
         pltpu.make_async_copy(source, target, sems.at[k])
@@ -98,12 +106,8 @@
     ]
     for copy in small:
         copy.start()
-    table = [
-        pltpu.make_async_copy(table_hbm.at[part], table_ref.at[part], table_sems.at[part])
-        for part in range(PARTS)
-    ]
-    for copy in table:
-        copy.start()
+    table = pltpu.make_async_copy(table_hbm, table_ref, sems.at[len(small)])
+    table.start()
     power_ref[...] = jnp.zeros_like(power_ref)
     for copy in small:
         copy.wait()
@@ -111,49 +115,49 @@
 
     lane = lane_index(PAIRS)
     channel = lax.rem(pilot_ref[0], CH)
-    odd_pair = lax.broadcasted_iota(jnp.int32, (PAIRS, LANES), 0) % 2 == 1
+    odd_pair = lax.broadcasted_iota(jnp.int32, (PAIRS, LANES), 0) // 8 % 2 == 1
     flip = jnp.where(odd_pair, -1.0, 1.0)
-    for slab in range(PARTS):
-        table[slab].wait()
-        products = [
-            jnp.dot(table_ref[slab, parity], wave_ref[parity, 0], preferred_element_type=F32)
-            + jnp.dot(table_ref[slab, parity], wave_ref[parity, 1], preferred_element_type=F32)
-            for parity in range(2)
-        ]
-        for local_band in range(BANDS // PARTS):
-            band = slab * (BANDS // PARTS) + local_band
-            at = 2 * PAIRS * local_band
-            parts = {}
-            cosine = products[0][at : at + PAIRS]
-            sine = products[0][at + PAIRS : at + 2 * PAIRS]
-            parts[0, 0] = cosine[:, :LANES] - flip * sine[:, LANES:]
-            parts[1, 0] = -sine[:, :LANES] - flip * cosine[:, LANES:]
-            cosine = products[1][at : at + PAIRS]
-            sine = products[1][at + PAIRS : at + 2 * PAIRS]
-            parts[0, 1] = jnp.where(odd_pair, cosine[:, LANES:], cosine[:, :LANES])
-            parts[1, 1] = -jnp.where(odd_pair, sine[:, LANES:], sine[:, :LANES])
-            for parity in range(2):
-                real = parts[0, parity].astype(BF16).astype(F32)
-                imag = parts[1, parity].astype(BF16).astype(F32)
-                place = 2 * band + parity
-                power = pltpu.roll(
-                    real * real + imag * imag, lax.rem(place - channel + LANES, LANES), 1
-                )
-                power_ref[...] = jnp.where(lane % 32 == place, power, power_ref[...])
-            for seg in range(SEG):
-                line = None
-                for side in range(2):
-                    for parity in range(2):
-                        group = side * 2 + parity
-                        part = parts[side, parity]
-                        if group != seg:
-                            part = pltpu.roll(part, (group - seg) * 32 % LANES, 1)
-                        line = part if line is None else jnp.where(lane // 32 == group, part, line)
-                line = line.astype(BF16)
-                for half in range(HALVES):
-                    block_ref[band, half, seg * FEW : (seg + 1) * FEW, :] = line[
-                        half * FEW : (half + 1) * FEW
-                    ]
+    table.wait()
+    odd = jnp.dot(table_ref[0], wave_ref[0, 0], preferred_element_type=F32)
+    odd = odd + jnp.dot(table_ref[0], wave_ref[0, 1], preferred_element_type=F32)
+    even = []
+    for k in range(2):
+        rows = pl.ds(k * BANDS * PAIRS, BANDS * PAIRS)
+        product = jnp.dot(table_ref[1, rows], wave_ref[1, k], preferred_element_type=F32)
+        even.append(product[:, :LANES] + product[:, LANES:])
+    for band in range(BANDS):
+        at = 2 * PAIRS * band
+        cosine, sine = odd[at : at + PAIRS], odd[at + PAIRS : at + 2 * PAIRS]
+        parts = {
+            (0, 0): cosine[:, :LANES] - flip * sine[:, LANES:],
+            (1, 0): -sine[:, :LANES] - flip * cosine[:, LANES:],
+        }
+        for side in range(2):
+            at = PAIRS * band + FEW * side
+            rows = [even[k][at + 8 * half : at + 8 * half + 8] for half in range(2) for k in range(2)]
+            parts[side, 1] = jnp.concatenate(rows, axis=0) * (1.0, -1.0)[side]
+        for parity in range(2):
+            real = parts[0, parity].astype(BF16).astype(F32)
+            imag = parts[1, parity].astype(BF16).astype(F32)
+            place = 2 * band + parity
+            power = pltpu.roll(
+                real * real + imag * imag, lax.rem(place - channel + LANES, LANES), 1
+            )
+            power_ref[...] = jnp.where(lane % 32 == place, power, power_ref[...])
+        for seg in range(SEG):
+            line = None
+            for side in range(2):
+                for parity in range(2):
+                    group = side * 2 + parity
+                    part = parts[side, parity]
+                    if group != seg:
+                        part = pltpu.roll(part, (group - seg) * 32 % LANES, 1)
+                    line = part if line is None else jnp.where(lane // 32 == group, part, line)
+            line = line.astype(BF16)
+            for half in range(HALVES):
+                block_ref[band, half, seg * FEW : (seg + 1) * FEW, :] = line[
+                    half * FEW : (half + 1) * FEW
+                ]
     mine = pilot_ref[0] // CH == lax.axis_index("rgrp")
     guide_ref[...] = jnp.where(mine, jnp.sqrt(power_ref[...]), 0.0).astype(BF16)
 
@@ -177,12 +181,11 @@
             pltpu.SMEM((1, CH), jnp.int32),
             pltpu.SMEM((1,), jnp.int32),
             pltpu.VMEM((CH, SPAN), BF16),
-            pltpu.VMEM((PARTS, 2, 2 * PAIRS * BANDS // PARTS, QUARTER), BF16),
+            pltpu.VMEM((2, 2 * PAIRS * BANDS, QUARTER), BF16),
             pltpu.VMEM((2, 2 * LANES, QUARTER), F32),
             pltpu.VMEM((2, 2, QUARTER, 2 * LANES), BF16),
             pltpu.VMEM((PAIRS, LANES), F32),
-            pltpu.SemaphoreType.DMA((4,)),
-            pltpu.SemaphoreType.DMA((PARTS,)),
+            pltpu.SemaphoreType.DMA((5,)),
         ],
         compiler_params=pltpu.CompilerParams(vmem_limit_bytes=16 * 1024 * 1024),
         name="spectra",
@@ -276,6 +279,7 @@
 
 
 def stack_pair(pair, left, rights, stack_refs):
+    pair = 2 * (pair % 8) + pair // 8
     sign = jnp.where(lane_index(BANDS * SEG) < 64, 1.0, -1.0)
     turned = jnp.transpose(left)
     left = jnp.concatenate([turned[:64], turned[64:]], axis=1).astype(BF16)

time: 77.6 us -> 77.3 us (level)
  no operation moved by 1% of the time
where the time goes in v11:
time: 77.3 us; the launch traced here: 76.8 us
  blocking collectives  52.8 us (68%)
  starting transfers between devices  9.5 us (12%)
  Pallas kernels  8.61 us (11%)
  waiting for transfers between devices  5.2 us (7%)
    all_to_all x1, blocking collectives, local(): lax.all_to_all(white, ('freq', 'rgrp'), split_axis=0, concat_axis=0, tile...  27.1 us
    all_to_all x1, blocking collectives, local(): lax.all_to_all(jnp.broadcast_to(guide, (16, PAIRS, LANES)), 'rgrp', split...  25.6 us
    ppermute x2, starting transfers between devices, beside(): return lax.ppermute(value, 'rgrp', [(g, g ^ 1) for g in range(32)])  5.95 us
    ppermute x2, waiting for transfers between devices, beside(): return lax.ppermute(value, 'rgrp', [(g, g ^ 1) for g in range(32)])  5.19 us
    ppermute x1, starting transfers between devices, local(): far = lax.ppermute(own, 'rgrp', [(g, (g + 2) % 32) for g in range(32)])  3.55 us
    pallas_call x1, Pallas kernels, spectra_of(): pl.pallas_call(spectra_kernel, in_specs=[pl.BlockSpec(memory_space=pl.ANY...  3.19 us
    pallas_call x1, Pallas kernels, other_of(): pl.pallas_call(other_kernel, in_specs=[vmem], out_specs=[vmem, vmem], out...  1.81 us
  transfers between devices with their start and end apart: 3, of which 1 were waited for; matrix products, arithmetic and copies ran while one was open for 0% of the time, Pallas kernels for 2%

profile of v11, /device:TPU:1, one launch (start us, length us, event | category | flops | bytes accessed | tf_op | source)
XLA Modules:
  0.0 76.8 jit_solution(14938678473573245699)
XLA Ops:
  0.7 3.2 %spectra.1 = (bf16[16,2,64,128]{3,2,1,0:T(8,128)(2,1)S(1)}, bf16[32,128]{1,0:T(8,128)(2,1)S(1)}) custom-call(s32[4]{0:T(128)} %offset_hbm.1, s32[1,32]{1,0:T(1,128)} %order_hbm.1, s32[1]{0:T(128)S(6)} %copy.6.pilot_hbm, bf16[32,9216]{1,0:T(8,128)(2,1)} %traces_hbm.1, bf16[2,1024,512]{2,1,0:T(8,128)(2,1)} %constant.2.clone.table_hbm), custom_call_target="tpu_custom_call" | custom-call | tf_op jit(solution)/shard_map/spectra/pallas_call | solution.py:171
  3.8 4.0 %collective-permute-start = (bf16[32,128]{1,0:T(8,128)(2,1)S(1)}, bf16[32,128]{1,0:T(8,128)(2,1)S(1)}, u32[]{:S(2)}, u32[]{:S(2)}) collective-permute-start(bf16[32,128]{1,0:T(8,128)(2,1)S(1)} %get-tuple-element.9), channel_id=1, source_target_pairs={{0,1},{1,0},{2,3},{3,2},{4,5},{5,4},{6,7},{7,6},{8,9},{9,8},{10,11... | collective-permute-start | bytes 24584 | tf_op jit(solution)/shard_map/ppermute | solution.py:394
  7.9 3.5 %collective-permute-start.1 = (bf16[16,2,64,128]{3,2,1,0:T(8,128)(2,1)S(1)}, bf16[16,2,64,128]{3,2,1,0:T(8,128)(2,1)S(1)}, u32[]{:S(2)}, u32[]{:S(2)}) collective-permute-start(bf16[16,2,64,128]{3,2,1,0:T(8,128)(2,1)S(1)} %get-tuple-element.10.own_ref), channel_id=1, source_target_pairs={{0,2},{1,3},{2,4},{3,5},{4,6},{5,7},{6,8},{7,9},{8,10},{9,11},{10,... | collective-permute-start | bytes 1572872 | tf_op jit(solution)/shard_map/ppermute | solution.py:399
  11.4 0.0 collective-permute-done
  11.5 25.6 %all_to_all.10.guides_ref = bf16[16,32,128]{2,1,0:T(8,128)(2,1)S(1)} all-to-all(bf16[16,32,128]{2,1,0:T(8,128)(2,1)S(1)} %broadcast_in_dim.3), channel_id=1, replica_groups={{0,2,4,6,8,10,12,14,16,18,20,22,24,26,28,30},{1,3,5,7,9,11,13,15,17,19,..., dimensions={0} | all-to-all | bytes 262144 | tf_op jit(solution)/shard_map/all_to_all | solution.py:402
  37.2 0.0 collective-permute-done.1.far_ref
  37.2 1.0 %whiten.1 = bf16[32,2,64,128]{3,2,1,0:T(8,128)(2,1)S(1)} custom-call(f32[32,128]{1,0:T(8,128)S(1)} %total.1.guide_ref, bf16[16,2,64,128]{3,2,1,0:T(8,128)(2,1)S(1)} %get-tuple-element.10.own_ref, bf16[16,2,64,128]{3,2,1,0:T(8,128)(2,1)S(1)} %collective-permute-done.1.far_ref), custom_call_target="tpu_custom_call" | custom-call | tf_op jit(solution)/shard_map/whiten/pallas_call | solution.py:254
  38.2 27.1 %all_to_all.11.parts_ref = bf16[32,2,64,128]{3,2,1,0:T(8,128)(2,1)S(1)} all-to-all(bf16[32,2,64,128]{3,2,1,0:T(8,128)(2,1)S(1)} %whiten.1), channel_id=1, replica_groups={{0,1,32,33,64,65,96,97,128,129,160,161,192,193,224,225,256,257,288,289,..., dimensions={0} | all-to-all | bytes 2097152 | tf_op jit(solution)/shard_map/all_to_all | solution.py:412
  65.3 1.8 %cross_other.1 = (bf16[32,32,128]{2,1,0:T(8,128)(2,1)S(1)}, bf16[16,3,64,128]{3,2,1,0:T(8,128)(2,1)S(1)}) custom-call(bf16[32,2,64,128]{3,2,1,0:T(8,128)(2,1)S(1)} %all_to_all.11.parts_ref), custom_call_target="tpu_custom_call" | custom-call | tf_op jit(solution)/shard_map/cross_other/pallas_call | solution.py:340
  67.2 1.9 %collective-permute-start.2 = (bf16[32,32,128]{2,1,0:T(8,128)(2,1)S(1)}, bf16[32,32,128]{2,1,0:T(8,128)(2,1)S(1)}, u32[]{:S(2)}, u32[]{:S(2)}) collective-permute-start(bf16[32,32,128]{2,1,0:T(8,128)(2,1)S(1)} %get-tuple-element.12), channel_id=1, source_target_pairs={{0,1},{1,0},{2,3},{3,2},{4,5},{5,4},{6,7},{7,6},{8,9},{9,8},{10,11... | collective-permute-start | bytes 786440 | tf_op jit(solution)/shard_map/ppermute | solution.py:394
  69.1 1.5 %cross_mine.1.own_ref = bf16[32,32,128]{2,1,0:T(8,128)(2,1)S(1)} custom-call(bf16[16,3,64,128]{3,2,1,0:T(8,128)(2,1)S(1)} %get-tuple-element.11.block_ref), custom_call_target="tpu_custom_call" | custom-call | flops 268435456 | bytes 8388608 | tf_op jit(solution)/shard_map/cross_mine/pallas_call | solution.py:353
  70.6 5.2 %collective-permute-done.2.other_ref = bf16[32,32,128]{2,1,0:T(8,128)(2,1)S(1)} collective-permute-done((bf16[32,32,128]{2,1,0:T(8,128)(2,1)S(1)}, bf16[32,32,128]{2,1,0:T(8,128)(2,1)S(1)}, u32[]{:S(2)}, u32[]{:S(2)}) %collective-permute-start.2) | collective-permute-done | bytes 262176 | tf_op jit(solution)/shard_map/ppermute | solution.py:394
  75.8 1.0 %merge.1 = bf16[2,32,32,128]{3,2,1,0:T(8,128)(2,1)} custom-call(bf16[32,32,128]{2,1,0:T(8,128)(2,1)S(1)} %cross_mine.1.own_ref, bf16[32,32,128]{2,1,0:T(8,128)(2,1)S(1)} %collective-permute-done.2.other_ref), custom_call_target="tpu_custom_call" | custom-call | tf_op jit(solution)/shard_map/merge/pallas_call | solution.py:383
  (3 shorter events, 0.0 us)
Async XLA Ops:
  3.8 7.6 %collective-permute-start = (bf16[32,128]{1,0:T(8,128)(2,1)S(1)}, bf16[32,128]{1,0:T(8,128)(2,1)S(1)}, u32[]{:S(2)}, u32[]{:S(2)}) collective-permute-start(bf16[32,128]{1,0:T(8,128)(2,1)S(1)} %get-tuple-element.9), channel_id=1, source_target_pairs={{0,1},{1,0},{2,3},{3,2},{4,5},{5,4},{6,7},{7,6},{8,9},{9,8},{10,11... | collective-permute-start | bytes 24584 | tf_op jit(solution)/shard_map/ppermute | solution.py:394
  7.9 29.3 %collective-permute-start.1 = (bf16[16,2,64,128]{3,2,1,0:T(8,128)(2,1)S(1)}, bf16[16,2,64,128]{3,2,1,0:T(8,128)(2,1)S(1)}, u32[]{:S(2)}, u32[]{:S(2)}) collective-permute-start(bf16[16,2,64,128]{3,2,1,0:T(8,128)(2,1)S(1)} %get-tuple-element.10.own_ref), channel_id=1, source_target_pairs={{0,2},{1,3},{2,4},{3,5},{4,6},{5,7},{6,8},{7,9},{8,10},{9,11},{10,... | collective-permute-start | bytes 1572872 | tf_op jit(solution)/shard_map/ppermute | solution.py:399
  67.2 8.6 %collective-permute-start.2 = (bf16[32,32,128]{2,1,0:T(8,128)(2,1)S(1)}, bf16[32,32,128]{2,1,0:T(8,128)(2,1)S(1)}, u32[]{:S(2)}, u32[]{:S(2)}) collective-permute-start(bf16[32,32,128]{2,1,0:T(8,128)(2,1)S(1)} %get-tuple-element.12), channel_id=1, source_target_pairs={{0,1},{1,0},{2,3},{3,2},{4,5},{5,4},{6,7},{7,6},{8,9},{9,8},{10,11... | collective-permute-start | bytes 786440 | tf_op jit(solution)/shard_map/ppermute | solution.py:394

commit v12 on v11

--- a/solution.py
+++ b/solution.py
@@ -296,7 +296,7 @@
         pieces = {}
         for back, stack_ref in enumerate(stack_refs):
             rows = [stack_ref[pl.ds(first + k, 2 * FEW, stride=CH), :] for k in range(4)]
-            turned = jnp.transpose(jnp.concatenate(rows, axis=0)) * 0.125
+            turned = jnp.transpose((jnp.concatenate(rows, axis=0) * 0.125).astype(BF16))
             pieces[back] = jnp.where(even, turned[:32], turned[32:64])
             pieces[2 + back] = jnp.where(even, turned[64:96], turned[96:])
         for k in range(4):
@@ -306,7 +306,7 @@
                 if group != k:
                     part = pltpu.roll(part, (group - k) * 32 % LANES, 1)
                 line = part if line is None else jnp.where(lane // 32 == group, part, line)
-            out_ref[first + k] = line.astype(BF16)
+            out_ref[first + k] = line
 
 
 def other_kernel(parts_ref, out_ref, block_ref, wide_ref, near_ref, far_ref):
@@ -362,29 +362,38 @@
     )(blocks)
 
 
-def merge_kernel(own_ref, other_ref, out_ref):
+def merge_kernel(own_ref, other_ref, out_hbm, out_ref, sems):
     first = lax.axis_index("rgrp") % 2 == 0
     even = (lane_index(CH) // 32) % 2 == 0
-
-    def channel(i, carry):
-        own = own_ref[i].astype(F32)
-        other = other_ref[i].astype(F32)
-        low = jnp.where(first, own, other)
-        high = jnp.where(first, other, own)
-        out_ref[0, i] = jnp.where(even, low, pltpu.roll(high, 32, 1)).astype(BF16)
-        out_ref[1, i] = jnp.where(even, pltpu.roll(low, 96, 1), high).astype(BF16)
-        return carry
-
-    lax.fori_loop(0, CH, channel, 0, unroll=CH)
+    copies = []
+    for part in range(4):
+        rows = pl.ds(part * (CH // 4), CH // 4)
+        for i in range(part * (CH // 4), (part + 1) * (CH // 4)):
+            own = own_ref[i].astype(F32)
+            other = other_ref[i].astype(F32)
+            low = jnp.where(first, own, other)
+            high = jnp.where(first, other, own)
+            out_ref[0, i] = jnp.where(even, low, pltpu.roll(high, 32, 1)).astype(BF16)
+            out_ref[1, i] = jnp.where(even, pltpu.roll(low, 96, 1), high).astype(BF16)
+        for back in range(2):
+            copy = pltpu.make_async_copy(
+                out_ref.at[back, rows], out_hbm.at[back, rows], sems.at[2 * part + back]
+            )
+            copy.start()
+            copies.append(copy)
+    for copy in copies:
+        copy.wait()
 
 
 def merged_of(own, other):
     vmem = pl.BlockSpec(memory_space=pltpu.VMEM)
+    shape = (2, CH, CH, LANES)
     return pl.pallas_call(
         merge_kernel,
         in_specs=[vmem] * 2,
-        out_specs=vmem,
-        out_shape=jax.ShapeDtypeStruct((2, CH, CH, LANES), BF16),
+        out_specs=pl.BlockSpec(memory_space=pl.ANY),
+        out_shape=jax.ShapeDtypeStruct(shape, BF16),
+        scratch_shapes=[pltpu.VMEM(shape, BF16), pltpu.SemaphoreType.DMA((2 * 4,))],
         compiler_params=pltpu.CompilerParams(vmem_limit_bytes=32 * 1024 * 1024),
         name="merge",
     )(own, other)

time: 77.3 us -> 77.2 us (level)
  no operation moved by 1% of the time
where the time goes in v12:
time: 77.2 us; the launch traced here: 76.7 us
  blocking collectives  52.8 us (68%)
  starting transfers between devices  9.5 us (12%)
  Pallas kernels  8.43 us (11%)
  waiting for transfers between devices  5.27 us (7%)
    all_to_all x1, blocking collectives, local(): lax.all_to_all(white, ('freq', 'rgrp'), split_axis=0, concat_axis=0, tile...  27.1 us
    all_to_all x1, blocking collectives, local(): lax.all_to_all(jnp.broadcast_to(guide, (16, PAIRS, LANES)), 'rgrp', split...  25.6 us
    ppermute x2, starting transfers between devices, beside(): return lax.ppermute(value, 'rgrp', [(g, g ^ 1) for g in range(32)])  5.95 us
    ppermute x2, waiting for transfers between devices, beside(): return lax.ppermute(value, 'rgrp', [(g, g ^ 1) for g in range(32)])  5.27 us
    ppermute x1, starting transfers between devices, local(): far = lax.ppermute(own, 'rgrp', [(g, (g + 2) % 32) for g in range(32)])  3.55 us
    pallas_call x1, Pallas kernels, spectra_of(): pl.pallas_call(spectra_kernel, in_specs=[pl.BlockSpec(memory_space=pl.ANY...  3.19 us
    pallas_call x1, Pallas kernels, other_of(): pl.pallas_call(other_kernel, in_specs=[vmem], out_specs=[vmem, vmem], out...  1.76 us
  transfers between devices with their start and end apart: 3, of which 1 were waited for; matrix products, arithmetic and copies ran while one was open for 0% of the time, Pallas kernels for 2%

profile of v12, /device:TPU:1, one launch (start us, length us, event | category | flops | bytes accessed | tf_op | source)
XLA Modules:
  0.0 76.7 jit_solution(14015370380346620385)
XLA Ops:
  0.7 3.2 %spectra.1 = (bf16[16,2,64,128]{3,2,1,0:T(8,128)(2,1)S(1)}, bf16[32,128]{1,0:T(8,128)(2,1)S(1)}) custom-call(s32[4]{0:T(128)} %offset_hbm.1, s32[1,32]{1,0:T(1,128)} %order_hbm.1, s32[1]{0:T(128)S(6)} %copy.6.pilot_hbm, bf16[32,9216]{1,0:T(8,128)(2,1)} %traces_hbm.1, bf16[2,1024,512]{2,1,0:T(8,128)(2,1)} %constant.2.clone.table_hbm), custom_call_target="tpu_custom_call" | custom-call | tf_op jit(solution)/shard_map/spectra/pallas_call | solution.py:171
  3.8 4.0 %collective-permute-start = (bf16[32,128]{1,0:T(8,128)(2,1)S(1)}, bf16[32,128]{1,0:T(8,128)(2,1)S(1)}, u32[]{:S(2)}, u32[]{:S(2)}) collective-permute-start(bf16[32,128]{1,0:T(8,128)(2,1)S(1)} %get-tuple-element.9), channel_id=1, source_target_pairs={{0,1},{1,0},{2,3},{3,2},{4,5},{5,4},{6,7},{7,6},{8,9},{9,8},{10,11... | collective-permute-start | bytes 24584 | tf_op jit(solution)/shard_map/ppermute | solution.py:403
  7.9 3.5 %collective-permute-start.1 = (bf16[16,2,64,128]{3,2,1,0:T(8,128)(2,1)S(1)}, bf16[16,2,64,128]{3,2,1,0:T(8,128)(2,1)S(1)}, u32[]{:S(2)}, u32[]{:S(2)}) collective-permute-start(bf16[16,2,64,128]{3,2,1,0:T(8,128)(2,1)S(1)} %get-tuple-element.10.own_ref), channel_id=1, source_target_pairs={{0,2},{1,3},{2,4},{3,5},{4,6},{5,7},{6,8},{7,9},{8,10},{9,11},{10,... | collective-permute-start | bytes 1572872 | tf_op jit(solution)/shard_map/ppermute | solution.py:408
  11.4 0.0 collective-permute-done
  11.5 25.6 %all_to_all.10.guides_ref = bf16[16,32,128]{2,1,0:T(8,128)(2,1)S(1)} all-to-all(bf16[16,32,128]{2,1,0:T(8,128)(2,1)S(1)} %broadcast_in_dim.3), channel_id=1, replica_groups={{0,2,4,6,8,10,12,14,16,18,20,22,24,26,28,30},{1,3,5,7,9,11,13,15,17,19,..., dimensions={0} | all-to-all | bytes 262144 | tf_op jit(solution)/shard_map/all_to_all | solution.py:411
  37.2 0.0 collective-permute-done.1.far_ref
  37.2 1.0 %whiten.1 = bf16[32,2,64,128]{3,2,1,0:T(8,128)(2,1)S(1)} custom-call(f32[32,128]{1,0:T(8,128)S(1)} %total.1.guide_ref, bf16[16,2,64,128]{3,2,1,0:T(8,128)(2,1)S(1)} %get-tuple-element.10.own_ref, bf16[16,2,64,128]{3,2,1,0:T(8,128)(2,1)S(1)} %collective-permute-done.1.far_ref), custom_call_target="tpu_custom_call" | custom-call | tf_op jit(solution)/shard_map/whiten/pallas_call | solution.py:254
  38.2 27.1 %all_to_all.11.parts_ref = bf16[32,2,64,128]{3,2,1,0:T(8,128)(2,1)S(1)} all-to-all(bf16[32,2,64,128]{3,2,1,0:T(8,128)(2,1)S(1)} %whiten.1), channel_id=1, replica_groups={{0,1,32,33,64,65,96,97,128,129,160,161,192,193,224,225,256,257,288,289,..., dimensions={0} | all-to-all | bytes 2097152 | tf_op jit(solution)/shard_map/all_to_all | solution.py:421
  65.3 1.8 %cross_other.1 = (bf16[32,32,128]{2,1,0:T(8,128)(2,1)S(1)}, bf16[16,3,64,128]{3,2,1,0:T(8,128)(2,1)S(1)}) custom-call(bf16[32,2,64,128]{3,2,1,0:T(8,128)(2,1)S(1)} %all_to_all.11.parts_ref), custom_call_target="tpu_custom_call" | custom-call | tf_op jit(solution)/shard_map/cross_other/pallas_call | solution.py:340
  67.1 1.9 %collective-permute-start.2 = (bf16[32,32,128]{2,1,0:T(8,128)(2,1)S(1)}, bf16[32,32,128]{2,1,0:T(8,128)(2,1)S(1)}, u32[]{:S(2)}, u32[]{:S(2)}) collective-permute-start(bf16[32,32,128]{2,1,0:T(8,128)(2,1)S(1)} %get-tuple-element.12), channel_id=1, source_target_pairs={{0,1},{1,0},{2,3},{3,2},{4,5},{5,4},{6,7},{7,6},{8,9},{9,8},{10,11... | collective-permute-start | bytes 786440 | tf_op jit(solution)/shard_map/ppermute | solution.py:403
  69.0 1.4 %cross_mine.1.own_ref = bf16[32,32,128]{2,1,0:T(8,128)(2,1)S(1)} custom-call(bf16[16,3,64,128]{3,2,1,0:T(8,128)(2,1)S(1)} %get-tuple-element.11.block_ref), custom_call_target="tpu_custom_call" | custom-call | flops 268435456 | bytes 8388608 | tf_op jit(solution)/shard_map/cross_mine/pallas_call | solution.py:353
  70.5 5.3 %collective-permute-done.2.other_ref = bf16[32,32,128]{2,1,0:T(8,128)(2,1)S(1)} collective-permute-done((bf16[32,32,128]{2,1,0:T(8,128)(2,1)S(1)}, bf16[32,32,128]{2,1,0:T(8,128)(2,1)S(1)}, u32[]{:S(2)}, u32[]{:S(2)}) %collective-permute-start.2) | collective-permute-done | bytes 262176 | tf_op jit(solution)/shard_map/ppermute | solution.py:403
  75.8 1.0 %merge.1 = bf16[2,32,32,128]{3,2,1,0:T(8,128)(2,1)} custom-call(bf16[32,32,128]{2,1,0:T(8,128)(2,1)S(1)} %cross_mine.1.own_ref, bf16[32,32,128]{2,1,0:T(8,128)(2,1)S(1)} %collective-permute-done.2.other_ref), custom_call_target="tpu_custom_call" | custom-call | tf_op jit(solution)/shard_map/merge/pallas_call | solution.py:391
  (3 shorter events, 0.0 us)
Async XLA Ops:
  3.8 7.6 %collective-permute-start = (bf16[32,128]{1,0:T(8,128)(2,1)S(1)}, bf16[32,128]{1,0:T(8,128)(2,1)S(1)}, u32[]{:S(2)}, u32[]{:S(2)}) collective-permute-start(bf16[32,128]{1,0:T(8,128)(2,1)S(1)} %get-tuple-element.9), channel_id=1, source_target_pairs={{0,1},{1,0},{2,3},{3,2},{4,5},{5,4},{6,7},{7,6},{8,9},{9,8},{10,11... | collective-permute-start | bytes 24584 | tf_op jit(solution)/shard_map/ppermute | solution.py:403
  7.9 29.3 %collective-permute-start.1 = (bf16[16,2,64,128]{3,2,1,0:T(8,128)(2,1)S(1)}, bf16[16,2,64,128]{3,2,1,0:T(8,128)(2,1)S(1)}, u32[]{:S(2)}, u32[]{:S(2)}) collective-permute-start(bf16[16,2,64,128]{3,2,1,0:T(8,128)(2,1)S(1)} %get-tuple-element.10.own_ref), channel_id=1, source_target_pairs={{0,2},{1,3},{2,4},{3,5},{4,6},{5,7},{6,8},{7,9},{8,10},{9,11},{10,... | collective-permute-start | bytes 1572872 | tf_op jit(solution)/shard_map/ppermute | solution.py:408
  67.1 8.6 %collective-permute-start.2 = (bf16[32,32,128]{2,1,0:T(8,128)(2,1)S(1)}, bf16[32,32,128]{2,1,0:T(8,128)(2,1)S(1)}, u32[]{:S(2)}, u32[]{:S(2)}) collective-permute-start(bf16[32,32,128]{2,1,0:T(8,128)(2,1)S(1)} %get-tuple-element.12), channel_id=1, source_target_pairs={{0,1},{1,0},{2,3},{3,2},{4,5},{5,4},{6,7},{7,6},{8,9},{9,8},{10,11... | collective-permute-start | bytes 786440 | tf_op jit(solution)/shard_map/ppermute | solution.py:403

commit v13 on v11

--- a/solution.py
+++ b/solution.py
@@ -212,7 +212,7 @@
     )(guides)
 
 
-def whiten_kernel(guide_ref, own_ref, far_ref, white_ref, value_ref):
+def whiten_kernel(guide_ref, own_ref, far_ref, white_ref, weight_ref):
     guide = guide_ref[...]
     place = lane_index(PAIRS) // 2
     parity = lax.broadcasted_iota(jnp.int32, (LANES, LANES), 0) % 2
@@ -224,6 +224,7 @@
         weight = jnp.dot(
             jnp.concatenate(picked, axis=0).astype(BF16), spread, preferred_element_type=F32
         )
+        weight_ref[band] = weight
         for seg in range(SEG):
             rows = slice(seg * FEW, (seg + 1) * FEW)
             for half in range(HALVES):
@@ -231,7 +232,6 @@
                 part = weight[at : at + FEW]
                 for k, block_ref in enumerate(blocks):
                     value = block_ref[band, half, rows, :].astype(F32) * part
-                    value_ref[band * HALVES + half, k, rows, :] = value
                     totals[k][seg] = totals[k][seg] + value * value
     for k in range(len(blocks)):
         for seg in range(SEG):
@@ -242,7 +242,9 @@
             level = (total * (0.1 / (64.0 * BANDS)) + 1e-06)[:1]
             rows = slice(seg * FEW, (seg + 1) * FEW)
             for place in range(BANDS * HALVES):
-                value = value_ref[place, k, rows, :]
+                at = seg * PAIRS + place % HALVES * FEW
+                part = weight_ref[place // HALVES, at : at + FEW, :]
+                value = blocks[k][place // HALVES, place % HALVES, rows, :].astype(F32) * part
                 energy = value * value
                 energy = energy + pltpu.roll(energy, 64, 1)
                 white_ref[place, k, rows, :] = (value * lax.rsqrt(energy + level)).astype(BF16)
@@ -256,7 +258,7 @@
         in_specs=[vmem] * 3,
         out_specs=vmem,
         out_shape=jax.ShapeDtypeStruct(shape, BF16),
-        scratch_shapes=[pltpu.VMEM(shape, F32)],
+        scratch_shapes=[pltpu.VMEM((BANDS, SEG * PAIRS, LANES), F32)],
         compiler_params=pltpu.CompilerParams(vmem_limit_bytes=32 * 1024 * 1024),
         name="whiten",
     )(guides, own, far)

time: 77.3 us -> 77.3 us (level)
  no operation moved by 1% of the time
where the time goes in v13:
time: 77.3 us; the launch traced here: 76.8 us
  blocking collectives  52.8 us (68%)
  starting transfers between devices  9.5 us (12%)
  Pallas kernels  8.62 us (11%)
  waiting for transfers between devices  5.2 us (7%)
    all_to_all x1, blocking collectives, local(): lax.all_to_all(white, ('freq', 'rgrp'), split_axis=0, concat_axis=0, tile...  27.1 us
    all_to_all x1, blocking collectives, local(): lax.all_to_all(jnp.broadcast_to(guide, (16, PAIRS, LANES)), 'rgrp', split...  25.6 us
    ppermute x2, starting transfers between devices, beside(): return lax.ppermute(value, 'rgrp', [(g, g ^ 1) for g in range(32)])  5.95 us
    ppermute x2, waiting for transfers between devices, beside(): return lax.ppermute(value, 'rgrp', [(g, g ^ 1) for g in range(32)])  5.19 us
    ppermute x1, starting transfers between devices, local(): far = lax.ppermute(own, 'rgrp', [(g, (g + 2) % 32) for g in range(32)])  3.55 us
    pallas_call x1, Pallas kernels, spectra_of(): pl.pallas_call(spectra_kernel, in_specs=[pl.BlockSpec(memory_space=pl.ANY...  3.19 us
    pallas_call x1, Pallas kernels, other_of(): pl.pallas_call(other_kernel, in_specs=[vmem], out_specs=[vmem, vmem], out...  1.81 us
  transfers between devices with their start and end apart: 3, of which 1 were waited for; matrix products, arithmetic and copies ran while one was open for 0% of the time, Pallas kernels for 2%

profile of v13, /device:TPU:1, one launch (start us, length us, event | category | flops | bytes accessed | tf_op | source)
XLA Modules:
  0.0 76.8 jit_solution(17756794165538071822)
XLA Ops:
  0.7 3.2 %spectra.1 = (bf16[16,2,64,128]{3,2,1,0:T(8,128)(2,1)S(1)}, bf16[32,128]{1,0:T(8,128)(2,1)S(1)}) custom-call(s32[4]{0:T(128)} %offset_hbm.1, s32[1,32]{1,0:T(1,128)} %order_hbm.1, s32[1]{0:T(128)S(6)} %copy.6.pilot_hbm, bf16[32,9216]{1,0:T(8,128)(2,1)} %traces_hbm.1, bf16[2,1024,512]{2,1,0:T(8,128)(2,1)} %constant.2.clone.table_hbm), custom_call_target="tpu_custom_call" | custom-call | tf_op jit(solution)/shard_map/spectra/pallas_call | solution.py:171
  3.8 4.0 %collective-permute-start = (bf16[32,128]{1,0:T(8,128)(2,1)S(1)}, bf16[32,128]{1,0:T(8,128)(2,1)S(1)}, u32[]{:S(2)}, u32[]{:S(2)}) collective-permute-start(bf16[32,128]{1,0:T(8,128)(2,1)S(1)} %get-tuple-element.9), channel_id=1, source_target_pairs={{0,1},{1,0},{2,3},{3,2},{4,5},{5,4},{6,7},{7,6},{8,9},{9,8},{10,11... | collective-permute-start | bytes 24584 | tf_op jit(solution)/shard_map/ppermute | solution.py:396
  7.9 3.5 %collective-permute-start.1 = (bf16[16,2,64,128]{3,2,1,0:T(8,128)(2,1)S(1)}, bf16[16,2,64,128]{3,2,1,0:T(8,128)(2,1)S(1)}, u32[]{:S(2)}, u32[]{:S(2)}) collective-permute-start(bf16[16,2,64,128]{3,2,1,0:T(8,128)(2,1)S(1)} %get-tuple-element.10.own_ref), channel_id=1, source_target_pairs={{0,2},{1,3},{2,4},{3,5},{4,6},{5,7},{6,8},{7,9},{8,10},{9,11},{10,... | collective-permute-start | bytes 1572872 | tf_op jit(solution)/shard_map/ppermute | solution.py:401
  11.4 0.0 collective-permute-done
  11.5 25.6 %all_to_all.10.guides_ref = bf16[16,32,128]{2,1,0:T(8,128)(2,1)S(1)} all-to-all(bf16[16,32,128]{2,1,0:T(8,128)(2,1)S(1)} %broadcast_in_dim.3), channel_id=1, replica_groups={{0,2,4,6,8,10,12,14,16,18,20,22,24,26,28,30},{1,3,5,7,9,11,13,15,17,19,..., dimensions={0} | all-to-all | bytes 262144 | tf_op jit(solution)/shard_map/all_to_all | solution.py:404
  37.2 0.0 collective-permute-done.1.far_ref
  37.2 1.1 %whiten.1 = bf16[32,2,64,128]{3,2,1,0:T(8,128)(2,1)S(1)} custom-call(f32[32,128]{1,0:T(8,128)S(1)} %total.1.guide_ref, bf16[16,2,64,128]{3,2,1,0:T(8,128)(2,1)S(1)} %get-tuple-element.10.own_ref, bf16[16,2,64,128]{3,2,1,0:T(8,128)(2,1)S(1)} %collective-permute-done.1.far_ref), custom_call_target="tpu_custom_call" | custom-call | tf_op jit(solution)/shard_map/whiten/pallas_call | solution.py:256
  38.2 27.1 %all_to_all.11.parts_ref = bf16[32,2,64,128]{3,2,1,0:T(8,128)(2,1)S(1)} all-to-all(bf16[32,2,64,128]{3,2,1,0:T(8,128)(2,1)S(1)} %whiten.1), channel_id=1, replica_groups={{0,1,32,33,64,65,96,97,128,129,160,161,192,193,224,225,256,257,288,289,..., dimensions={0} | all-to-all | bytes 2097152 | tf_op jit(solution)/shard_map/all_to_all | solution.py:414
  65.4 1.8 %cross_other.1 = (bf16[32,32,128]{2,1,0:T(8,128)(2,1)S(1)}, bf16[16,3,64,128]{3,2,1,0:T(8,128)(2,1)S(1)}) custom-call(bf16[32,2,64,128]{3,2,1,0:T(8,128)(2,1)S(1)} %all_to_all.11.parts_ref), custom_call_target="tpu_custom_call" | custom-call | tf_op jit(solution)/shard_map/cross_other/pallas_call | solution.py:342
  67.2 1.9 %collective-permute-start.2 = (bf16[32,32,128]{2,1,0:T(8,128)(2,1)S(1)}, bf16[32,32,128]{2,1,0:T(8,128)(2,1)S(1)}, u32[]{:S(2)}, u32[]{:S(2)}) collective-permute-start(bf16[32,32,128]{2,1,0:T(8,128)(2,1)S(1)} %get-tuple-element.12), channel_id=1, source_target_pairs={{0,1},{1,0},{2,3},{3,2},{4,5},{5,4},{6,7},{7,6},{8,9},{9,8},{10,11... | collective-permute-start | bytes 786440 | tf_op jit(solution)/shard_map/ppermute | solution.py:396
  69.1 1.5 %cross_mine.1.own_ref = bf16[32,32,128]{2,1,0:T(8,128)(2,1)S(1)} custom-call(bf16[16,3,64,128]{3,2,1,0:T(8,128)(2,1)S(1)} %get-tuple-element.11.block_ref), custom_call_target="tpu_custom_call" | custom-call | flops 268435456 | bytes 8388608 | tf_op jit(solution)/shard_map/cross_mine/pallas_call | solution.py:355
  70.6 5.2 %collective-permute-done.2.other_ref = bf16[32,32,128]{2,1,0:T(8,128)(2,1)S(1)} collective-permute-done((bf16[32,32,128]{2,1,0:T(8,128)(2,1)S(1)}, bf16[32,32,128]{2,1,0:T(8,128)(2,1)S(1)}, u32[]{:S(2)}, u32[]{:S(2)}) %collective-permute-start.2) | collective-permute-done | bytes 262176 | tf_op jit(solution)/shard_map/ppermute | solution.py:396
  75.8 1.0 %merge.1 = bf16[2,32,32,128]{3,2,1,0:T(8,128)(2,1)} custom-call(bf16[32,32,128]{2,1,0:T(8,128)(2,1)S(1)} %cross_mine.1.own_ref, bf16[32,32,128]{2,1,0:T(8,128)(2,1)S(1)} %collective-permute-done.2.other_ref), custom_call_target="tpu_custom_call" | custom-call | tf_op jit(solution)/shard_map/merge/pallas_call | solution.py:385
  (3 shorter events, 0.0 us)
Async XLA Ops:
  3.8 7.6 %collective-permute-start = (bf16[32,128]{1,0:T(8,128)(2,1)S(1)}, bf16[32,128]{1,0:T(8,128)(2,1)S(1)}, u32[]{:S(2)}, u32[]{:S(2)}) collective-permute-start(bf16[32,128]{1,0:T(8,128)(2,1)S(1)} %get-tuple-element.9), channel_id=1, source_target_pairs={{0,1},{1,0},{2,3},{3,2},{4,5},{5,4},{6,7},{7,6},{8,9},{9,8},{10,11... | collective-permute-start | bytes 24584 | tf_op jit(solution)/shard_map/ppermute | solution.py:396
  7.9 29.3 %collective-permute-start.1 = (bf16[16,2,64,128]{3,2,1,0:T(8,128)(2,1)S(1)}, bf16[16,2,64,128]{3,2,1,0:T(8,128)(2,1)S(1)}, u32[]{:S(2)}, u32[]{:S(2)}) collective-permute-start(bf16[16,2,64,128]{3,2,1,0:T(8,128)(2,1)S(1)} %get-tuple-element.10.own_ref), channel_id=1, source_target_pairs={{0,2},{1,3},{2,4},{3,5},{4,6},{5,7},{6,8},{7,9},{8,10},{9,11},{10,... | collective-permute-start | bytes 1572872 | tf_op jit(solution)/shard_map/ppermute | solution.py:401
  67.2 8.6 %collective-permute-start.2 = (bf16[32,32,128]{2,1,0:T(8,128)(2,1)S(1)}, bf16[32,32,128]{2,1,0:T(8,128)(2,1)S(1)}, u32[]{:S(2)}, u32[]{:S(2)}) collective-permute-start(bf16[32,32,128]{2,1,0:T(8,128)(2,1)S(1)} %get-tuple-element.12), channel_id=1, source_target_pairs={{0,1},{1,0},{2,3},{3,2},{4,5},{5,4},{6,7},{7,6},{8,9},{9,8},{10,11... | collective-permute-start | bytes 786440 | tf_op jit(solution)/shard_map/ppermute | solution.py:396
